TPU v7x, 32 devices: a whole 2x2x4 slice. The times are simulated.
32 devices in a mesh: row: 8 (over y, x, core), col: 4 (over z).
Axes of the slice: x: 2, y: 2, z: 4, core: 2. Of those that a mesh axis runs over, the one named last changes fastest.
Arguments:
- attn_context: bfloat16 [4096, 4096], P('row', 'col'), may hold values from -6 to 6
- residual: bfloat16 [4096, 2048], P('row', 'col'), may hold values from -8 to 8
- w_out: bfloat16 [4096, 2048], P('col'), may hold values from -0.09375 to 0.09375
- gain_post: bfloat16 [2048], replicated, may hold values from 0.5 to 1.5
- gain_input: bfloat16 [2048], replicated, may hold values from 0.5 to 1.5
- routes: int32 [4096, 8], P('row'), may hold values from 0 to 15, all different within a row; in each aligned block of 512 rows (0 to 511, 512 to 1023, ...) at most 512 rows name the same one
- router_scores: float32 [4096, 8], P('row'), may hold values from 0.02 to 1
- w_gate: bfloat16 [32, 2048, 384], P(('row', 'col')), may hold values from -0.125 to 0.125
- w_up: bfloat16 [32, 2048, 384], P(('row', 'col')), may hold values from -0.125 to 0.125
- w_down: bfloat16 [32, 384, 2048], P(('row', 'col')), may hold values from -0.21875 to 0.21875
- w_query: bfloat16 [2048, 4096], P(None, 'col'), may hold values from -1 to 1
- w_keyval: bfloat16 [2048, 1024], P(None, 'col'), may hold values from -1 to 1
- segment_ids: int32 [8, 504], P('row'), may hold values from 0 to 3, never falling along the last dimension, each value on 1 to 252 neighbouring positions
- cache_lengths: int32 [64], P('row'), may hold values from 1 to 1024, 32768 in all
- holders: int32 [64], P('row'), may hold values from 0 to 63, each once
- cache_keys: bfloat16 [64, 1024, 512], P('row', 'col'), may hold values from -12 to 12
- cache_values: bfloat16 [64, 1024, 512], P('row', 'col'), may hold values from -12 to 12
Outputs:
- hidden_out: bfloat16 [4096, 2048], P('row', 'col')
- new_cache: bfloat16 [4096, 1024], P('row', 'col')
- attention_out: bfloat16 [4096, 4096], P('row', 'col')
Inputs may be any that keep to these rules, and one draw needn't show every extreme that they name: `routes`: in the 512 rows of one index of row, no expert is named by more than 512 rows, and in every draw some expert is named by exactly 512. `segment_ids`: each prompt has at most 252 rows and one has exactly that many. `cache_lengths`: the lengths sum to 32768 and the largest is 1024. `holders`: each cache entry belongs to exactly one decode row.
All inputs are finite; a program needn't handle non-finite values. No bound on the sum of `cache_lengths` on one device may be relied on, other than what follows from the above.
Results may differ from a plain program's by a relative error of at most 0.0175.
Values may be sent and summed in bfloat16 or wider, within the bound.
No kernel may reach another device: no remote copies, remote signals or barrier semaphores. Data moves between devices by JAX's collectives and lax.ppermute only.
A program may use at most 128 MiB of HBM per device.

v0:
```python
import jax
import jax.numpy as jnp
from jax import lax
from jax.sharding import PartitionSpec as P

TOP = 8
QH = 32
KVH = 4
HD = 128


EPSILON = 1e-06
ROPE_THETA = 1000000.0
NEGATIVE = -1e30


def merged_2(value, axis, join):
    pieces = jax.tree.map(lambda part: lax.all_gather(part, axis), value)
    head = jax.tree.map(lambda part: part[0], pieces)
    tail = jax.tree.map(lambda part: part[1:], pieces)
    running, _ = lax.scan(lambda running, share: (join(running, share), None), head, tail)
    return running


def rms_norm(hidden, gain_vector):
    values = hidden.astype(jnp.float32)
    inverse = lax.rsqrt(jnp.mean(values * values, axis=-1, keepdims=True) + EPSILON)
    return (values * inverse * gain_vector.astype(jnp.float32)).astype(jnp.bfloat16)


def rotate(values, positions):
    head_width = values.shape[-1]
    half_width = head_width // 2
    indices = jnp.arange(half_width).astype(jnp.float32)
    inverse = ROPE_THETA ** (-2.0 * indices / head_width)
    angles = positions.astype(jnp.float32)[:, None] * inverse[None, :]
    cosine = jnp.concatenate([jnp.cos(angles), jnp.cos(angles)], axis=-1)[:, None, :]
    sine_part = jnp.concatenate([jnp.sin(angles), jnp.sin(angles)], axis=-1)[:, None, :]
    floats = values.astype(jnp.float32)
    turned = jnp.concatenate([-floats[..., half_width:], floats[..., :half_width]], axis=-1)
    return (floats * cosine + turned * sine_part).astype(jnp.bfloat16)


def segment_positions(segment_rows):
    earlier = jnp.sum((segment_rows[None, :] < segment_rows[:, None]).astype(jnp.int32), axis=1)
    return jnp.arange(segment_rows.shape[0], dtype=jnp.int32) - earlier


def spread_norm(hidden, gain_vector):
    gathered = lax.all_gather(hidden, "col", axis=1, tiled=True)
    return (gathered, rms_norm(gathered, gain_vector))


def join_partials(first, second):
    highest = jnp.maximum(first[0], second[0])
    factor_one = jnp.exp(first[0] - highest)
    factor_two = jnp.exp(second[0] - highest)
    weight_mass = first[1] * factor_one + second[1] * factor_two
    accum_out = first[2] * factor_one[..., None] + second[2] * factor_two[..., None]
    return (highest, weight_mass, accum_out)


def shards(
    attn_context,
    residual,
    w_out,
    gain_post,
    gain_input,
    routes,
    router_scores,
    w_gate,
    w_up,
    w_down,
    w_query,
    w_keyval,
    segment_ids,
    cache_lengths,
    holders,
    cache_keys,
    cache_values,
):
    col_index = lax.axis_index("col")
    col_count = lax.axis_size("col")
    row_count = lax.axis_size("row")
    tok_rows = attn_context.shape[0]
    share_width = residual.shape[1]
    model_width = share_width * col_count
    projected = jnp.dot(attn_context, w_out, preferred_element_type=jnp.float32)
    summed = lax.psum_scatter(projected, "col", scatter_dimension=1, tiled=True)
    hidden_mid = (residual.astype(jnp.float32) + summed).astype(jnp.bfloat16)
    full_mid, normed = spread_norm(hidden_mid, gain_post)
    group_width = col_count // 2
    expert_count = row_count * group_width
    capacity = 2 * tok_rows * TOP // expert_count
    route_weight = router_scores / jnp.sum(router_scores, axis=1, keepdims=True)
    matching = routes % group_width == col_index // 2
    target = routes // group_width
    dest_ids = jnp.arange(row_count, dtype=jnp.int32)
    hitting = matching[:, :, None] & (target[:, :, None] == dest_ids[None, None, :])
    sent_flag = jnp.sum(hitting.astype(jnp.int32), axis=1)
    sent_weight = jnp.sum(jnp.where(hitting, route_weight[:, :, None], 0.0), axis=1)
    place = jnp.cumsum(sent_flag, axis=0) - sent_flag
    dest_or_drop = jnp.where(sent_flag > 0, dest_ids[None, :], row_count)
    row_ids = jnp.broadcast_to(
        jnp.arange(tok_rows, dtype=jnp.int32)[:, None], (tok_rows, row_count)
    )
    slot_rows = (
        jnp.full((row_count, capacity), tok_rows, jnp.int32)
        .at[dest_or_drop, place]
        .set(row_ids, mode="drop")
    )
    slot_weight = (
        jnp.zeros((row_count, capacity), jnp.float32)
        .at[dest_or_drop, place]
        .set(sent_weight, mode="drop")
    )
    padded = jnp.concatenate([normed, jnp.zeros((1, model_width), jnp.bfloat16)], axis=0)
    outgoing = padded[slot_rows]
    gate_local = w_gate[0]
    up_local = w_up[0]
    down_local = w_down[0]
    arrived = lax.all_to_all(outgoing, "row", split_axis=0, concat_axis=0, tiled=True)
    flat_rows = arrived.reshape(-1, arrived.shape[2])
    gate_part = jnp.dot(flat_rows, gate_local, preferred_element_type=jnp.float32)
    up_part = jnp.dot(flat_rows, up_local, preferred_element_type=jnp.float32)
    inner = (jax.nn.silu(gate_part) * up_part).astype(jnp.bfloat16)
    result = jnp.dot(inner, down_local, preferred_element_type=jnp.float32).astype(jnp.bfloat16)
    returned = lax.all_to_all(
        result.reshape(arrived.shape), "row", split_axis=0, concat_axis=0, tiled=True
    )
    weighted = slot_weight[:, :, None] * returned.astype(jnp.float32)
    partial_moe = (
        jnp.zeros((tok_rows, model_width), jnp.float32)
        .at[slot_rows.reshape(-1)]
        .add(weighted.reshape(-1, model_width), mode="drop")
    )
    moe_share = lax.psum_scatter(partial_moe, "col", scatter_dimension=1, tiled=True)
    hidden_out = (hidden_mid.astype(jnp.float32) + moe_share).astype(jnp.bfloat16)
    _, x_in = spread_norm(hidden_out, gain_input)
    heads_local = QH // col_count
    dec_count = cache_lengths.shape[0]
    score_scale = HD ** (-0.5)
    query_local = (
        jnp.dot(x_in, w_query, preferred_element_type=jnp.float32)
        .astype(jnp.bfloat16)
        .reshape(tok_rows, heads_local, HD)
    )
    keyval_local = jnp.dot(x_in, w_keyval, preferred_element_type=jnp.float32).astype(jnp.bfloat16)
    position = jnp.concatenate([cache_lengths, segment_positions(segment_ids[0])], axis=0)
    query_rot = rotate(query_local, position)
    dec_query = query_rot[:dec_count].reshape(dec_count, heads_local * HD)
    keyval_all, payload = (
        lax.all_gather(keyval_local, "col", axis=1, tiled=True),
        lax.all_gather(dec_query, "col", axis=1, tiled=True),
    )
    keyval_heads = keyval_all.reshape(tok_rows, KVH, 2, HD)
    key_rot = rotate(keyval_heads[:, :, 0, :], position)
    value_rows = keyval_heads[:, :, 1, :]
    cache_full = jnp.stack([key_rot, value_rows], axis=2).reshape(tok_rows, 2 * KVH * HD)
    cache_share = cache_full.shape[1] // col_count
    new_cache = lax.dynamic_slice_in_dim(cache_full, col_index * cache_share, cache_share, 1)
    head_kv = col_index * heads_local // (QH // KVH)
    my_keys = lax.dynamic_index_in_dim(key_rot, head_kv, 1, keepdims=False)
    my_values = lax.dynamic_index_in_dim(value_rows, head_kv, 1, keepdims=False)
    prompt_query = query_rot[dec_count:]
    prompt_keys = my_keys[dec_count:]
    prompt_values = my_values[dec_count:]
    prompt_rows = prompt_query.shape[0]
    scores = (
        jnp.einsum("ihd,jd->hij", prompt_query, prompt_keys, preferred_element_type=jnp.float32)
        * score_scale
    )
    ordinal = jnp.arange(prompt_rows)
    segment_rows = segment_ids[0]
    allowed = (segment_rows[:, None] == segment_rows[None, :]) & (
        ordinal[None, :] <= ordinal[:, None]
    )
    scores = jnp.where(allowed[None, :, :], scores, NEGATIVE)
    highest = jnp.max(scores, axis=-1, keepdims=True)
    exponent = jnp.exp(scores - highest)
    probability = (exponent / jnp.sum(exponent, axis=-1, keepdims=True)).astype(jnp.bfloat16)
    prompt_out = jnp.einsum(
        "hij,jd->ihd", probability, prompt_values, preferred_element_type=jnp.float32
    )
    prompt_out = prompt_out.astype(jnp.bfloat16).reshape(prompt_rows, heads_local * HD)
    holder_dev = holders // dec_count
    holder_slot = holders % dec_count
    outbox = (
        jnp.zeros((row_count, dec_count, payload.shape[1]), jnp.bfloat16)
        .at[holder_dev, holder_slot]
        .set(payload)
    )
    length_box = (
        jnp.zeros((row_count, dec_count), jnp.int32).at[holder_dev, holder_slot].set(cache_lengths)
    )
    inbox, length_in = (
        lax.all_to_all(outbox, "row", split_axis=0, concat_axis=0, tiled=True),
        lax.all_to_all(length_box, "row", split_axis=0, concat_axis=0, tiled=True),
    )
    slot_query = jnp.sum(inbox.astype(jnp.float32), axis=0).astype(jnp.bfloat16)
    slot_length = jnp.sum(length_in, axis=0)
    span_len = cache_keys.shape[1]
    span_start = col_index * span_len
    grouped = slot_query.reshape(dec_count, KVH, QH // KVH, HD)
    held_keys = cache_keys.reshape(dec_count, span_len, KVH, HD)
    held_values = cache_values.reshape(dec_count, span_len, KVH, HD).astype(jnp.float32)
    held_scores = (
        jnp.einsum("sgqd,stgd->sgqt", grouped, held_keys, preferred_element_type=jnp.float32)
        * score_scale
    )
    valid = ((span_start + jnp.arange(span_len))[None, :] < slot_length[:, None])[:, None, None, :]
    held_scores = jnp.where(valid, held_scores, NEGATIVE)
    score_top = jnp.max(held_scores, axis=-1)
    held_exp = jnp.where(valid, jnp.exp(held_scores - score_top[..., None]), 0.0)
    weight_mass = jnp.sum(held_exp, axis=-1).reshape(dec_count, QH)
    accum_out = jnp.einsum(
        "sgqt,stgd->sgqd", held_exp, held_values, precision=lax.Precision.HIGHEST
    ).reshape(dec_count, QH, HD)
    score_top = score_top.reshape(dec_count, QH)
    merged = merged_2((score_top, weight_mass, accum_out), "col", join_partials)
    part_top = lax.dynamic_slice_in_dim(merged[0], col_index * heads_local, heads_local, 1)
    part_mass = lax.dynamic_slice_in_dim(merged[1], col_index * heads_local, heads_local, 1)
    part_accum = lax.dynamic_slice_in_dim(merged[2], col_index * heads_local, heads_local, 1)
    reply_top = jnp.broadcast_to(part_top[None], (row_count,) + part_top.shape)
    reply_mass = jnp.broadcast_to(part_mass[None], (row_count,) + part_mass.shape)
    reply_accum = jnp.broadcast_to(part_accum[None], (row_count,) + part_accum.shape)
    back_top, back_mass, back_accum = (
        lax.all_to_all(reply_top, "row", split_axis=0, concat_axis=0, tiled=True),
        lax.all_to_all(reply_mass, "row", split_axis=0, concat_axis=0, tiled=True),
        lax.all_to_all(reply_accum, "row", split_axis=0, concat_axis=0, tiled=True),
    )
    remote_top = back_top[holder_dev, holder_slot]
    remote_mass = back_mass[holder_dev, holder_slot]
    remote_accum = back_accum[holder_dev, holder_slot]
    own_query = query_rot[:dec_count].astype(jnp.float32)
    own_key = my_keys[:dec_count].astype(jnp.float32)
    own_value = my_values[:dec_count].astype(jnp.float32)
    own_score = (
        jnp.einsum("shd,sd->sh", own_query, own_key, precision=lax.Precision.HIGHEST) * score_scale
    )
    final_top = jnp.maximum(remote_top, own_score)
    remote_factor = jnp.exp(remote_top - final_top)
    own_factor = jnp.exp(own_score - final_top)
    numerator = (
        remote_accum * remote_factor[..., None] + own_factor[..., None] * own_value[:, None, :]
    )
    denominator = remote_mass * remote_factor + own_factor
    decode_out = (
        (numerator / denominator[..., None])
        .reshape(dec_count, heads_local * HD)
        .astype(jnp.bfloat16)
    )
    attention_out = jnp.concatenate([decode_out, prompt_out], axis=0)
    return (hidden_out, new_cache, attention_out)


def solution(mesh):
    return jax.shard_map(
        shards,
        mesh=mesh,
        in_specs=(
            P("row", "col"),
            P("row", "col"),
            P("col", None),
            P(),
            P(),
            P("row", None),
            P("row", None),
            P(("row", "col"), None, None),
            P(("row", "col"), None, None),
            P(("row", "col"), None, None),
            P(None, "col"),
            P(None, "col"),
            P("row", None),
            P("row"),
            P("row"),
            P("row", "col", None),
            P("row", "col", None),
        ),
        out_specs=(P("row", "col"), P("row", "col"), P("row", "col")),
        check_vma=False,
    )
```

profile of v0, /device:TPU:0, one launch (start us, length us, event | category | flops | bytes accessed | tf_op | source)
XLA Modules:
  0.0 961.8 jit_solution(10303194060444963409)
XLA Ops:
  7.2 6.9 fusion.94
  14.2 79.6 %reduce-scatter.3.cloned.1.call-done = f32[512,512]{1,0:T(8,128)} async-done(((f32[512,2048]{1,0:T(8,128)}), f32[512,512]{1,0:T(8,128)}) %reduce-scatter.3.cloned.1.call-update) | async-done | bytes 1048592 | tf_op jit(solution)/shard_map/reduce_scatter | solution.py:89
  98.2 15.5 %scatter_custom_fusion.3 = s32[4096]{0:T(1024)S(1)} fusion(s32[4096]{0:T(1024)S(1)} %reshape.353, s32[4096]{0:T(1024)S(1)} %reshape.355, s32[]{:T(128)} %constant.122.clone.1), kind=kCustom, calls=%fused_computation.130 | custom fusion | bytes 16388
  113.8 28.8 %all-gather.4.cloned.1.call-done = bf16[512,2048]{1,0:T(8,128)(2,1)} async-done(((bf16[512,512]{1,0:T(8,128)(2,1)}), bf16[512,2048]{1,0:T(8,128)(2,1)}) %all-gather.4.cloned.1.call-update) | async-done | bytes 2097168 | tf_op jit(solution)/shard_map/all_gather | solution.py:50
  148.3 33.2 %gather_fusion = bf16[4096,2048]{1,0:T(8,128)(2,1)} fusion(bf16[513,2048]{1,0:T(8,128)(2,1)} %concatenate.52, s32[4096]{0:T(1024)S(1)} %broadcast_clamp_fusion), kind=kCustom, calls=%fused_computation | custom fusion | bytes 33570816 | tf_op jit(solution)/shard_map/gather | solution.py:118
  181.5 188.4 %all_to_all.39 = bf16[8,512,2048]{2,1,0:T(8,128)(2,1)S(1)} all-to-all(bf16[8,512,2048]{2,1,0:T(8,128)(2,1)} %bitcast.166), channel_id=1, replica_groups=mesh['row'=8,'col'=4] {'row'}, dimensions={0} | all-to-all | bytes 33554432 | tf_op jit(solution)/shard_map/all_to_all | solution.py:122
  369.9 5.7 copy-done.1
  375.6 10.8 %fusion.29 = f32[4096,384]{1,0:T(8,128)} fusion(bf16[4096,2048]{1,0:T(8,128)(2,1)S(1)} %bitcast.170, bf16[1,2048,384]{2,1,0:T(8,128)(2,1)S(1)} %copy-done.21), kind=kOutput, calls=%fused_computation.56 | convolution fusion | flops 6442450944 | bytes 24641536 | tf_op jit(solution)/shard_map/dot_general | solution.py:124
  386.4 24.8 %convolution_convert_fusion = bf16[4096,2048]{1,0:T(8,128)(2,1)} fusion(bf16[4096,2048]{1,0:T(8,128)(2,1)} %bitcast.171, f32[4096,384]{1,0:T(8,128)} %fusion.29, bf16[1,384,2048]{2,1,0:T(8,128)(2,1)} %param.28, bf16[1,2048,384]{2,1,0:T(8,128)(2,1)} %param.27), kind=kOutput, calls=%fused_computation.19 | convolution fusion | flops 12902727680 | bytes 42991616 | tf_op jit(solution)/shard_map/dot_general | solution.py:127
  411.2 5.9 all-to-all-start.1
  417.5 15.7 %scatter_custom_fusion.4 = f32[4096]{0:T(1024)S(1)} fusion(s32[4096]{0:T(1024)S(1)} %reshape.353, f32[4096]{0:T(1024)S(1)} %reshape.361, f32[]{:T(128)} %constant.121.clone.1), kind=kCustom, calls=%fused_computation.128 | custom fusion | bytes 16388
  433.3 167.7 %all-to-all-done.1 = bf16[8,512,2048]{2,1,0:T(8,128)(2,1)} async-done(((bf16[8,512,2048]{2,1,0:T(8,128)(2,1)}), bf16[8,512,2048]{2,1,0:T(8,128)(2,1)}, u32[]{:S(2)}, u32[]{:S(2)}) %all-to-all-start.1) | async-done | bytes 16777248 | tf_op jit(solution)/shard_map/all_to_all | solution.py:128
  601.1 18.4 %convert_multiply_fusion = f32[8,512,2048]{2,1,0:T(8,128)} fusion(bf16[8,512,2048]{2,1,0:T(8,128)(2,1)} %all-to-all-done.1, f32[8,512]{1,0:T(8,128)S(1)} %reshape.302), kind=kLoop, calls=%fused_computation.18 | loop fusion | flops 16777216 | bytes 50348032 | tf_op jit(solution)/shard_map/mul | solution.py:131
  619.4 54.3 %scatter_custom_fusion = f32[512,2048]{1,0:T(8,128)} fusion(s32[4096]{0:T(1024)S(1)} %bitcast.181, f32[4096,2048]{1,0:T(8,128)} %bitcast.167, f32[]{:T(128)} %constant.121.clone.1), kind=kCustom, calls=%fused_computation.52 | custom fusion | flops 8388608 | bytes 4194816 | tf_op jit(solution)/shard_map/scatter-add | solution.py:135
  673.8 73.8 %reduce-scatter.5.cloned.1.call-done = f32[512,512]{1,0:T(8,128)} async-done(((f32[512,2048]{1,0:T(8,128)}), f32[512,512]{1,0:T(8,128)}) %reduce-scatter.5.cloned.1.call-update) | async-done | bytes 1048592 | tf_op jit(solution)/shard_map/reduce_scatter | solution.py:137
  761.4 35.0 %all-gather.6.cloned.1.call-done = bf16[512,2048]{1,0:T(8,128)(2,1)} async-done(((bf16[512,512]{1,0:T(8,128)(2,1)}), bf16[512,2048]{1,0:T(8,128)(2,1)}) %all-gather.6.cloned.1.call-update) | async-done | bytes 2097168 | tf_op jit(solution)/shard_map/all_gather | solution.py:50
  798.5 5.2 convert_bitcast_fusion
  806.2 13.2 %all_gather.24 = bf16[8,4096]{1,0:T(8,128)(2,1)S(1)} all-gather(bf16[8,1024]{1,0:T(8,128)(2,1)S(1)} %get-tuple-element.78), channel_id=1, replica_groups=mesh['row'=8,'col'=4] {'col'}, dimensions={1}, use_global_device_ids=true | all-gather | bytes 81920 | tf_op jit(solution)/shard_map/all_gather | solution.py:154
  830.6 6.3 all-to-all-done.3
  840.4 21.0 %all_gather.27 = f32[4,8,32,128]{3,2,1,0:T(8,128)S(1)} all-gather(f32[1,8,32,128]{3,2,1,0:T(8,128)S(1)} %fusion.39), channel_id=1, replica_groups=mesh['row'=8,'col'=4] {'col'}, dimensions={0}, use_global_device_ids=true | all-gather | bytes 655360 | tf_op jit(solution)/shard_map/all_gather | solution.py:18
  861.8 13.3 %all_gather.26 = f32[4,8,32]{2,1,0:T(8,128)S(1)} all-gather(f32[1,8,32]{2,1,0:T(8,128)S(1)} %all_gather_reshape.10), channel_id=1, replica_groups=mesh['row'=8,'col'=4] {'col'}, dimensions={0}, use_global_device_ids=true | all-gather | bytes 5120 | tf_op jit(solution)/shard_map/all_gather | solution.py:18
  875.2 13.1 %all_gather.25 = f32[4,8,32]{2,1,0:T(8,128)S(1)} all-gather(f32[1,8,32]{2,1,0:T(8,128)S(1)} %all_gather_reshape.9), channel_id=1, replica_groups=mesh['row'=8,'col'=4] {'col'}, dimensions={0}, use_global_device_ids=true | all-gather | bytes 5120 | tf_op jit(solution)/shard_map/all_gather | solution.py:18
  912.8 4.8 all-to-all-done.4
  930.2 9.2 fusion.92
  (171 shorter events, 97.1 us)
Async XLA Ops:
  7.2 829.8 %copy-start = (bf16[8,256,512]{2,1,0:T(8,128)(2,1)S(1)}, bf16[8,256,512]{2,1,0:T(8,128)(2,1)}, u32[]{:S(2)}) copy-start(bf16[8,256,512]{2,1,0:T(8,128)(2,1)} %param.34) | copy-start | bytes 6291460
  7.2 86.6 %reduce-scatter.3.cloned.1.call-start = ((), (), s32[]{:S(2)}) async-start(), calls=%async_computation.9 | async-start | bytes 5242880 | tf_op jit(solution)/shard_map/reduce_scatter | solution.py:89
  14.1 79.7 %copy-start.11 = (bf16[512,512]{1,0:T(8,128)(2,1)S(1)}, bf16[512,512]{1,0:T(8,128)(2,1)}, u32[]{:S(2)}) copy-start(bf16[512,512]{1,0:T(8,128)(2,1)} %param.20) | copy-start | bytes 1572868
  14.1 81.9 %copy-start.13 = (s32[512,8]{0,1:T(8,128)S(1)}, s32[512,8]{0,1:T(8,128)}, u32[]{:S(2)}) copy-start(s32[512,8]{0,1:T(8,128)} %param.24) | copy-start | bytes 49156
  14.1 83.5 %copy-start.20 = (s32[2]{0:T(128)S(1)}, s32[2]{0:T(128)}, u32[]{:S(2)}) copy-start(s32[2]{0:T(128)} %constant.151) | copy-start | bytes 28
  14.1 83.5 %copy-start.19 = (s32[2]{0:T(128)S(1)}, s32[2]{0:T(128)}, u32[]{:S(2)}) copy-start(s32[2]{0:T(128)} %constant.154) | copy-start | bytes 28
  14.1 99.7 %copy-start.16 = (bf16[2048]{0:T(1024)(128)(2,1)S(1)}, bf16[2048]{0:T(1024)(128)(2,1)}, u32[]{:S(2)}) copy-start(bf16[2048]{0:T(1024)(128)(2,1)} %param.22) | copy-start | bytes 12292
  14.2 128.4 %all-gather.4.cloned.1.call-start = ((), (), s32[]{:S(2)}) async-start(), calls=%async_computation.10 | async-start | bytes 2621440 | tf_op jit(solution)/shard_map/all_gather | solution.py:50
  181.5 194.1 %copy-start.21 = (bf16[1,2048,384]{2,1,0:T(8,128)(2,1)S(1)}, bf16[1,2048,384]{2,1,0:T(8,128)(2,1)}, u32[]{:S(2)}) copy-start(bf16[1,2048,384]{2,1,0:T(8,128)(2,1)} %param.26) | copy-start | bytes 4718596
  411.2 189.8 %all-to-all-start.1 = ((bf16[8,512,2048]{2,1,0:T(8,128)(2,1)}), bf16[8,512,2048]{2,1,0:T(8,128)(2,1)}, u32[]{:S(2)}, u32[]{:S(2)}) async-start(bf16[8,512,2048]{2,1,0:T(8,128)(2,1)} %bitcast.169), calls=%async_computation.2 | async-start | bytes 33554432 | tf_op jit(solution)/shard_map/all_to_all | solution.py:128
  417.1 330.5 %reduce-scatter.5.cloned.1.call-start = ((), (), s32[]{:S(2)}) async-start(), calls=%async_computation.11 | async-start | bytes 5242880 | tf_op jit(solution)/shard_map/reduce_scatter | solution.py:137
  619.4 128.2 %copy-start.4 = (bf16[512,512]{1,0:T(8,128)(2,1)S(1)}, bf16[512,512]{1,0:T(8,128)(2,1)}, u32[]{:S(2)}) copy-start(bf16[512,512]{1,0:T(8,128)(2,1)} %add_convert_fusion.1) | copy-start | bytes 1572868
  673.7 76.1 %copy-start.22 = (s32[8]{0:T(128)S(1)}, s32[8]{0:T(128)}, u32[]{:S(2)}) copy-start(s32[8]{0:T(128)} %param.33) | copy-start | bytes 100
  673.7 76.7 %copy-start.18 = (s32[8]{0:T(128)S(1)}, s32[8]{0:T(128)}, u32[]{:S(2)}) copy-start(s32[8]{0:T(128)} %param.32) | copy-start | bytes 100
  673.7 83.1 %copy-start.17 = (bf16[2048]{0:T(1024)(128)(2,1)S(1)}, bf16[2048]{0:T(1024)(128)(2,1)}, u32[]{:S(2)}) copy-start(bf16[2048]{0:T(1024)(128)(2,1)} %param.23) | copy-start | bytes 12292
  673.7 83.2 %copy-start.15 = (s32[1,504]{1,0:T(1,128)S(1)}, s32[1,504]{1,0:T(1,128)}, u32[]{:S(2)}) copy-start(s32[1,504]{1,0:T(1,128)} %param.31) | copy-start | bytes 6052
  673.7 122.7 %all-gather.6.cloned.1.call-start = ((), (), s32[]{:S(2)}) async-start(), calls=%async_computation.12 | async-start | bytes 2621440 | tf_op jit(solution)/shard_map/all_gather | solution.py:50
  752.7 8.6 all-to-all-start.2
  758.4 46.2 %copy-start.5 = (f32[512,128]{1,0:T(8,128)}, f32[512,128]{1,0:T(8,128)S(1)}, u32[]{:S(2)}) copy-start(f32[512,128]{1,0:T(8,128)S(1)} %get-tuple-element.94) | copy-start | bytes 786436
  823.6 13.4 %all-to-all-start.3 = ((bf16[8,8,4096]{2,1,0:T(8,128)(2,1)}), bf16[8,8,4096]{2,1,0:T(8,128)(2,1)S(1)}, u32[]{:S(2)}, u32[]{:S(2)}) async-start(bf16[8,8,4096]{2,1,0:T(8,128)(2,1)} %scatter_fusion.1), calls=%async_computation.5 | async-start | bytes 1048576 | tf_op jit(solution)/shard_map/all_to_all | solution.py:197
  827.2 91.0 %all-gather.8.cloned.1.call-start = ((), (), s32[]{:S(2)}) async-start(), calls=%async_computation.13 | async-start | bytes 1310720 | tf_op jit(solution)/shard_map/all_gather | solution.py:153
  889.6 8.1 all-to-all-start.5
  898.3 8.1 all-to-all-start.6
  907.1 10.5 %all-to-all-start.4 = ((f32[8,8,8,128]{3,2,1,0:T(8,128)}), f32[8,8,8,128]{3,2,1,0:T(8,128)S(1)}, u32[]{:S(2)}, u32[]{:S(2)}) async-start(f32[8,8,8,128]{3,2,1,0:T(8,128)} %broadcast_in_dim.99), calls=%async_computation.6 | async-start | bytes 524288 | tf_op jit(solution)/shard_map/all_to_all | solution.py:230
  (10 other events, 43.0 us)
Sparse Core Ops, SparseCore 0:
  14.3 79.4 reduce-scatter.2
  96.1 46.4 all-gather.3
  673.9 73.6 reduce-scatter.4
  749.9 46.4 all-gather.5
  830.8 36.9 all-gather.7
where the time goes:
time: 968 us; the launch traced here: 962 us
  waiting for transfers between devices  409 us (42%)
  blocking collectives  249 us (26%)
  other arithmetic  106 us (11%)
  local copies, waits for them, and re-layouts  97.9 us (10%)
  matrix products  61.9 us (6%)
  starting transfers between devices  24 us (2%)
  between operations  14.6 us (2%)
    all_to_all x1, blocking collectives, shards(): lax.all_to_all(outgoing, 'row', split_axis=0, concat_axis=0, tiled=True)  188 us
    all_to_all x1, waiting for transfers between devices, shards(): lax.all_to_all(result.reshape(arrived.shape), 'row', split_axis=0, concat...  168 us
    reduce_scatter x1, waiting for transfers between devices, shards(): summed = lax.psum_scatter(projected, 'col', scatter_dimension=1, tiled=True)  79.6 us
    reduce_scatter x1, waiting for transfers between devices, shards(): lax.psum_scatter(partial_moe, 'col', scatter_dimension=1, tiled=True)  73.8 us
    all_gather x2, waiting for transfers between devices, spread_norm(): gathered = lax.all_gather(hidden, 'col', axis=1, tiled=True)  63.8 us
    scatter-add x1, other arithmetic, shards(): partial_moe = jnp.zeros((tok_rows, model_width), jnp.float32).at[slot_row...  54.3 us
    all_gather x3, blocking collectives, merged_2(): pieces = jax.tree.map(lambda part: lax.all_gather(part, axis), value)  47.5 us
    unnamed x54, local copies, waits for them, and re-layouts  42.5 us
  transfers between devices with their start and end apart: 11, of which 10 were waited for; matrix products, arithmetic and copies ran while one was open for 5% of the time, Pallas kernels for 0%

commit v1 on v0

v1 whole, which is shorter than its diff:
```python
import jax
import jax.numpy as jnp
from jax import lax
from jax.sharding import PartitionSpec as P

TOP = 8
QH = 32
KVH = 4
HD = 128


EPSILON = 1e-06
ROPE_THETA = 1000000.0
NEGATIVE = -1e30
DOWN_PARTS = 2


def rms_norm(hidden, gain_vector):
    values = hidden.astype(jnp.float32)
    inverse = lax.rsqrt(jnp.mean(values * values, axis=-1, keepdims=True) + EPSILON)
    return (values * inverse * gain_vector.astype(jnp.float32)).astype(jnp.bfloat16)


def rotate(values, positions):
    head_width = values.shape[-1]
    half_width = head_width // 2
    indices = jnp.arange(half_width).astype(jnp.float32)
    inverse = ROPE_THETA ** (-2.0 * indices / head_width)
    angles = positions.astype(jnp.float32)[:, None] * inverse[None, :]
    cosine = jnp.concatenate([jnp.cos(angles), jnp.cos(angles)], axis=-1)[:, None, :]
    sine_part = jnp.concatenate([jnp.sin(angles), jnp.sin(angles)], axis=-1)[:, None, :]
    floats = values.astype(jnp.float32)
    turned = jnp.concatenate([-floats[..., half_width:], floats[..., :half_width]], axis=-1)
    return (floats * cosine + turned * sine_part).astype(jnp.bfloat16)


def segment_positions(segment_rows):
    earlier = jnp.sum((segment_rows[None, :] < segment_rows[:, None]).astype(jnp.int32), axis=1)
    return jnp.arange(segment_rows.shape[0], dtype=jnp.int32) - earlier


def line_scatter(blocks, axis):
    count = blocks.shape[0]
    index = lax.axis_index(axis)

    def own(which):
        return lax.dynamic_index_in_dim(blocks, jnp.clip(which, 0, count - 1), 0, keepdims=False)

    up = down = None
    for step in range(1, count):
        send_up, send_down = own(count - step + index), own(step - count + index)
        if up is not None:
            send_up = send_up + up.astype(jnp.float32)
            send_down = send_down + down.astype(jnp.float32)
        up = lax.ppermute(
            send_up.astype(jnp.bfloat16), axis, [(i, i + 1) for i in range(step)]
        )
        down = lax.ppermute(
            send_down.astype(jnp.bfloat16),
            axis,
            [(count - 1 - i, count - 2 - i) for i in range(step)],
        )
    return own(index) + up.astype(jnp.float32) + down.astype(jnp.float32)


def line_gather(block, axis, count):
    index = lax.axis_index(axis)
    ups, downs = [block], [block]
    for step in range(1, count):
        ups.append(lax.ppermute(ups[-1], axis, [(i, i + 1) for i in range(step - 1, count - 1)]))
        downs.append(
            lax.ppermute(
                downs[-1], axis, [(count - 1 - i, count - 2 - i) for i in range(step - 1, count - 1)]
            )
        )
    return [block] + [
        jnp.where(index >= step, ups[step], downs[count - step]) for step in range(1, count)
    ]


def gather_features(block, axis, count):
    index = lax.axis_index(axis)
    full = jnp.zeros((block.shape[0], count, block.shape[1]), block.dtype)
    for step, piece in enumerate(line_gather(block, axis, count)):
        full = lax.dynamic_update_slice_in_dim(full, piece[:, None], (index - step) % count, 1)
    return full


def row_copies(piece):
    first = [(r, r ^ (4 if r & 1 else 2)) for r in range(8)]
    second = [(r, r ^ (2 if r & 1 else 4)) for r in range(8)]
    core = [(r, r ^ 1) for r in range(8)]
    near = lax.ppermute(piece, "row", first)
    far = lax.ppermute(piece, "row", second)
    diagonal = lax.ppermute(near, "row", second)
    mine = [piece, near, far, diagonal]
    out = []
    for value in mine:
        out.extend([value, lax.ppermute(value, "row", core)])
    return out


def row_sources():
    row = lax.axis_index("row")
    one = jnp.where(row % 2 == 0, 2, 4)
    other = 6 - one
    flips = [0, 1, one, 1 + other, other, 1 + one, 6, 7]
    return [row ^ flip for flip in flips]


def experts_local(normed, routes, route_weight, w_gate, w_up, w_down, col_count, parts):
    tok_rows, model_width = normed.shape
    half = w_gate.shape[2]
    col_index = lax.axis_index("col")
    both = jnp.concatenate([w_gate[0], w_up[0]], axis=1)
    share = model_width // col_count
    down_parts = w_down[0].reshape(half, col_count, parts, share // parts)
    inners = []
    for weights, source in zip(row_copies(both), row_sources()):
        expert = (source * col_count + col_index) // 2
        factor = jnp.sum(jnp.where(routes == expert, route_weight, 0.0), axis=1, keepdims=True)
        products = jnp.dot(normed, weights, preferred_element_type=jnp.float32)
        inners.append(
            (jax.nn.silu(products[:, :half]) * products[:, half:] * factor).astype(jnp.bfloat16)
        )
    sums = []
    for part in range(parts):
        piece = down_parts[:, :, part].reshape(half, col_count * (share // parts))
        total = None
        for inner, weights in zip(inners, row_copies(piece)):
            product = jnp.dot(inner, weights, preferred_element_type=jnp.float32)
            total = product if total is None else total + product
        sums.append(total.reshape(tok_rows, col_count, share // parts))
    return sums


def experts_sent(normed, routes, route_weight, w_gate, w_up, w_down, col_count):
    col_index = lax.axis_index("col")
    row_count = lax.axis_size("row")
    tok_rows, model_width = normed.shape
    group_width = col_count // 2
    capacity = 2 * tok_rows * TOP // (row_count * group_width)
    matching = routes % group_width == col_index // 2
    target = routes // group_width
    dest_ids = jnp.arange(row_count, dtype=jnp.int32)
    hitting = matching[:, :, None] & (target[:, :, None] == dest_ids[None, None, :])
    sent_flag = jnp.sum(hitting.astype(jnp.int32), axis=1)
    sent_weight = jnp.sum(jnp.where(hitting, route_weight[:, :, None], 0.0), axis=1)
    place = jnp.cumsum(sent_flag, axis=0) - sent_flag
    dest_or_drop = jnp.where(sent_flag > 0, dest_ids[None, :], row_count)
    row_ids = jnp.broadcast_to(
        jnp.arange(tok_rows, dtype=jnp.int32)[:, None], (tok_rows, row_count)
    )
    slot_rows = (
        jnp.full((row_count, capacity), tok_rows, jnp.int32)
        .at[dest_or_drop, place]
        .set(row_ids, mode="drop")
    )
    slot_weight = (
        jnp.zeros((row_count, capacity), jnp.float32)
        .at[dest_or_drop, place]
        .set(sent_weight, mode="drop")
    )
    padded = jnp.concatenate([normed, jnp.zeros((1, model_width), jnp.bfloat16)], axis=0)
    outgoing = padded[slot_rows]
    arrived = lax.all_to_all(outgoing, "row", split_axis=0, concat_axis=0, tiled=True)
    flat_rows = arrived.reshape(-1, arrived.shape[2])
    gate_part = jnp.dot(flat_rows, w_gate[0], preferred_element_type=jnp.float32)
    up_part = jnp.dot(flat_rows, w_up[0], preferred_element_type=jnp.float32)
    inner = (jax.nn.silu(gate_part) * up_part).astype(jnp.bfloat16)
    result = jnp.dot(inner, w_down[0], preferred_element_type=jnp.float32).astype(jnp.bfloat16)
    returned = lax.all_to_all(
        result.reshape(arrived.shape), "row", split_axis=0, concat_axis=0, tiled=True
    )
    weighted = slot_weight[:, :, None] * returned.astype(jnp.float32)
    return (
        jnp.zeros((tok_rows, model_width), jnp.float32)
        .at[slot_rows.reshape(-1)]
        .add(weighted.reshape(-1, model_width), mode="drop")
    )


def shards(
    attn_context,
    residual,
    w_out,
    gain_post,
    gain_input,
    routes,
    router_scores,
    w_gate,
    w_up,
    w_down,
    w_query,
    w_keyval,
    segment_ids,
    cache_lengths,
    holders,
    cache_keys,
    cache_values,
):
    col_index = lax.axis_index("col")
    col_count = lax.axis_size("col")
    row_count = lax.axis_size("row")
    tok_rows = attn_context.shape[0]
    share_width = residual.shape[1]
    model_width = share_width * col_count
    dec_count = cache_lengths.shape[0]
    expert_count = row_count * col_count // 2
    dense = row_count == 8 and expert_count <= 2 * TOP

    holder_dev = holders // dec_count
    holder_slot = holders % dec_count
    length_box = (
        jnp.zeros((row_count, dec_count), jnp.int32).at[holder_dev, holder_slot].set(cache_lengths)
    )
    length_in = lax.all_to_all(length_box, "row", split_axis=0, concat_axis=0, tiled=True)
    slot_length = jnp.sum(length_in, axis=0)

    projected = jnp.dot(attn_context, w_out, preferred_element_type=jnp.float32)
    summed = lax.psum_scatter(
        projected.astype(jnp.bfloat16), "col", scatter_dimension=1, tiled=True
    )
    hidden_mid = (residual.astype(jnp.float32) + summed.astype(jnp.float32)).astype(jnp.bfloat16)
    full_mid = lax.all_gather(hidden_mid, "col", axis=1, tiled=True)
    normed = rms_norm(full_mid, gain_post)
    route_weight = router_scores / jnp.sum(router_scores, axis=1, keepdims=True)
    if dense:
        parts = DOWN_PARTS
        width = share_width // parts
        sums = experts_local(
            normed, routes, route_weight, w_gate, w_up, w_down, col_count, parts
        )
        outs, fulls = [], []
        for part, total in enumerate(sums):
            moe_part = line_scatter(jnp.moveaxis(total, 1, 0), "col")
            mid_part = hidden_mid[:, part * width : (part + 1) * width].astype(jnp.float32)
            out_part = (mid_part + moe_part).astype(jnp.bfloat16)
            outs.append(out_part)
            fulls.append(gather_features(out_part, "col", col_count))
        hidden_out = jnp.concatenate(outs, axis=1)
        full_out = jnp.concatenate(fulls, axis=2).reshape(tok_rows, model_width)
    else:
        partial_moe = experts_sent(
            normed, routes, route_weight, w_gate, w_up, w_down, col_count
        )
        moe_share = lax.psum_scatter(partial_moe, "col", scatter_dimension=1, tiled=True)
        hidden_out = (hidden_mid.astype(jnp.float32) + moe_share).astype(jnp.bfloat16)
        full_out = lax.all_gather(hidden_out, "col", axis=1, tiled=True)
    x_in = rms_norm(full_out, gain_input)
    heads_local = QH // col_count
    score_scale = HD ** (-0.5)
    query_local = (
        jnp.dot(x_in, w_query, preferred_element_type=jnp.float32)
        .astype(jnp.bfloat16)
        .reshape(tok_rows, heads_local, HD)
    )
    keyval_local = jnp.dot(x_in, w_keyval, preferred_element_type=jnp.float32).astype(jnp.bfloat16)
    position = jnp.concatenate([cache_lengths, segment_positions(segment_ids[0])], axis=0)
    query_rot = rotate(query_local, position)

    dec_query = query_rot[:dec_count].reshape(dec_count, heads_local * HD)
    outbox = (
        jnp.zeros((row_count, dec_count, heads_local * HD), jnp.bfloat16)
        .at[holder_dev, holder_slot]
        .set(dec_query)
    )
    outbox = jnp.broadcast_to(outbox[:, None], (row_count, col_count) + outbox.shape[1:])
    inbox = lax.all_to_all(
        outbox.reshape((row_count * col_count,) + outbox.shape[2:]),
        ("row", "col"),
        split_axis=0,
        concat_axis=0,
        tiled=True,
    ).reshape(row_count, col_count, dec_count, heads_local * HD)
    slot_query = jnp.sum(inbox.astype(jnp.float32), axis=0).astype(jnp.bfloat16)
    slot_query = jnp.moveaxis(slot_query, 0, 1).reshape(dec_count, QH * HD)

    if keyval_local.shape[1] == 2 * HD:
        my_values = keyval_local[:, HD:]
        my_keys = rotate(keyval_local[:, None, :HD], position)[:, 0]
        new_cache = jnp.concatenate([my_keys, my_values], axis=1)
    else:
        keyval_all = lax.all_gather(keyval_local, "col", axis=1, tiled=True)
        keyval_heads = keyval_all.reshape(tok_rows, KVH, 2, HD)
        key_rot = rotate(keyval_heads[:, :, 0, :], position)
        value_rows = keyval_heads[:, :, 1, :]
        cache_full = jnp.stack([key_rot, value_rows], axis=2).reshape(tok_rows, 2 * KVH * HD)
        cache_share = cache_full.shape[1] // col_count
        new_cache = lax.dynamic_slice_in_dim(cache_full, col_index * cache_share, cache_share, 1)
        head_kv = col_index * heads_local // (QH // KVH)
        my_keys = lax.dynamic_index_in_dim(key_rot, head_kv, 1, keepdims=False)
        my_values = lax.dynamic_index_in_dim(value_rows, head_kv, 1, keepdims=False)

    prompt_query = query_rot[dec_count:]
    prompt_keys = my_keys[dec_count:]
    prompt_values = my_values[dec_count:]
    prompt_rows = prompt_query.shape[0]
    scores = (
        jnp.einsum("ihd,jd->hij", prompt_query, prompt_keys, preferred_element_type=jnp.float32)
        * score_scale
    )
    ordinal = jnp.arange(prompt_rows)
    segment_rows = segment_ids[0]
    allowed = (segment_rows[:, None] == segment_rows[None, :]) & (
        ordinal[None, :] <= ordinal[:, None]
    )
    scores = jnp.where(allowed[None, :, :], scores, NEGATIVE)
    highest = jnp.max(scores, axis=-1, keepdims=True)
    exponent = jnp.exp(scores - highest)
    probability = (exponent / jnp.sum(exponent, axis=-1, keepdims=True)).astype(jnp.bfloat16)
    prompt_out = jnp.einsum(
        "hij,jd->ihd", probability, prompt_values, preferred_element_type=jnp.float32
    )
    prompt_out = prompt_out.astype(jnp.bfloat16).reshape(prompt_rows, heads_local * HD)

    span_len = cache_keys.shape[1]
    span_start = col_index * span_len
    grouped = slot_query.reshape(dec_count, KVH, QH // KVH, HD)
    held_keys = cache_keys.reshape(dec_count, span_len, KVH, HD)
    held_values = cache_values.reshape(dec_count, span_len, KVH, HD).astype(jnp.float32)
    held_scores = (
        jnp.einsum("sgqd,stgd->sgqt", grouped, held_keys, preferred_element_type=jnp.float32)
        * score_scale
    )
    valid = ((span_start + jnp.arange(span_len))[None, :] < slot_length[:, None])[:, None, None, :]
    held_scores = jnp.where(valid, held_scores, NEGATIVE)
    score_top = jnp.max(held_scores, axis=-1)
    held_exp = jnp.where(valid, jnp.exp(held_scores - score_top[..., None]), 0.0)
    weight_mass = jnp.sum(held_exp, axis=-1)
    accum_out = jnp.einsum(
        "sgqt,stgd->sgqd", held_exp, held_values, precision=lax.Precision.HIGHEST
    )

    partial_terms = jnp.concatenate(
        [accum_out, score_top[..., None], weight_mass[..., None]], axis=-1
    ).reshape(dec_count, col_count, heads_local, HD + 2)
    spread_terms = lax.all_to_all(
        jnp.moveaxis(partial_terms, 1, 0), "col", split_axis=0, concat_axis=0, tiled=True
    )
    tops = spread_terms[..., HD]
    part_top = jnp.max(tops, axis=0)
    scale_by = jnp.exp(tops - part_top[None])
    part_mass = jnp.sum(spread_terms[..., HD + 1] * scale_by, axis=0)
    part_accum = jnp.sum(spread_terms[..., :HD] * scale_by[..., None], axis=0)
    reply = jnp.concatenate([part_accum, part_top[..., None], part_mass[..., None]], axis=-1)
    back = lax.all_to_all(
        jnp.broadcast_to(reply[None], (row_count,) + reply.shape),
        "row",
        split_axis=0,
        concat_axis=0,
        tiled=True,
    )
    remote = back[holder_dev, holder_slot]
    remote_top = remote[..., HD]
    remote_mass = remote[..., HD + 1]
    remote_accum = remote[..., :HD]
    own_query = query_rot[:dec_count].astype(jnp.float32)
    own_key = my_keys[:dec_count].astype(jnp.float32)
    own_value = my_values[:dec_count].astype(jnp.float32)
    own_score = jnp.sum(own_query * own_key[:, None, :], axis=-1) * score_scale
    final_top = jnp.maximum(remote_top, own_score)
    remote_factor = jnp.exp(remote_top - final_top)
    own_factor = jnp.exp(own_score - final_top)
    numerator = (
        remote_accum * remote_factor[..., None] + own_factor[..., None] * own_value[:, None, :]
    )
    denominator = remote_mass * remote_factor + own_factor
    decode_out = (
        (numerator / denominator[..., None])
        .reshape(dec_count, heads_local * HD)
        .astype(jnp.bfloat16)
    )
    attention_out = jnp.concatenate([decode_out, prompt_out], axis=0)
    return (hidden_out, new_cache, attention_out)


def solution(mesh):
    return jax.shard_map(
        shards,
        mesh=mesh,
        in_specs=(
            P("row", "col"),
            P("row", "col"),
            P("col", None),
            P(),
            P(),
            P("row", None),
            P("row", None),
            P(("row", "col"), None, None),
            P(("row", "col"), None, None),
            P(("row", "col"), None, None),
            P(None, "col"),
            P(None, "col"),
            P("row", None),
            P("row"),
            P("row"),
            P("row", "col", None),
            P("row", "col", None),
        ),
        out_specs=(P("row", "col"), P("row", "col"), P("row", "col")),
        check_vma=False,
    )
```

time: 968 us -> 440 us (0.45)
  waiting for transfers between devices: 409 us -> 133 us
  blocking collectives: 249 us -> 0 us
  starting transfers between devices: 24 us -> 83.7 us
  other arithmetic: 106 us -> 49 us
  local copies, waits for them, and re-layouts: 97.9 us -> 75.3 us
  matrix products: 61.9 us -> 78.2 us
    all_to_all x1 -> x0, blocking collectives: 188 us -> none  [shards(): lax.all_to_all(outgoing, 'row', split_axis=0, concat_axis=0, tiled=True)]
    all_to_all x5 -> x3, waiting for transfers between devices: 188 us -> 19.4 us  [the longest x1 9.79 us: shards(): lax.all_to_all(jnp.moveaxis(partial_terms, 1, 0), 'col', split_axis=0, co...]
    reduce_scatter x2 -> x1, waiting for transfers between devices: 153 us -> 39.9 us  [shards(): lax.psum_scatter(projected.astype(jnp.bfloat16), 'col', scatter_dimension...]
    ppermute x0 -> x45, starting transfers between devices: none -> 65.7 us  [the longest x6 21.4 us: line_scatter(): lax.ppermute(send_up.astype(jnp.bfloat16), axis, [(i, i + 1) for i in ran...]
    all_gather x4 -> x0, blocking collectives: 60.7 us -> none  [the longest x3 47.5 us: merged_2(): pieces = jax.tree.map(lambda part: lax.all_gather(part, axis), value)]
    scatter-add x1 -> x0, other arithmetic: 54.3 us -> none  [shards(): partial_moe = jnp.zeros((tok_rows, model_width), jnp.float32).at[slot_row...]
    ppermute x0 -> x45, waiting for transfers between devices: none -> 46.6 us  [the longest x3 19.3 us: row_copies(): diagonal = lax.ppermute(near, 'row', second)]
    all_gather x3 -> x1, waiting for transfers between devices: 63.8 us -> 26.7 us  [shards(): full_mid = lax.all_gather(hidden_mid, 'col', axis=1, tiled=True)]
  transfers between devices with their start and end apart: 11 -> 51, of which waited for: 10 -> 13; matrix products, arithmetic and copies ran while one was open for 5% -> 36% of each run, Pallas kernels for 0% -> 0%
where the time goes in v1:
time: 440 us; the launch traced here: 434 us
  waiting for transfers between devices  133 us (30%)
  starting transfers between devices  83.7 us (19%)
  matrix products  78.2 us (18%)
  local copies, waits for them, and re-layouts  75.3 us (17%)
  other arithmetic  49 us (11%)
  between operations  15.6 us (4%)
    reduce_scatter x1, waiting for transfers between devices, shards(): lax.psum_scatter(projected.astype(jnp.bfloat16), 'col', scatter_dimension...  39.9 us
    dot_general x16, matrix products, experts_local(): product = jnp.dot(inner, weights, preferred_element_type=jnp.float32)  35.3 us
    all_gather x1, waiting for transfers between devices, shards(): full_mid = lax.all_gather(hidden_mid, 'col', axis=1, tiled=True)  26.7 us
    another operation x14, local copies, waits for them, and re-layouts  26.5 us
    dot_general x8, matrix products, experts_local(): products = jnp.dot(normed, weights, preferred_element_type=jnp.float32)  24.5 us
    ppermute x6, starting transfers between devices, line_scatter(): lax.ppermute(send_up.astype(jnp.bfloat16), axis, [(i, i + 1) for i in ran...  21.4 us
    ppermute x3, waiting for transfers between devices, row_copies(): diagonal = lax.ppermute(near, 'row', second)  19.3 us
    unnamed x64, local copies, waits for them, and re-layouts  14.6 us
  transfers between devices with their start and end apart: 51, of which 13 were waited for; matrix products, arithmetic and copies ran while one was open for 36% of the time, Pallas kernels for 0%

profile of v1, /device:TPU:0, one launch (start us, length us, event | category | flops | bytes accessed | tf_op | source)
XLA Modules:
  0.0 434.4 jit_solution(9295417849150831700)
XLA Ops:
  7.2 6.3 %convolution_convert_fusion = bf16[512,2048]{1,0:T(8,128)(2,1)} fusion(bf16[512,1024]{1,0:T(8,128)(2,1)} %param.17, bf16[1024,2048]{1,0:T(8,128)(2,1)} %param.19), kind=kOutput, calls=%fused_computation.22 | convolution fusion | flops 2148532224 | bytes 7340032 | tf_op jit(solution)/shard_map/dot_general | solution.py:220
  13.7 3.8 pad_maximum_fusion
  20.4 39.9 %reduce-scatter.2.cloned.1.call-done = bf16[512,512]{1,0:T(8,128)(2,1)} async-done(((bf16[512,2048]{1,0:T(8,128)(2,1)}), bf16[512,512]{1,0:T(8,128)(2,1)}) %reduce-scatter.2.cloned.1.call-update) | async-done | bytes 524304 | tf_op jit(solution)/shard_map/reduce_scatter | solution.py:221
  81.2 26.7 %all-gather.2.cloned.1.call-done = bf16[512,2048]{1,0:T(8,128)(2,1)} async-done(((bf16[512,512]{1,0:T(8,128)(2,1)}), bf16[512,2048]{1,0:T(8,128)(2,1)}) %all-gather.2.cloned.1.call-update) | async-done | bytes 2097168 | tf_op jit(solution)/shard_map/all_gather | solution.py:225
  125.4 3.8 fusion.98
  129.2 13.3 %collective-permute-done.21 = bf16[384,1024]{0,1:T(8,128)(2,1)S(1)} collective-permute-done((bf16[384,1024]{0,1:T(8,128)(2,1)S(1)}, bf16[384,1024]{0,1:T(8,128)(2,1)S(1)}, u32[]{:S(2)}, u32[]{:S(2)}) %collective-permute-start.21) | collective-permute-done | bytes 786464 | tf_op jit(solution)/shard_map/ppermute | solution.py:93
  149.9 9.1 %collective-permute-done.10 = bf16[2048,768]{1,0:T(8,128)(2,1)} collective-permute-done((bf16[2048,768]{1,0:T(8,128)(2,1)}, bf16[2048,768]{1,0:T(8,128)(2,1)}, u32[]{:S(2)}, u32[]{:S(2)}) %collective-permute-start.10) | collective-permute-done | bytes 3145760 | tf_op jit(solution)/shard_map/ppermute | solution.py:95
  174.5 4.9 %collective-permute-done.11 = bf16[384,1024]{0,1:T(8,128)(2,1)S(1)} collective-permute-done((bf16[384,1024]{0,1:T(8,128)(2,1)}, bf16[384,1024]{0,1:T(8,128)(2,1)S(1)}, u32[]{:S(2)}, u32[]{:S(2)}) %collective-permute-start.11) | collective-permute-done | bytes 786464 | tf_op jit(solution)/shard_map/ppermute | solution.py:95
  182.6 5.3 %collective-permute-done.25 = bf16[384,1024]{0,1:T(8,128)(2,1)} collective-permute-done((bf16[384,1024]{0,1:T(8,128)(2,1)S(1)}, bf16[384,1024]{0,1:T(8,128)(2,1)}, u32[]{:S(2)}, u32[]{:S(2)}) %collective-permute-start.25) | collective-permute-done | bytes 786464 | tf_op jit(solution)/shard_map/ppermute | solution.py:95
  208.9 8.5 %add_add_fusion = f32[512,1024]{1,0:T(8,128)} fusion(f32[512,1024]{1,0:T(8,128)} %fusion.123, f32[512,1024]{1,0:T(8,128)} %fusion.122, f32[512,1024]{1,0:T(8,128)} %fusion.121, f32[512,1024]{1,0:T(8,128)} %fusion.120, f32[512,1024]{1,0:T(8,128)} %fusion.119, f32[512,1024]{1,0:T(8,128)} %fusion.117, f32[512,1024]{1,0:T(8,128)} %fusion.118, ...), kind=kOutput, calls=%fused_computation.36 | convolution fusion | flops 407699456 | bytes 19138560 | tf_op jit(solution)/shard_map/dot_general | solution.py:131
  228.0 4.7 %constant_dynamic-slice_fusion.4 = (f32[512,1,256]{0,2,1:T(8,128)}, f32[512,1,256]{0,2,1:T(8,128)}, f32[512,1,256]{0,2,1:T(8,128)}, f32[512,1,256]{0,2,1:T(8,128...) fusion(f32[512,4,256]{0,2,1:T(8,128)} %bitcast.242, ...), kind=kLoop, calls=%fused_computation.176 | loop fusion | bytes 10485780 | tf_op jit(solution)/shard_map/dynamic-slice.9
  259.1 4.8 %collective-permute-start.15 = (bf16[512,256]{1,0:T(8,128)(2,1)S(1)}, bf16[512,256]{1,0:T(8,128)(2,1)S(1)}, u32[]{:S(2)}, u32[]{:S(2)}) collective-permute-start(bf16[512,256]{1,0:T(8,128)(2,1)S(1)} %fusion.55), channel_id=1, source_target_pairs={{0,1},{1,2},{4,5},{5,6},{8,9},{9,10},{12,13},{13,14},{16,17},{17,1... | collective-permute-start | bytes 786440 | tf_op jit(solution)/shard_map/ppermute | solution.py:55
  265.5 5.2 %collective-permute-start.29 = (bf16[512,256]{1,0:T(8,128)(2,1)}, bf16[512,256]{1,0:T(8,128)(2,1)S(1)}, u32[]{:S(2)}, u32[]{:S(2)}) collective-permute-start(bf16[512,256]{1,0:T(8,128)(2,1)} %fusion.49), channel_id=1, source_target_pairs={{0,1},{1,2},{2,3},{4,5},{5,6},{6,7},{8,9},{9,10},{10,11},{12,13},{... | collective-permute-start | bytes 786440 | tf_op jit(solution)/shard_map/ppermute | solution.py:55
  273.5 6.0 %collective-permute-start.16 = (bf16[512,256]{1,0:T(8,128)(2,1)}, bf16[512,256]{1,0:T(8,128)(2,1)}, u32[]{:S(2)}, u32[]{:S(2)}) collective-permute-start(bf16[512,256]{1,0:T(8,128)(2,1)} %fusion.56), channel_id=1, source_target_pairs={{0,1},{1,2},{2,3},{4,5},{5,6},{6,7},{8,9},{9,10},{10,11},{12,13},{... | collective-permute-start | bytes 786440 | tf_op jit(solution)/shard_map/ppermute | solution.py:55
  290.7 3.8 collective-permute-start.33
  296.0 5.3 %collective-permute-start.39 = (bf16[512,256]{1,0:T(8,128)(2,1)S(1)}, bf16[512,256]{1,0:T(8,128)(2,1)}, u32[]{:S(2)}, u32[]{:S(2)}) collective-permute-start(bf16[512,256]{1,0:T(8,128)(2,1)S(1)} %get-tuple-element.45), channel_id=1, source_target_pairs={{0,1},{1,2},{2,3},{4,5},{5,6},{6,7},{8,9},{9,10},{10,11},{12,13},{... | collective-permute-start | bytes 786440 | tf_op jit(solution)/shard_map/ppermute | solution.py:70
  317.5 6.4 %collective-permute-done.41 = bf16[512,256]{1,0:T(8,128)(2,1)S(1)} collective-permute-done((bf16[512,256]{1,0:T(8,128)(2,1)}, bf16[512,256]{1,0:T(8,128)(2,1)S(1)}, u32[]{:S(2)}, u32[]{:S(2)}) %collective-permute-start.41) | collective-permute-done | bytes 262176 | tf_op jit(solution)/shard_map/ppermute | solution.py:72
  360.9 4.5 %fusion.27 = f32[504,504,8]{1,0,2:T(8,128)} fusion(bf16[512,8,128]{2,0,1:T(8,128)(2,1)S(1)} %fusion.18, bf16[512,128]{1,0:T(8,128)(2,1)S(1)} %get-tuple-element.50), kind=kOutput, calls=%fused_computation.46 | convolution fusion | flops 520224768 | bytes 9289728 | tf_op jit(solution)/shard_map/ihd,jd->hij/dot_general | solution.py:300
  367.4 6.0 %all-to-all-start.1 = ((bf16[32,8,1024]{2,1,0:T(8,128)(2,1)}), bf16[32,8,1024]{2,1,0:T(8,128)(2,1)S(1)}, u32[]{:S(2)}, u32[]{:S(2)}) async-start(bf16[32,8,1024]{2,1,0:T(8,128)(2,1)} %bitcast.40), calls=%async_computation.2 | async-start | bytes 1048576 | tf_op jit(solution)/shard_map/all_to_all | solution.py:269
  373.3 9.2 %fusion.106 = (f32[8,504]{1,0:T(8,128)S(1)}, f32[8,504,504]{1,2,0:T(8,128)S(1)}) fusion(f32[504,504,8]{1,0,2:T(8,128)} %fusion.27, pred[504,504]{0,1:T(8,128)(4,1)S(1)} %copy-done.19), kind=kOutput, calls=%fused_computation.224 | output fusion | flops 12193271 | bytes 16527168 | tf_op jit(solution)/shard_map/sub | solution.py:310
  391.7 4.1 all-to-all-start.2
  395.8 9.8 %all-to-all-done.2 = f32[4,8,8,130]{3,2,1,0:T(8,128)S(1)} async-done(((f32[4,8,8,130]{3,2,1,0:T(8,128)}), f32[4,8,8,130]{3,2,1,0:T(8,128)S(1)}, u32[]{:S(2)}, u32[]{:S(2)}) %all-to-all-start.2) | async-done | bytes 133152 | tf_op jit(solution)/shard_map/all_to_all | solution.py:338
  407.6 4.1 all-to-all-start.3
  414.1 7.3 %all-to-all-done.3 = f32[8,8,8,130]{3,2,1,0:T(8,128)} async-done(((f32[8,8,8,130]{3,2,1,0:T(8,128)}), f32[8,8,8,130]{3,2,1,0:T(8,128)}, u32[]{:S(2)}, u32[]{:S(2)}) %all-to-all-start.3) | async-done | bytes 266272 | tf_op jit(solution)/shard_map/all_to_all | solution.py:347
  (293 shorter events, 216.3 us)
Async XLA Ops:
  7.2 53.1 %reduce-scatter.2.cloned.1.call-start = ((), (), s32[]{:S(2)}) async-start(), calls=%async_computation.5 | async-start | bytes 2621440 | tf_op jit(solution)/shard_map/reduce_scatter | solution.py:221
  13.6 94.2 %all-gather.2.cloned.1.call-start = ((), (), s32[]{:S(2)}) async-start(), calls=%async_computation.6 | async-start | bytes 2621440 | tf_op jit(solution)/shard_map/all_gather | solution.py:225
  17.5 61.6 %collective-permute-start.2 = (bf16[2048,768]{1,0:T(8,128)(2,1)}, bf16[2048,768]{1,0:T(8,128)(2,1)}, u32[]{:S(2)}, u32[]{:S(2)}) collective-permute-start(bf16[2048,768]{1,0:T(8,128)(2,1)} %pad_maximum_fusion), channel_id=1, source_target_pairs={{0,8},{4,20},{8,0},{12,28},{16,24},{20,4},{24,16},{28,12},{1,9},{5... | collective-permute-start | bytes 9437192 | tf_op jit(solution)/shard_map/ppermute | solution.py:93
  62.3 80.2 %collective-permute-start.6 = (bf16[2048,768]{1,0:T(8,128)(2,1)}, bf16[2048,768]{1,0:T(8,128)(2,1)}, u32[]{:S(2)}, u32[]{:S(2)}) collective-permute-start(bf16[2048,768]{1,0:T(8,128)(2,1)} %pad_maximum_fusion), channel_id=1, source_target_pairs={{0,16},{4,12},{8,24},{12,4},{16,0},{20,28},{24,8},{28,20},{1,17},{... | collective-permute-start | bytes 9437192 | tf_op jit(solution)/shard_map/ppermute | solution.py:94
  68.9 53.1 %collective-permute-start.3 = (bf16[384,1024]{0,1:T(8,128)(2,1)}, bf16[384,1024]{0,1:T(8,128)(2,1)}, u32[]{:S(2)}, u32[]{:S(2)}) collective-permute-start(bf16[384,1024]{0,1:T(8,128)(2,1)} %bitcast.3), channel_id=1, source_target_pairs={{0,8},{4,20},{8,0},{12,28},{16,24},{20,4},{24,16},{28,12},{1,9},{5... | collective-permute-start | bytes 2359304 | tf_op jit(solution)/shard_map/ppermute | solution.py:93
  70.4 97.0 %collective-permute-start.7 = (bf16[384,1024]{0,1:T(8,128)(2,1)}, bf16[384,1024]{0,1:T(8,128)(2,1)}, u32[]{:S(2)}, u32[]{:S(2)}) collective-permute-start(bf16[384,1024]{0,1:T(8,128)(2,1)} %bitcast.3), channel_id=1, source_target_pairs={{0,16},{4,12},{8,24},{12,4},{16,0},{20,28},{24,8},{28,20},{1,17},{... | collective-permute-start | bytes 2359304 | tf_op jit(solution)/shard_map/ppermute | solution.py:94
  73.9 222.1 %all-to-all-start = ((s32[8,1,8]{2,1,0:T(1,128)}), s32[8,1,8]{2,1,0:T(1,128)S(1)}, u32[]{:S(2)}, u32[]{:S(2)}) async-start(s32[8,1,8]{2,1,0:T(1,128)} %bitcast.38), calls=%async_computation.1 | async-start | bytes 8192 | tf_op jit(solution)/shard_map/all_to_all | solution.py:217
  79.1 46.3 %collective-permute-start.4 = (bf16[2048,768]{1,0:T(8,128)(2,1)}, bf16[2048,768]{1,0:T(8,128)(2,1)}, u32[]{:S(2)}, u32[]{:S(2)}) collective-permute-start(bf16[2048,768]{1,0:T(8,128)(2,1)} %collective-permute-done.2), channel_id=1, source_target_pairs={{0,4},{4,0},{8,12},{12,8},{16,20},{20,16},{24,28},{28,24},{1,5},{5... | collective-permute-start | bytes 9437192 | tf_op jit(solution)/shard_map/ppermute | solution.py:99
  79.5 79.5 %collective-permute-start.10 = (bf16[2048,768]{1,0:T(8,128)(2,1)}, bf16[2048,768]{1,0:T(8,128)(2,1)}, u32[]{:S(2)}, u32[]{:S(2)}) collective-permute-start(bf16[2048,768]{1,0:T(8,128)(2,1)} %collective-permute-done.2), channel_id=1, source_target_pairs={{0,16},{4,12},{8,24},{12,4},{16,0},{20,28},{24,8},{28,20},{1,17},{... | collective-permute-start | bytes 9437192 | tf_op jit(solution)/shard_map/ppermute | solution.py:95
  122.0 20.5 %collective-permute-start.21 = (bf16[384,1024]{0,1:T(8,128)(2,1)S(1)}, bf16[384,1024]{0,1:T(8,128)(2,1)S(1)}, u32[]{:S(2)}, u32[]{:S(2)}) collective-permute-start(bf16[384,1024]{0,1:T(8,128)(2,1)S(1)} %bitcast.246), channel_id=1, source_target_pairs={{0,8},{4,20},{8,0},{12,28},{16,24},{20,4},{24,16},{28,12},{1,9},{5... | collective-permute-start | bytes 2359304 | tf_op jit(solution)/shard_map/ppermute | solution.py:93
  125.4 65.8 %collective-permute-start = (bf16[2048,768]{1,0:T(8,128)(2,1)}, bf16[2048,768]{1,0:T(8,128)(2,1)S(1)}, u32[]{:S(2)}, u32[]{:S(2)}) collective-permute-start(bf16[2048,768]{1,0:T(8,128)(2,1)} %pad_maximum_fusion), channel_id=1, source_target_pairs={{0,4},{4,0},{8,12},{12,8},{16,20},{20,16},{24,28},{28,24},{1,5},{5... | collective-permute-start | bytes 9437192 | tf_op jit(solution)/shard_map/ppermute | solution.py:99
  142.5 37.7 %collective-permute-start.8 = (bf16[2048,768]{1,0:T(8,128)(2,1)}, bf16[2048,768]{1,0:T(8,128)(2,1)S(1)}, u32[]{:S(2)}, u32[]{:S(2)}) collective-permute-start(bf16[2048,768]{1,0:T(8,128)(2,1)} %collective-permute-done.6), channel_id=1, source_target_pairs={{0,4},{4,0},{8,12},{12,8},{16,20},{20,16},{24,28},{28,24},{1,5},{5... | collective-permute-start | bytes 9437192 | tf_op jit(solution)/shard_map/ppermute | solution.py:99
  167.4 30.1 %collective-permute-start.1 = (bf16[384,1024]{0,1:T(8,128)(2,1)}, bf16[384,1024]{0,1:T(8,128)(2,1)S(1)}, u32[]{:S(2)}, u32[]{:S(2)}) collective-permute-start(bf16[384,1024]{0,1:T(8,128)(2,1)} %bitcast.3), channel_id=1, source_target_pairs={{0,4},{4,0},{8,12},{12,8},{16,20},{20,16},{24,28},{28,24},{1,5},{5... | collective-permute-start | bytes 2359304 | tf_op jit(solution)/shard_map/ppermute | solution.py:99
  171.0 17.0 %collective-permute-start.25 = (bf16[384,1024]{0,1:T(8,128)(2,1)S(1)}, bf16[384,1024]{0,1:T(8,128)(2,1)}, u32[]{:S(2)}, u32[]{:S(2)}) collective-permute-start(bf16[384,1024]{0,1:T(8,128)(2,1)S(1)} %collective-permute-done.21), channel_id=1, source_target_pairs={{0,16},{4,12},{8,24},{12,4},{16,0},{20,28},{24,8},{28,20},{1,17},{... | collective-permute-start | bytes 2359304 | tf_op jit(solution)/shard_map/ppermute | solution.py:95
  179.4 21.0 %collective-permute-start.12 = (bf16[2048,768]{1,0:T(8,128)(2,1)}, bf16[2048,768]{1,0:T(8,128)(2,1)S(1)}, u32[]{:S(2)}, u32[]{:S(2)}) collective-permute-start(bf16[2048,768]{1,0:T(8,128)(2,1)} %collective-permute-done.10), channel_id=1, source_target_pairs={{0,4},{4,0},{8,12},{12,8},{16,20},{20,16},{24,28},{28,24},{1,5},{5... | collective-permute-start | bytes 9437192 | tf_op jit(solution)/shard_map/ppermute | solution.py:99
  180.2 18.1 %collective-permute-start.20 = (bf16[384,1024]{0,1:T(8,128)(2,1)S(1)}, bf16[384,1024]{0,1:T(8,128)(2,1)S(1)}, u32[]{:S(2)}, u32[]{:S(2)}) collective-permute-start(bf16[384,1024]{0,1:T(8,128)(2,1)S(1)} %bitcast.248), channel_id=1, source_target_pairs={{0,4},{4,0},{8,12},{12,8},{16,20},{20,16},{24,28},{28,24},{1,5},{5... | collective-permute-start | bytes 2359304 | tf_op jit(solution)/shard_map/ppermute | solution.py:99
  223.5 29.8 %collective-permute-start.27 = (bf16[512,256]{1,0:T(8,128)(2,1)}, bf16[512,256]{1,0:T(8,128)(2,1)}, u32[]{:S(2)}, u32[]{:S(2)}) collective-permute-start(bf16[512,256]{1,0:T(8,128)(2,1)} %bitcast.181), channel_id=1, source_target_pairs={{0,1},{4,5},{8,9},{12,13},{16,17},{20,21},{24,25},{28,29}} | collective-permute-start | bytes 786440 | tf_op jit(solution)/shard_map/ppermute | solution.py:55
  226.5 29.6 %collective-permute-start.30 = (bf16[512,256]{1,0:T(8,128)(2,1)}, bf16[512,256]{1,0:T(8,128)(2,1)}, u32[]{:S(2)}, u32[]{:S(2)}) collective-permute-start(bf16[512,256]{1,0:T(8,128)(2,1)} %bitcast.180), channel_id=1, source_target_pairs={{3,2},{7,6},{11,10},{15,14},{19,18},{23,22},{27,26},{31,30}} | collective-permute-start | bytes 786440 | tf_op jit(solution)/shard_map/ppermute | solution.py:58
  242.7 15.4 %collective-permute-start.14 = (bf16[512,256]{1,0:T(8,128)(2,1)}, bf16[512,256]{1,0:T(8,128)(2,1)}, u32[]{:S(2)}, u32[]{:S(2)}) collective-permute-start(bf16[512,256]{1,0:T(8,128)(2,1)} %bitcast.258), channel_id=1, source_target_pairs={{0,1},{4,5},{8,9},{12,13},{16,17},{20,21},{24,25},{28,29}} | collective-permute-start | bytes 786440 | tf_op jit(solution)/shard_map/ppermute | solution.py:55
  264.1 15.5 %collective-permute-start.18 = (bf16[512,256]{1,0:T(8,128)(2,1)S(1)}, bf16[512,256]{1,0:T(8,128)(2,1)S(1)}, u32[]{:S(2)}, u32[]{:S(2)}) collective-permute-start(bf16[512,256]{1,0:T(8,128)(2,1)S(1)} %fusion.53), channel_id=1, source_target_pairs={{3,2},{2,1},{7,6},{6,5},{11,10},{10,9},{15,14},{14,13},{19,18},{18... | collective-permute-start | bytes 786440 | tf_op jit(solution)/shard_map/ppermute | solution.py:58
  265.5 20.9 %collective-permute-start.29 = (bf16[512,256]{1,0:T(8,128)(2,1)}, bf16[512,256]{1,0:T(8,128)(2,1)S(1)}, u32[]{:S(2)}, u32[]{:S(2)}) collective-permute-start(bf16[512,256]{1,0:T(8,128)(2,1)} %fusion.49), channel_id=1, source_target_pairs={{0,1},{1,2},{2,3},{4,5},{5,6},{6,7},{8,9},{9,10},{10,11},{12,13},{... | collective-permute-start | bytes 786440 | tf_op jit(solution)/shard_map/ppermute | solution.py:55
  313.8 16.5 %collective-permute-start.38 = (bf16[512,256]{1,0:T(8,128)(2,1)}, bf16[512,256]{1,0:T(8,128)(2,1)}, u32[]{:S(2)}, u32[]{:S(2)}) collective-permute-start(bf16[512,256]{1,0:T(8,128)(2,1)} %collective-permute-done.37), channel_id=1, source_target_pairs={{2,3},{6,7},{10,11},{14,15},{18,19},{22,23},{26,27},{30,31}} | collective-permute-start | bytes 786440 | tf_op jit(solution)/shard_map/ppermute | solution.py:70
  315.2 16.8 %collective-permute-start.36 = (bf16[512,256]{1,0:T(8,128)(2,1)}, bf16[512,256]{1,0:T(8,128)(2,1)}, u32[]{:S(2)}, u32[]{:S(2)}) collective-permute-start(bf16[512,256]{1,0:T(8,128)(2,1)} %collective-permute-done.35), channel_id=1, source_target_pairs={{1,0},{5,4},{9,8},{13,12},{17,16},{21,20},{25,24},{29,28}} | collective-permute-start | bytes 786440 | tf_op jit(solution)/shard_map/ppermute | solution.py:72
  367.4 20.3 %all-to-all-start.1 = ((bf16[32,8,1024]{2,1,0:T(8,128)(2,1)}), bf16[32,8,1024]{2,1,0:T(8,128)(2,1)S(1)}, u32[]{:S(2)}, u32[]{:S(2)}) async-start(bf16[32,8,1024]{2,1,0:T(8,128)(2,1)} %bitcast.40), calls=%async_computation.2 | async-start | bytes 1048576 | tf_op jit(solution)/shard_map/all_to_all | solution.py:269
  (55 other events, 929.6 us)
Sparse Core Ops, SparseCore 0:
  13.7 46.5 reduce-scatter.1
  62.5 45.2 all-gather.1

commit v2 on v1

v2 whole, which is shorter than its diff:
```python
import jax
import jax.numpy as jnp
from jax import lax
from jax.experimental import pallas as pl
from jax.experimental.pallas import tpu as pltpu
from jax.sharding import PartitionSpec as P

TOP = 8
QH = 32
KVH = 4
HD = 128


EPSILON = 1e-06
ROPE_THETA = 1000000.0
NEGATIVE = -1e30
PARTS = (1,)
VMEM_BYTES = 52 * 1024 * 1024


def rms_norm(hidden, gain_vector):
    values = hidden.astype(jnp.float32)
    inverse = lax.rsqrt(jnp.mean(values * values, axis=-1, keepdims=True) + EPSILON)
    return (values * inverse * gain_vector.astype(jnp.float32)).astype(jnp.bfloat16)


def rotary_tables(positions):
    half_width = HD // 2
    indices = jnp.arange(half_width).astype(jnp.float32)
    inverse = ROPE_THETA ** (-2.0 * indices / HD)
    angles = positions.astype(jnp.float32)[:, None] * inverse[None, :]
    cosine, sine_part = jnp.cos(angles), jnp.sin(angles)
    return (
        jnp.concatenate([cosine, cosine], axis=-1),
        jnp.concatenate([-sine_part, sine_part], axis=-1),
    )


def rotate(values, tables):
    cosine, sine_part = (table[:, None, :] for table in tables)
    half_width = HD // 2
    floats = values.astype(jnp.float32)
    turned = jnp.concatenate([floats[..., half_width:], floats[..., :half_width]], axis=-1)
    return (floats * cosine + turned * sine_part).astype(jnp.bfloat16)


def segment_positions(segment_rows):
    earlier = jnp.sum((segment_rows[None, :] < segment_rows[:, None]).astype(jnp.int32), axis=1)
    return jnp.arange(segment_rows.shape[0], dtype=jnp.int32) - earlier


def shifted(block, axis, count, shift):
    return lax.ppermute(block, axis, [(i, (i + shift) % count) for i in range(count)])


def shared_sum(block, axis):
    count = lax.axis_size(axis)
    spread = jnp.broadcast_to(block[None], (count,) + block.shape)
    return jnp.sum(lax.all_to_all(spread, axis, 0, 0, tiled=True), axis=0)


def inner_kernel(x_ref, *refs):
    sets, outs = refs[:6], refs[6:]
    tile = outs[0].shape[1]
    weights = jnp.concatenate([sets[0][...], sets[1][...], sets[3][...], sets[4][...]], axis=1)
    products = jnp.dot(x_ref[...], weights, preferred_element_type=jnp.float32)
    for which, out in enumerate(outs):
        gate = products[:, 2 * which * tile : (2 * which + 1) * tile]
        up = products[:, (2 * which + 1) * tile : (2 * which + 2) * tile]
        out[...] = (jax.nn.silu(gate) * up * sets[3 * which + 2][...]).astype(jnp.bfloat16)


def inner_pair(normed, sets):
    tok_rows, model_width = normed.shape
    half = sets[0][0].shape[1] // 2
    tile = 128
    steps = half // tile
    gate = pl.BlockSpec((model_width, tile), lambda step: (0, step))
    up = pl.BlockSpec((model_width, tile), lambda step: (0, step + steps))
    factor = pl.BlockSpec((tok_rows, 1), lambda step: (0, 0))
    return pl.pallas_call(
        inner_kernel,
        grid=(steps,),
        out_shape=[jax.ShapeDtypeStruct((tok_rows, half), jnp.bfloat16)] * 2,
        in_specs=[pl.BlockSpec((tok_rows, model_width), lambda step: (0, 0))]
        + [gate, up, factor] * 2,
        out_specs=[pl.BlockSpec((tok_rows, tile), lambda step: (0, step))] * 2,
        compiler_params=pltpu.CompilerParams(vmem_limit_bytes=VMEM_BYTES),
        cost_estimate=pl.CostEstimate(
            flops=8 * tok_rows * model_width * half,
            bytes_accessed=2 * model_width * (tok_rows + 4 * half),
            transcendentals=2 * tok_rows * half,
        ),
    )(normed, *[value for both, factor in sets for value in (both, both, factor)])


def down_kernel(sets, *refs):
    inners, downs = refs[:sets], refs[sets : 2 * sets]
    acc = None
    for pair in range(0, sets, 2):
        left = jnp.concatenate([inners[pair][...], inners[pair + 1][...]], axis=1)
        right = jnp.concatenate([downs[pair][...], downs[pair + 1][...]], axis=0)
        product = jnp.dot(left, right, preferred_element_type=jnp.float32)
        acc = product if acc is None else acc + product
    if len(refs) == 2 * sets + 1:
        refs[-1][...] = acc
    else:
        before, total_ref, top_ref = refs[2 * sets :]
        acc = acc + before[...]
        total_ref[...] = acc.astype(jnp.bfloat16)
        top_ref[...] = acc[0 : top_ref.shape[0], :]


def down_sum(inners, downs, before=None, tops=0):
    sets = len(inners)
    tok_rows, half = inners[0].shape
    width = downs[0].shape[1]
    tile = 256

    def moving(rows):
        return pl.BlockSpec((rows, tile), lambda step: (0, step))

    whole = jax.ShapeDtypeStruct((tok_rows, width), jnp.float32)
    rounded = [
        jax.ShapeDtypeStruct((tok_rows, width), jnp.bfloat16),
        jax.ShapeDtypeStruct((tops, width), jnp.float32),
    ]
    last = before is not None
    return pl.pallas_call(
        lambda *refs: down_kernel(sets, *refs),
        grid=(width // tile,),
        out_shape=rounded if last else whole,
        in_specs=[pl.BlockSpec((tok_rows, half), lambda step: (0, 0))] * sets
        + [moving(half)] * sets
        + [moving(tok_rows)] * last,
        out_specs=[moving(tok_rows), moving(tops)] if last else moving(tok_rows),
        compiler_params=pltpu.CompilerParams(vmem_limit_bytes=VMEM_BYTES),
        cost_estimate=pl.CostEstimate(
            flops=2 * tok_rows * width * sets * half,
            bytes_accessed=2 * sets * half * (width + tok_rows) + 4 * tok_rows * width,
            transcendentals=0,
        ),
    )(*inners, *downs, *([before] if last else []))


def tail_kernel(count, parts, decs, window, col_ref, *refs):
    fulls = refs[:parts]
    (gain, wq, wkv, cosine, sine, seg_col, seg_row, dec, hidden_ref, cache_ref, out_ref) = refs[
        parts : parts + 11
    ]
    hidden, x_in, keys, values, bias = refs[parts + 11 :]
    tok_rows = x_in.shape[0]
    rows = tok_rows // count

    def turn(block):
        floats = block.astype(jnp.float32)
        turned = pltpu.roll(floats, HD // 2, 1)
        return (floats * cosine[...] + turned * sine[...]).astype(jnp.bfloat16)

    @pl.when(pl.program_id(0) == 0)
    def _():
        col = col_ref[0]
        begin = 0
        for device in range(count):
            for full in fulls:
                width = full.shape[1] // count
                hidden[:, begin : begin + width] = full[:, device * width : (device + 1) * width]
                begin += width
        for start in range(0, tok_rows, rows):
            place = slice(start, start + rows)
            floats = hidden[place, :].astype(jnp.float32)
            inverse = lax.rsqrt(jnp.mean(floats * floats, axis=-1, keepdims=True) + EPSILON)
            x_in[place, :] = (floats * inverse * gain[...].astype(jnp.float32)).astype(jnp.bfloat16)
        share = hidden_ref.shape[1]
        hidden_ref[...] = hidden[:, pl.ds(pl.multiple_of(col * share, share), share)]
        keyval = jnp.dot(x_in[...], wkv[...], preferred_element_type=jnp.float32)
        keyval = keyval.astype(jnp.bfloat16)
        keys[...] = turn(keyval[:, :HD])
        values[...] = keyval[:, HD:]
        cache_ref[:, :HD] = keys[...]
        cache_ref[:, HD:] = values[...]
        ordinal = lax.broadcasted_iota(jnp.int32, (tok_rows, tok_rows), 0)
        other = lax.broadcasted_iota(jnp.int32, (tok_rows, tok_rows), 1)
        allowed = (seg_col[...] == seg_row[...]) & (other <= ordinal)
        bias[...] = jnp.where(allowed, 0.0, NEGATIVE)

    queries = jnp.dot(x_in[...], wq[...], preferred_element_type=jnp.float32).astype(jnp.bfloat16)
    step = 128
    for head in range(wq.shape[1] // HD):
        lanes = slice(head * HD, (head + 1) * HD)
        query = turn(queries[:, lanes])
        for start in range(0, tok_rows, step):
            first = max(0, (start - window + 1) // step * step)
            stop = start + step
            scores = (
                lax.dot_general(
                    query[start:stop],
                    keys[first:stop, :],
                    (((1,), (1,)), ((), ())),
                    preferred_element_type=jnp.float32,
                )
                * HD ** (-0.5)
                + bias[start:stop, first:stop]
            )
            highest = jnp.max(scores, axis=-1, keepdims=True)
            exponent = jnp.exp(scores - highest)
            mass = jnp.sum(exponent, axis=-1, keepdims=True)
            weights = (exponent * (1.0 / mass)).astype(jnp.bfloat16)
            mixed = jnp.dot(weights, values[first:stop, :], preferred_element_type=jnp.float32)
            mixed = mixed.astype(jnp.bfloat16)
            if start == 0:
                top = lax.broadcasted_iota(jnp.int32, (16, HD), 0)
                out_ref[0:16, lanes] = jnp.where(top < decs, dec[:, lanes], mixed[0:16])
                out_ref[16:stop, lanes] = mixed[16:]
            else:
                out_ref[start:stop, lanes] = mixed


def tail(fulls, count, gain, w_query, w_keyval, cosine, sine, segments, decode_out, col_index):
    decs = decode_out.shape[0]
    tok_rows = segments.shape[0]
    model_width = w_query.shape[0]
    query_width = w_query.shape[1]
    pair = 2 * HD
    dec_rows = jnp.pad(decode_out, ((0, 16 - decs), (0, 0)))

    def fixed(shape):
        return pl.BlockSpec(shape, lambda step: (0, 0))

    def moving(shape):
        return pl.BlockSpec(shape, lambda step: (0, step))

    share = model_width // count
    return pl.pallas_call(
        lambda *refs: tail_kernel(count, len(fulls), decs, (tok_rows - decs) // 2, *refs),
        grid=(query_width // pair,),
        out_shape=[
            jax.ShapeDtypeStruct((tok_rows, share), jnp.bfloat16),
            jax.ShapeDtypeStruct((tok_rows, pair), jnp.bfloat16),
            jax.ShapeDtypeStruct((tok_rows, query_width), jnp.bfloat16),
        ],
        in_specs=[pl.BlockSpec(memory_space=pltpu.SMEM)]
        + [fixed(full.shape) for full in fulls]
        + [
            fixed((1, model_width)),
            moving((model_width, pair)),
            fixed((model_width, pair)),
            fixed((tok_rows, HD)),
            fixed((tok_rows, HD)),
            fixed((tok_rows, 1)),
            fixed((1, tok_rows)),
            moving((16, pair)),
        ],
        out_specs=[fixed((tok_rows, share)), fixed((tok_rows, pair)), moving((tok_rows, pair))],
        scratch_shapes=[
            pltpu.VMEM((tok_rows, model_width), jnp.bfloat16),
            pltpu.VMEM((tok_rows, model_width), jnp.bfloat16),
            pltpu.VMEM((tok_rows, HD), jnp.bfloat16),
            pltpu.VMEM((tok_rows, HD), jnp.bfloat16),
            pltpu.VMEM((tok_rows, tok_rows), jnp.float32),
        ],
        compiler_params=pltpu.CompilerParams(vmem_limit_bytes=VMEM_BYTES),
        cost_estimate=pl.CostEstimate(
            flops=2 * tok_rows * model_width * (query_width + pair),
            bytes_accessed=2 * model_width * (query_width + pair + 2 * tok_rows),
            transcendentals=tok_rows * tok_rows * query_width // HD,
        ),
    )(
        col_index[None],
        *fulls,
        gain[None],
        w_query,
        w_keyval,
        cosine,
        sine,
        segments[:, None],
        segments[None],
        dec_rows,
    )


def ordered(*values):
    return lax.optimization_barrier(values)


def row_pairs():
    first = [(r, r ^ (4 if r & 1 else 2)) for r in range(8)]
    second = [(r, r ^ (2 if r & 1 else 4)) for r in range(8)]
    core = [(r, r ^ 1) for r in range(8)]
    return first, second, core


def both_cores(*values):
    core = row_pairs()[2]
    out = []
    for value in values:
        out.extend([value, lax.ppermute(value, "row", core)])
    return out


def row_sources():
    row = lax.axis_index("row")
    one = jnp.where(row % 2 == 0, 2, 4)
    other = 6 - one
    flips = [0, 1, one, 1 + other, other, 1 + one, 6, 7]
    return [row ^ flip for flip in flips]


def expert_of(source, col_count):
    return (source * col_count + lax.axis_index("col")) // 2


def naming(routes, route_weight, expert):
    return jnp.sum(jnp.where(routes == expert, route_weight, 0.0), axis=1, keepdims=True)


def inner_of(rows, gate, up, factor):
    gate_part = jnp.dot(rows, gate, preferred_element_type=jnp.float32)
    up_part = jnp.dot(rows, up, preferred_element_type=jnp.float32)
    return (jax.nn.silu(gate_part) * up_part * factor).astype(jnp.bfloat16)


def experts_sent(normed, routes, route_weight, w_gate, w_up, w_down, col_count):
    col_index = lax.axis_index("col")
    row_count = lax.axis_size("row")
    tok_rows, model_width = normed.shape
    group_width = col_count // 2
    capacity = 2 * tok_rows * TOP // (row_count * group_width)
    matching = routes % group_width == col_index // 2
    target = routes // group_width
    dest_ids = jnp.arange(row_count, dtype=jnp.int32)
    hitting = matching[:, :, None] & (target[:, :, None] == dest_ids[None, None, :])
    sent_flag = jnp.sum(hitting.astype(jnp.int32), axis=1)
    sent_weight = jnp.sum(jnp.where(hitting, route_weight[:, :, None], 0.0), axis=1)
    place = jnp.cumsum(sent_flag, axis=0) - sent_flag
    dest_or_drop = jnp.where(sent_flag > 0, dest_ids[None, :], row_count)
    row_ids = jnp.broadcast_to(
        jnp.arange(tok_rows, dtype=jnp.int32)[:, None], (tok_rows, row_count)
    )
    slot_rows = (
        jnp.full((row_count, capacity), tok_rows, jnp.int32)
        .at[dest_or_drop, place]
        .set(row_ids, mode="drop")
    )
    slot_weight = (
        jnp.zeros((row_count, capacity), jnp.float32)
        .at[dest_or_drop, place]
        .set(sent_weight, mode="drop")
    )
    padded = jnp.concatenate([normed, jnp.zeros((1, model_width), jnp.bfloat16)], axis=0)
    outgoing = padded[slot_rows]
    arrived = lax.all_to_all(outgoing, "row", split_axis=0, concat_axis=0, tiled=True)
    flat_rows = arrived.reshape(-1, arrived.shape[2])
    gate_part = jnp.dot(flat_rows, w_gate[0], preferred_element_type=jnp.float32)
    up_part = jnp.dot(flat_rows, w_up[0], preferred_element_type=jnp.float32)
    inner = (jax.nn.silu(gate_part) * up_part).astype(jnp.bfloat16)
    result = jnp.dot(inner, w_down[0], preferred_element_type=jnp.float32).astype(jnp.bfloat16)
    returned = lax.all_to_all(
        result.reshape(arrived.shape), "row", split_axis=0, concat_axis=0, tiled=True
    )
    weighted = slot_weight[:, :, None] * returned.astype(jnp.float32)
    return (
        jnp.zeros((tok_rows, model_width), jnp.float32)
        .at[slot_rows.reshape(-1)]
        .add(weighted.reshape(-1, model_width), mode="drop")
    )


def prompt_attention(prompt_query, prompt_keys, prompt_values, segment_rows):
    prompt_rows = prompt_query.shape[0]
    scores = jnp.einsum(
        "ihd,jd->hij", prompt_query, prompt_keys, preferred_element_type=jnp.float32
    ) * HD ** (-0.5)
    ordinal = jnp.arange(prompt_rows)
    allowed = (segment_rows[:, None] == segment_rows[None, :]) & (
        ordinal[None, :] <= ordinal[:, None]
    )
    scores = jnp.where(allowed[None, :, :], scores, NEGATIVE)
    highest = jnp.max(scores, axis=-1, keepdims=True)
    exponent = jnp.exp(scores - highest)
    probability = (exponent / jnp.sum(exponent, axis=-1, keepdims=True)).astype(jnp.bfloat16)
    prompt_out = jnp.einsum(
        "hij,jd->ihd", probability, prompt_values, preferred_element_type=jnp.float32
    )
    return prompt_out.astype(jnp.bfloat16).reshape(prompt_rows, -1)


def shards(
    attn_context,
    residual,
    w_out,
    gain_post,
    gain_input,
    routes,
    router_scores,
    w_gate,
    w_up,
    w_down,
    w_query,
    w_keyval,
    segment_ids,
    cache_lengths,
    holders,
    cache_keys,
    cache_values,
):
    col_index = lax.axis_index("col")
    col_count = lax.axis_size("col")
    row_count = lax.axis_size("row")
    tok_rows = attn_context.shape[0]
    share_width = residual.shape[1]
    model_width = share_width * col_count
    dec_count = cache_lengths.shape[0]
    expert_count = row_count * col_count // 2
    dense = row_count == 8 and expert_count <= 2 * TOP and col_count == KVH

    holder_dev = holders // dec_count
    holder_slot = holders % dec_count
    heads_local = QH // col_count
    score_scale = HD ** (-0.5)
    prompt_pos = segment_positions(segment_ids[0])
    tables = rotary_tables(jnp.concatenate([cache_lengths, prompt_pos], axis=0))
    dec_tables = [table[:dec_count] for table in tables]

    def project(rows, weights):
        return jnp.dot(rows, weights, preferred_element_type=jnp.float32).astype(jnp.bfloat16)

    boxes = (
        (holder_dev[None, None, :] == jnp.arange(row_count)[:, None, None])
        & (holder_slot[None, None, :] == jnp.arange(dec_count)[None, :, None])
    ).astype(jnp.float32)
    length_box = jnp.sum(boxes * cache_lengths.astype(jnp.float32)[None, None, :], axis=2)
    route_weight = router_scores / jnp.sum(router_scores, axis=1, keepdims=True)
    slot_length = lax.all_to_all(length_box, "row", split_axis=0, concat_axis=0, tiled=True)
    slot_length = jnp.sum(slot_length, axis=0).astype(jnp.int32)

    projected = jnp.dot(attn_context, w_out, preferred_element_type=jnp.float32)
    summed = lax.psum_scatter(
        projected.astype(jnp.bfloat16), "col", scatter_dimension=1, tiled=True
    )
    if dense:
        first, second, _ = row_pairs()

        def to(value, pairs):
            return lax.ppermute(value, "row", pairs)

        both = jnp.concatenate([w_gate[0], w_up[0]], axis=1)
        both_near = to(both, first)
        summed, both_near = ordered(summed, both_near)
    hidden_mid = (residual.astype(jnp.float32) + summed.astype(jnp.float32)).astype(jnp.bfloat16)
    full_mid = lax.all_gather(hidden_mid, "col", axis=1, tiled=True)
    if dense:
        both_near, both_again = ordered(both_near, both)
        both_far, both_far_2 = to(both_again, second), to(both_near, second)
        normed = rms_norm(full_mid, gain_post)
        both_far, down_again = ordered(both_far, w_down[0])
        sources = row_sources()
        factors = [naming(routes, route_weight, expert_of(source, col_count)) for source in sources]
        boths = both_cores(both, both_near, both_far)
        inners = []
        for at in range(0, 6, 2):
            inners += inner_pair(normed, list(zip(boths[at : at + 2], factors[at : at + 2])))
        inners[3], both_far_2 = ordered(inners[3], both_far_2)
        inners += inner_pair(normed, list(zip(both_cores(both_far_2), factors[6:])))
        widths = [share_width * part // sum(PARTS) for part in PARTS]
        by_device = down_again.reshape(-1, col_count, share_width)
        begin = 0
        outs, fulls, dec_sums = [], [], []
        for width in widths:
            cut = by_device[:, :, begin : begin + width].reshape(-1, col_count * width)
            near, far = to(cut, first), to(cut, second)
            inners[5], near, far = ordered(inners[5], near, far)
            last = to(near, second)
            total = down_sum(inners[:6], both_cores(cut, near, far))
            total, inners[7], last = ordered(total, inners[7], last)
            last = both_cores(last)
            total, top = down_sum(inners[6:], last, total, dec_count)
            dec_sums.append(top.reshape(dec_count, col_count, width))
            moe_part = lax.psum_scatter(total, "col", scatter_dimension=1, tiled=True)
            mid_part = hidden_mid[:, begin : begin + width].astype(jnp.float32)
            outs.append((mid_part + moe_part.astype(jnp.float32)).astype(jnp.bfloat16))
            fulls.append(lax.all_gather(outs[-1], "col", axis=1, tiled=True))
            begin += width
        dec_sums = jnp.concatenate(dec_sums, axis=2).reshape(dec_count, model_width)
        dec_hidden = full_mid[:dec_count].astype(jnp.float32) + shared_sum(dec_sums, "col")
        dec_in = rms_norm(dec_hidden.astype(jnp.bfloat16), gain_input)
    else:
        normed = rms_norm(full_mid, gain_post)
        partial_moe = experts_sent(
            normed, routes, route_weight, w_gate, w_up, w_down, col_count
        )
        moe_share = lax.psum_scatter(partial_moe, "col", scatter_dimension=1, tiled=True)
        hidden_out = (hidden_mid.astype(jnp.float32) + moe_share).astype(jnp.bfloat16)
        full_out = lax.all_gather(hidden_out, "col", axis=1, tiled=True)
        x_in = rms_norm(full_out, gain_input)
        dec_in = x_in[:dec_count]
    dec_rot = rotate(project(dec_in, w_query).reshape(dec_count, heads_local, HD), dec_tables)
    dec_query = dec_rot.reshape(dec_count, heads_local * HD)
    outbox = jnp.sum(
        boxes[..., None] * dec_query.astype(jnp.float32)[None, None], axis=2
    ).astype(jnp.bfloat16)
    outbox = jnp.broadcast_to(outbox[:, None], (row_count, col_count) + outbox.shape[1:])
    inbox = lax.all_to_all(
        outbox.reshape((row_count * col_count,) + outbox.shape[2:]),
        ("row", "col"),
        split_axis=0,
        concat_axis=0,
        tiled=True,
    ).reshape(row_count, col_count, dec_count, heads_local * HD)
    slot_query = jnp.sum(inbox.astype(jnp.float32), axis=0).astype(jnp.bfloat16)
    slot_query = jnp.moveaxis(slot_query, 0, 1).reshape(dec_count, QH * HD)

    if dense:
        dec_keyval = project(dec_in, w_keyval)
        dec_keys = rotate(dec_keyval[:, None, :HD], dec_tables)[:, 0]
        dec_values = dec_keyval[:, HD:]
    else:
        query_rot = rotate(project(x_in, w_query).reshape(tok_rows, heads_local, HD), tables)
        keyval_local = project(x_in, w_keyval)
        keyval_all = lax.all_gather(keyval_local, "col", axis=1, tiled=True)
        keyval_heads = keyval_all.reshape(tok_rows, KVH, 2, HD)
        key_rot = rotate(keyval_heads[:, :, 0, :], tables)
        value_rows = keyval_heads[:, :, 1, :]
        cache_full = jnp.stack([key_rot, value_rows], axis=2).reshape(tok_rows, 2 * KVH * HD)
        cache_share = cache_full.shape[1] // col_count
        new_cache = lax.dynamic_slice_in_dim(cache_full, col_index * cache_share, cache_share, 1)
        head_kv = col_index * heads_local // (QH // KVH)
        my_keys = lax.dynamic_index_in_dim(key_rot, head_kv, 1, keepdims=False)
        my_values = lax.dynamic_index_in_dim(value_rows, head_kv, 1, keepdims=False)
        dec_keys, dec_values = my_keys[:dec_count], my_values[:dec_count]
        prompt_out = prompt_attention(
            query_rot[dec_count:], my_keys[dec_count:], my_values[dec_count:], segment_ids[0]
        )

    span_len = cache_keys.shape[1]
    span_start = col_index * span_len
    grouped = slot_query.reshape(dec_count, KVH, QH // KVH, HD)
    held_keys = cache_keys.reshape(dec_count, span_len, KVH, HD)
    held_values = cache_values.reshape(dec_count, span_len, KVH, HD).astype(jnp.float32)
    held_scores = (
        jnp.einsum("sgqd,stgd->sgqt", grouped, held_keys, preferred_element_type=jnp.float32)
        * score_scale
    )
    valid = ((span_start + jnp.arange(span_len))[None, :] < slot_length[:, None])[:, None, None, :]
    held_scores = jnp.where(valid, held_scores, NEGATIVE)
    score_top = jnp.max(held_scores, axis=-1)
    held_exp = jnp.where(valid, jnp.exp(held_scores - score_top[..., None]), 0.0)
    weight_mass = jnp.sum(held_exp, axis=-1)
    accum_out = jnp.einsum(
        "sgqt,stgd->sgqd", held_exp, held_values, precision=lax.Precision.HIGHEST
    )

    partial_terms = jnp.concatenate(
        [accum_out, score_top[..., None], weight_mass[..., None]], axis=-1
    ).reshape(dec_count, col_count, heads_local, HD + 2)
    spread_terms = lax.all_to_all(
        jnp.moveaxis(partial_terms, 1, 0), "col", split_axis=0, concat_axis=0, tiled=True
    )
    tops = spread_terms[..., HD]
    part_top = jnp.max(tops, axis=0)
    scale_by = jnp.exp(tops - part_top[None])
    part_mass = jnp.sum(spread_terms[..., HD + 1] * scale_by, axis=0)
    part_accum = jnp.sum(spread_terms[..., :HD] * scale_by[..., None], axis=0)
    reply = jnp.concatenate([part_accum, part_top[..., None], part_mass[..., None]], axis=-1)
    back = lax.all_to_all(
        jnp.broadcast_to(reply[None], (row_count,) + reply.shape),
        "row",
        split_axis=0,
        concat_axis=0,
        tiled=True,
    )
    remote = jnp.einsum("rsj,rshd->jhd", boxes, back, precision=lax.Precision.HIGHEST)
    remote_top = remote[..., HD]
    remote_mass = remote[..., HD + 1]
    remote_accum = remote[..., :HD]
    own_query = dec_rot.astype(jnp.float32)
    own_key = dec_keys.astype(jnp.float32)
    own_value = dec_values.astype(jnp.float32)
    own_score = jnp.sum(own_query * own_key[:, None, :], axis=-1) * score_scale
    final_top = jnp.maximum(remote_top, own_score)
    remote_factor = jnp.exp(remote_top - final_top)
    own_factor = jnp.exp(own_score - final_top)
    numerator = (
        remote_accum * remote_factor[..., None] + own_factor[..., None] * own_value[:, None, :]
    )
    denominator = remote_mass * remote_factor + own_factor
    decode_out = (
        (numerator / denominator[..., None])
        .reshape(dec_count, heads_local * HD)
        .astype(jnp.bfloat16)
    )
    if dense:
        segments = jnp.concatenate([jnp.full((dec_count,), -1, jnp.int32), segment_ids[0]])
        return tuple(
            tail(
                fulls,
                col_count,
                gain_input,
                w_query,
                w_keyval,
                tables[0],
                tables[1],
                segments,
                decode_out,
                col_index,
            )
        )
    attention_out = jnp.concatenate([decode_out, prompt_out], axis=0)
    return (hidden_out, new_cache, attention_out)


def solution(mesh):
    return jax.shard_map(
        shards,
        mesh=mesh,
        in_specs=(
            P("row", "col"),
            P("row", "col"),
            P("col", None),
            P(),
            P(),
            P("row", None),
            P("row", None),
            P(("row", "col"), None, None),
            P(("row", "col"), None, None),
            P(("row", "col"), None, None),
            P(None, "col"),
            P(None, "col"),
            P("row", None),
            P("row"),
            P("row"),
            P("row", "col", None),
            P("row", "col", None),
        ),
        out_specs=(P("row", "col"), P("row", "col"), P("row", "col")),
        check_vma=False,
    )
```

time: 440 us -> 355 us (0.81)
  Pallas kernels: 0 us -> 66.2 us
  matrix products: 78.2 us -> 15.5 us
  local copies, waits for them, and re-layouts: 75.3 us -> 20.5 us
  starting transfers between devices: 83.7 us -> 31.9 us
  waiting for transfers between devices: 133 us -> 176 us
  other arithmetic: 49 us -> 28.4 us
    pallas_call x0 -> x7, Pallas kernels: none -> 66.2 us  [the longest x4 26.9 us: inner_pair(): pl.pallas_call(inner_kernel, grid=(steps,), out_shape=[jax.ShapeDtypeStru...]
    dot_general x28 -> x3, matrix products: 70.1 us -> 4.82 us  [the longest x2 3.21 us: project(): jnp.dot(rows, weights, preferred_element_type=jnp.float32)]
    ppermute x45 -> x14, waiting for transfers between devices: 46.6 us -> 110 us  [the longest x6 106 us: to(): return lax.ppermute(value, 'row', pairs)]
    ppermute x45 -> x14, starting transfers between devices: 65.7 us -> 11.2 us  [the longest x6 9.95 us: to(): return lax.ppermute(value, 'row', pairs)]
    reduce_scatter x1, waiting for transfers between devices: 39.9 us -> 4.55 us  [shards(): lax.psum_scatter(projected.astype(jnp.bfloat16), 'col', scatter_dimension...]
    another operation x14 -> x0, local copies, waits for them, and re-layouts: 26.5 us -> none
    all_gather x1, waiting for transfers between devices: 26.7 us -> 9.37 us  [shards(): full_mid = lax.all_gather(hidden_mid, 'col', axis=1, tiled=True)]
    all_to_all x0 -> x1, waiting for transfers between devices: none -> 14.6 us  [shared_sum(): return jnp.sum(lax.all_to_all(spread, axis, 0, 0, tiled=True), axis=0)]
  transfers between devices with their start and end apart: 51 -> 23, of which waited for: 13 -> 13; matrix products, arithmetic and copies ran while one was open for 36% -> 14% of each run, Pallas kernels for 0% -> 11%
where the time goes in v2:
time: 355 us; the launch traced here: 353 us
  waiting for transfers between devices  176 us (50%)
  Pallas kernels  66.2 us (19%)
  starting transfers between devices  31.9 us (9%)
  other arithmetic  28.4 us (8%)
  local copies, waits for them, and re-layouts  20.5 us (6%)
  matrix products  15.5 us (4%)
  between operations  14.4 us (4%)
    ppermute x6, waiting for transfers between devices, to(): return lax.ppermute(value, 'row', pairs)  106 us
    pallas_call x4, Pallas kernels, inner_pair(): pl.pallas_call(inner_kernel, grid=(steps,), out_shape=[jax.ShapeDtypeStru...  26.9 us
    pallas_call x1, Pallas kernels, tail(): pl.pallas_call(lambda *refs: tail_kernel(count, len(fulls), decs, (tok_ro...  19.9 us
    pallas_call x2, Pallas kernels, down_sum(): pl.pallas_call(lambda *refs: down_kernel(sets, *refs), grid=(width // til...  19.3 us
    all_to_all x1, waiting for transfers between devices, shared_sum(): return jnp.sum(lax.all_to_all(spread, axis, 0, 0, tiled=True), axis=0)  14.6 us
    all_to_all x1, waiting for transfers between devices, shards(): lax.all_to_all(jnp.moveaxis(partial_terms, 1, 0), 'col', split_axis=0, co...  14.2 us
    unnamed x68, local copies, waits for them, and re-layouts  10.1 us
    ppermute x6, starting transfers between devices, to(): return lax.ppermute(value, 'row', pairs)  9.95 us
  transfers between devices with their start and end apart: 23, of which 13 were waited for; matrix products, arithmetic and copies ran while one was open for 14% of the time, Pallas kernels for 11%

profile of v2, /device:TPU:0, one launch (start us, length us, event | category | flops | bytes accessed | tf_op | source)
XLA Modules:
  0.0 353.3 jit_solution(4721327311861890550)
XLA Ops:
  7.2 6.3 %convolution_convert_fusion = bf16[512,2048]{1,0:T(8,128)(2,1)} fusion(bf16[512,1024]{1,0:T(8,128)(2,1)} %param.17, bf16[1024,2048]{1,0:T(8,128)(2,1)} %param.19), kind=kOutput, calls=%fused_computation.6 | convolution fusion | flops 2148532224 | bytes 7340032 | tf_op jit(solution)/shard_map/dot_general | solution.py:437
  20.4 35.4 %collective-permute-done.refs_0_.refs_1_ = bf16[2048,768]{1,0:T(8,128)(2,1)} collective-permute-done((bf16[2048,768]{1,0:T(8,128)(2,1)S(1)}, bf16[2048,768]{1,0:T(8,128)(2,1)}, u32[]{:S(2)}, u32[]{:S(2)}) %collective-permute-start) | collective-permute-done | bytes 3145760 | tf_op jit(solution)/shard_map/ppermute | solution.py:445
  55.8 4.5 %reduce-scatter.3.cloned.1.call-done = bf16[512,512]{1,0:T(8,128)(2,1)} async-done(((bf16[512,2048]{1,0:T(8,128)(2,1)}), bf16[512,512]{1,0:T(8,128)(2,1)}) %reduce-scatter.3.cloned.1.call-update) | async-done | bytes 524304 | tf_op jit(solution)/shard_map/reduce_scatter | solution.py:438
  64.7 33.1 %collective-permute-done.5.refs_0_.refs_1_ = bf16[2048,768]{1,0:T(8,128)(2,1)} collective-permute-done((bf16[2048,768]{1,0:T(8,128)(2,1)}, bf16[2048,768]{1,0:T(8,128)(2,1)}, u32[]{:S(2)}, u32[]{:S(2)}) %collective-permute-start.5) | collective-permute-done | bytes 3145760 | tf_op jit(solution)/shard_map/ppermute | solution.py:445
  98.9 9.4 %all-gather.3.cloned.1.call-done = bf16[512,2048]{1,0:T(8,128)(2,1)} async-done(((bf16[512,512]{1,0:T(8,128)(2,1)}), bf16[512,2048]{1,0:T(8,128)(2,1)}) %all-gather.3.cloned.1.call-update) | async-done | bytes 2097168 | tf_op jit(solution)/shard_map/all_gather | solution.py:451
  112.4 6.7 %shard_map.184 = (bf16[512,384]{1,0:T(8,128)(2,1)S(1)}, bf16[512,384]{1,0:T(8,128)(2,1)S(1)}) custom-call(bf16[512,2048]{1,0:T(8,128)(2,1)} %fusion.2.x_ref, bf16[2048,768]{1,0:T(8,128)(2,1)} %collective-permute-done.refs_0_.refs_1_, bf16[2048,768]{1,0:T(8,128)(2,1)} %collective-permute-done.refs_0_.refs_1_, f32[512,1]{1,0:T(8,128)S(1)} %copy.159.refs_2_, ...), custom_call_target="tpu_custom_call" | custom-call | flops 3221225472 | bytes 8388608 | tf_op jit(solution)/shard_map/pallas_call | solution.py:81
  119.2 12.4 %collective-permute-done.2.refs_0_.refs_1_ = bf16[2048,768]{1,0:T(8,128)(2,1)} collective-permute-done((bf16[2048,768]{1,0:T(8,128)(2,1)}, bf16[2048,768]{1,0:T(8,128)(2,1)}, u32[]{:S(2)}, u32[]{:S(2)}) %collective-permute-start.2) | collective-permute-done | bytes 3145760 | tf_op jit(solution)/shard_map/ppermute | solution.py:445
  134.9 6.7 %shard_map.187 = (bf16[512,384]{1,0:T(8,128)(2,1)S(1)}, bf16[512,384]{1,0:T(8,128)(2,1)S(1)}) custom-call(bf16[512,2048]{1,0:T(8,128)(2,1)} %fusion.2.x_ref, bf16[2048,768]{1,0:T(8,128)(2,1)} %collective-permute-done.5.refs_0_.refs_1_, bf16[2048,768]{1,0:T(8,128)(2,1)} %collective-permute-done.5.refs_0_.refs_1_, f32[512,1]{1,0:T(8,128)S(1)} %copy.165.refs_2_, ...), custom_call_target="tpu_custom_call" | custom-call | flops 3221225472 | bytes 8388608 | tf_op jit(solution)/shard_map/pallas_call | solution.py:81
  143.2 25.3 %collective-permute-done.7.refs_8_ = bf16[384,2048]{1,0:T(8,128)(2,1)} collective-permute-done((bf16[384,2048]{1,0:T(8,128)(2,1)}, bf16[384,2048]{1,0:T(8,128)(2,1)}, u32[]{:S(2)}, u32[]{:S(2)}) %collective-permute-start.7) | collective-permute-done | bytes 1572896 | tf_op jit(solution)/shard_map/ppermute | solution.py:445
  171.6 6.7 %shard_map.186 = (bf16[512,384]{1,0:T(8,128)(2,1)S(1)}, bf16[512,384]{1,0:T(8,128)(2,1)S(1)}) custom-call(bf16[512,2048]{1,0:T(8,128)(2,1)} %fusion.2.x_ref, bf16[2048,768]{1,0:T(8,128)(2,1)} %copy-done.9, bf16[2048,768]{1,0:T(8,128)(2,1)} %copy-done.9, f32[512,1]{1,0:T(8,128)S(1)} %copy.163.refs_2_, ...), custom_call_target="tpu_custom_call" | custom-call | flops 3221225472 | bytes 8388608 | tf_op jit(solution)/shard_map/pallas_call | solution.py:81
  178.4 6.8 %shard_map.185 = (bf16[512,384]{1,0:T(8,128)(2,1)S(1)}, bf16[512,384]{1,0:T(8,128)(2,1)S(1)}) custom-call(bf16[512,2048]{1,0:T(8,128)(2,1)} %fusion.2.x_ref, bf16[2048,768]{1,0:T(8,128)(2,1)} %collective-permute-done.2.refs_0_.refs_1_, bf16[2048,768]{1,0:T(8,128)(2,1)} %collective-permute-done.2.refs_0_.refs_1_, f32[512,1]{1,0:T(8,128)S(1)} %copy.161.refs_2_, ...), custom_call_target="tpu_custom_call" | custom-call | flops 3221225472 | bytes 8388608 | tf_op jit(solution)/shard_map/pallas_call | solution.py:81
  185.2 11.1 %shard_map.188.refs_4_ = f32[512,2048]{1,0:T(8,128)} custom-call(bf16[512,384]{1,0:T(8,128)(2,1)S(1)} %get-tuple-element.33.refs_0_, bf16[512,384]{1,0:T(8,128)(2,1)S(1)} %get-tuple-element.34.refs_1_, bf16[512,384]{1,0:T(8,128)(2,1)S(1)} %get-tuple-element.35.refs_2_, bf16[512,384]{1,0:T(8,128)(2,1)S(1)} %copy-done.5, bf16[512,384]{1,0:T(8,128)(2,1)S(1)} %copy-done.7, ...), custom_call_target="tpu_custom_call" | custom-call | flops 4831838208 | bytes 15990784 | tf_op jit(solution)/shard_map/pallas_call | solution.py:129
  201.2 8.2 %shard_map.189 = (bf16[512,2048]{1,0:T(8,128)(2,1)}, f32[8,2048]{1,0:T(8,128)S(1)}) custom-call(bf16[512,384]{1,0:T(8,128)(2,1)S(1)} %get-tuple-element.32.refs_0_, bf16[512,384]{1,0:T(8,128)(2,1)S(1)} %get-tuple-element.46.refs_1_, bf16[384,2048]{1,0:T(8,128)(2,1)} %collective-permute-done.12.refs_2_, bf16[384,2048]{1,0:T(8,128)(2,1)} %copy-done.12, ...), custom_call_target="tpu_custom_call" | custom-call | flops 1610612736 | bytes 8126464 | tf_op jit(solution)/shard_map/pallas_call | solution.py:129
  211.0 4.0 %all-to-all-start.1 = ((f32[4,8,2048]{2,1,0:T(8,128)}), f32[4,8,2048]{2,1,0:T(8,128)}, u32[]{:S(2)}, u32[]{:S(2)}) async-start(f32[4,8,2048]{2,1,0:T(8,128)} %broadcast_in_dim.138), calls=%async_computation.3 | async-start | bytes 524288 | tf_op jit(solution)/shard_map/all_to_all | solution.py:59
  217.6 14.6 %all-to-all-done.1 = f32[4,8,2048]{2,1,0:T(8,128)} async-done(((f32[4,8,2048]{2,1,0:T(8,128)}), f32[4,8,2048]{2,1,0:T(8,128)}, u32[]{:S(2)}, u32[]{:S(2)}) %all-to-all-start.1) | async-done | bytes 262176 | tf_op jit(solution)/shard_map/all_to_all | solution.py:59
  232.2 4.0 %all-to-all-start = ((f32[8,1,8]{2,1,0:T(1,128)}), f32[8,1,8]{2,1,0:T(1,128)}, u32[]{:S(2)}, u32[]{:S(2)}) async-start(f32[8,1,8]{2,1,0:T(1,128)} %bitcast.17), calls=%async_computation.2 | async-start | bytes 8192 | tf_op jit(solution)/shard_map/all_to_all | solution.py:434
  245.2 4.3 %all-to-all-start.2 = ((bf16[32,8,1024]{2,1,0:T(8,128)(2,1)}), bf16[32,8,1024]{2,1,0:T(8,128)(2,1)}, u32[]{:S(2)}, u32[]{:S(2)}) async-start(bf16[32,8,1024]{2,1,0:T(8,128)(2,1)} %bitcast.117), calls=%async_computation.4 | async-start | bytes 1048576 | tf_op jit(solution)/shard_map/all_to_all | solution.py:503
  250.2 6.5 %reduce-scatter.5.cloned.1.call-done = bf16[512,512]{1,0:T(8,128)(2,1)} async-done(((bf16[512,2048]{1,0:T(8,128)(2,1)}), bf16[512,512]{1,0:T(8,128)(2,1)}) %reduce-scatter.5.cloned.1.call-update) | async-done | bytes 524304 | tf_op jit(solution)/shard_map/reduce_scatter | solution.py:479
  258.9 8.5 %all-to-all-done.2 = bf16[32,8,1024]{2,1,0:T(8,128)(2,1)} async-done(((bf16[32,8,1024]{2,1,0:T(8,128)(2,1)}), bf16[32,8,1024]{2,1,0:T(8,128)(2,1)}, u32[]{:S(2)}, u32[]{:S(2)}) %all-to-all-start.2) | async-done | bytes 524320 | tf_op jit(solution)/shard_map/all_to_all | solution.py:503
  276.4 4.0 %all-to-all-start.3 = ((f32[4,8,8,130]{3,2,1,0:T(8,128)}), f32[4,8,8,130]{3,2,1,0:T(8,128)}, u32[]{:S(2)}, u32[]{:S(2)}) async-start(f32[4,8,8,130]{3,2,1,0:T(8,128)} %copy.176), calls=%async_computation.5 | async-start | bytes 524288 | tf_op jit(solution)/shard_map/all_to_all | solution.py:556
  283.5 14.2 %all-to-all-done.3 = f32[4,8,8,130]{3,2,1,0:T(8,128)} async-done(((f32[4,8,8,130]{3,2,1,0:T(8,128)}), f32[4,8,8,130]{3,2,1,0:T(8,128)}, u32[]{:S(2)}, u32[]{:S(2)}) %all-to-all-start.3) | async-done | bytes 133152 | tf_op jit(solution)/shard_map/all_to_all | solution.py:556
  307.4 4.1 %all-to-all-start.4 = ((f32[8,8,8,130]{3,1,2,0:T(8,128)}), f32[8,8,8,130]{3,1,2,0:T(8,128)}, u32[]{:S(2)}, u32[]{:S(2)}) async-start(f32[8,8,8,130]{3,1,2,0:T(8,128)} %broadcast_in_dim.146), calls=%async_computation.6 | async-start | bytes 1048576 | tf_op jit(solution)/shard_map/all_to_all | solution.py:565
  312.4 8.9 %all-to-all-done.4 = f32[8,8,8,130]{3,1,2,0:T(8,128)} async-done(((f32[8,8,8,130]{3,1,2,0:T(8,128)}), f32[8,8,8,130]{3,1,2,0:T(8,128)}, u32[]{:S(2)}, u32[]{:S(2)}) %all-to-all-start.4) | async-done | bytes 266272 | tf_op jit(solution)/shard_map/all_to_all | solution.py:565
  326.8 19.9 %shard_map.190 = (bf16[512,512]{1,0:T(8,128)(2,1)}, bf16[512,256]{1,0:T(8,128)(2,1)}, bf16[512,1024]{1,0:T(8,128)(2,1)}) custom-call(s32[1]{0:T(128)} %bitcast.refs_0_, bf16[512,2048]{1,0:T(8,128)(2,1)} %all-gather.5.cloned.1.call-done.refs_1_, bf16[1,2048]{1,0:T(2,128)(2,1)S(1)} %broadcast_in_dim.134.refs_2_, bf16[2048,1024]{1,0:T(8,128)(2,1)} %refs_3_.1, ...), custom_call_target="tpu_custom_call" | custom-call | flops 2684354560 | bytes 9437184 | tf_op jit(solution)/shard_map/pallas_call | solution.py:234
  (181 shorter events, 72.9 us)
Async XLA Ops:
  7.2 262.0 %copy-start = (bf16[8,256,512]{2,1,0:T(8,128)(2,1)S(1)}, bf16[8,256,512]{2,1,0:T(8,128)(2,1)}, u32[]{:S(2)}) copy-start(bf16[8,256,512]{2,1,0:T(8,128)(2,1)} %param.32) | copy-start | bytes 6291460
  7.2 53.1 %reduce-scatter.3.cloned.1.call-start = ((), (), s32[]{:S(2)}) async-start(), calls=%async_computation.7 | async-start | bytes 2621440 | tf_op jit(solution)/shard_map/reduce_scatter | solution.py:438
  13.6 94.7 %all-gather.3.cloned.1.call-start = ((), (), s32[]{:S(2)}) async-start(), calls=%async_computation.8 | async-start | bytes 2621440 | tf_op jit(solution)/shard_map/all_gather | solution.py:451
  17.5 38.3 %collective-permute-start = (bf16[2048,768]{1,0:T(8,128)(2,1)S(1)}, bf16[2048,768]{1,0:T(8,128)(2,1)}, u32[]{:S(2)}, u32[]{:S(2)}) collective-permute-start(bf16[2048,768]{1,0:T(8,128)(2,1)S(1)} %pad_maximum_fusion.refs_0_.refs_1_), channel_id=1, source_target_pairs={{0,8},{4,20},{8,0},{12,28},{16,24},{20,4},{24,16},{28,12},{1,9},{5... | collective-permute-start | bytes 9437192 | tf_op jit(solution)/shard_map/ppermute | solution.py:445
  60.3 37.6 %collective-permute-start.5 = (bf16[2048,768]{1,0:T(8,128)(2,1)}, bf16[2048,768]{1,0:T(8,128)(2,1)}, u32[]{:S(2)}, u32[]{:S(2)}) collective-permute-start(bf16[2048,768]{1,0:T(8,128)(2,1)} %copy-done.9), channel_id=1, source_target_pairs={{0,16},{4,12},{8,24},{12,4},{16,0},{20,28},{24,8},{28,20},{1,17},{... | collective-permute-start | bytes 9437192 | tf_op jit(solution)/shard_map/ppermute | solution.py:445
  63.8 193.0 %reduce-scatter.5.cloned.1.call-start = ((), (), s32[]{:S(2)}) async-start(), calls=%async_computation.9 | async-start | bytes 2621440 | tf_op jit(solution)/shard_map/reduce_scatter | solution.py:479
  63.8 48.6 %collective-permute-start.1 = (bf16[2048,768]{1,0:T(8,128)(2,1)}, bf16[2048,768]{1,0:T(8,128)(2,1)}, u32[]{:S(2)}, u32[]{:S(2)}) collective-permute-start(bf16[2048,768]{1,0:T(8,128)(2,1)} %collective-permute-done.refs_0_.refs_1_), channel_id=1, source_target_pairs={{0,4},{4,0},{8,12},{12,8},{16,20},{20,16},{24,28},{28,24},{1,5},{5... | collective-permute-start | bytes 9437192 | tf_op jit(solution)/shard_map/ppermute | solution.py:297
  63.9 67.7 %collective-permute-start.2 = (bf16[2048,768]{1,0:T(8,128)(2,1)}, bf16[2048,768]{1,0:T(8,128)(2,1)}, u32[]{:S(2)}, u32[]{:S(2)}) collective-permute-start(bf16[2048,768]{1,0:T(8,128)(2,1)} %collective-permute-done.refs_0_.refs_1_), channel_id=1, source_target_pairs={{0,16},{4,12},{8,24},{12,4},{16,0},{20,28},{24,8},{28,20},{1,17},{... | collective-permute-start | bytes 9437192 | tf_op jit(solution)/shard_map/ppermute | solution.py:445
  97.9 37.0 %collective-permute-start.6 = (bf16[2048,768]{1,0:T(8,128)(2,1)}, bf16[2048,768]{1,0:T(8,128)(2,1)}, u32[]{:S(2)}, u32[]{:S(2)}) collective-permute-start(bf16[2048,768]{1,0:T(8,128)(2,1)} %collective-permute-done.5.refs_0_.refs_1_), channel_id=1, source_target_pairs={{0,4},{4,0},{8,12},{12,8},{16,20},{20,16},{24,28},{28,24},{1,5},{5... | collective-permute-start | bytes 9437192 | tf_op jit(solution)/shard_map/ppermute | solution.py:297
  97.9 71.3 %collective-permute-start.4 = (bf16[2048,768]{1,0:T(8,128)(2,1)}, bf16[2048,768]{1,0:T(8,128)(2,1)}, u32[]{:S(2)}, u32[]{:S(2)}) collective-permute-start(bf16[2048,768]{1,0:T(8,128)(2,1)} %copy-done.9), channel_id=1, source_target_pairs={{0,4},{4,0},{8,12},{12,8},{16,20},{20,16},{24,28},{28,24},{1,5},{5... | collective-permute-start | bytes 9437192 | tf_op jit(solution)/shard_map/ppermute | solution.py:297
  131.6 46.8 %collective-permute-start.3 = (bf16[2048,768]{1,0:T(8,128)(2,1)}, bf16[2048,768]{1,0:T(8,128)(2,1)}, u32[]{:S(2)}, u32[]{:S(2)}) collective-permute-start(bf16[2048,768]{1,0:T(8,128)(2,1)} %collective-permute-done.2.refs_0_.refs_1_), channel_id=1, source_target_pairs={{0,4},{4,0},{8,12},{12,8},{16,20},{20,16},{24,28},{28,24},{1,5},{5... | collective-permute-start | bytes 9437192 | tf_op jit(solution)/shard_map/ppermute | solution.py:297
  131.6 36.9 %collective-permute-start.7 = (bf16[384,2048]{1,0:T(8,128)(2,1)}, bf16[384,2048]{1,0:T(8,128)(2,1)}, u32[]{:S(2)}, u32[]{:S(2)}) collective-permute-start(bf16[384,2048]{1,0:T(8,128)(2,1)} %bitcast.9.refs_6_), channel_id=1, source_target_pairs={{0,8},{4,20},{8,0},{12,28},{16,24},{20,4},{24,16},{28,12},{1,9},{5... | collective-permute-start | bytes 4718600 | tf_op jit(solution)/shard_map/ppermute | solution.py:445
  133.1 35.7 %collective-permute-start.8 = (bf16[384,2048]{1,0:T(8,128)(2,1)}, bf16[384,2048]{1,0:T(8,128)(2,1)}, u32[]{:S(2)}, u32[]{:S(2)}) collective-permute-start(bf16[384,2048]{1,0:T(8,128)(2,1)} %bitcast.9.refs_6_), channel_id=1, source_target_pairs={{0,16},{4,12},{8,24},{12,4},{16,0},{20,28},{24,8},{28,20},{1,17},{... | collective-permute-start | bytes 4718600 | tf_op jit(solution)/shard_map/ppermute | solution.py:445
  134.9 50.3 %collective-permute-start.9 = (bf16[384,2048]{1,0:T(8,128)(2,1)}, bf16[384,2048]{1,0:T(8,128)(2,1)}, u32[]{:S(2)}, u32[]{:S(2)}) collective-permute-start(bf16[384,2048]{1,0:T(8,128)(2,1)} %bitcast.9.refs_6_), channel_id=1, source_target_pairs={{0,4},{4,0},{8,12},{12,8},{16,20},{20,16},{24,28},{28,24},{1,5},{5... | collective-permute-start | bytes 4718600 | tf_op jit(solution)/shard_map/ppermute | solution.py:297
  168.7 16.4 %collective-permute-start.10 = (bf16[384,2048]{1,0:T(8,128)(2,1)}, bf16[384,2048]{1,0:T(8,128)(2,1)}, u32[]{:S(2)}, u32[]{:S(2)}) collective-permute-start(bf16[384,2048]{1,0:T(8,128)(2,1)} %collective-permute-done.7.refs_8_), channel_id=1, source_target_pairs={{0,4},{4,0},{8,12},{12,8},{16,20},{20,16},{24,28},{28,24},{1,5},{5... | collective-permute-start | bytes 4718600 | tf_op jit(solution)/shard_map/ppermute | solution.py:297
  169.0 16.2 %collective-permute-start.11 = (bf16[384,2048]{1,0:T(8,128)(2,1)}, bf16[384,2048]{1,0:T(8,128)(2,1)}, u32[]{:S(2)}, u32[]{:S(2)}) collective-permute-start(bf16[384,2048]{1,0:T(8,128)(2,1)} %collective-permute-done.8.refs_10_), channel_id=1, source_target_pairs={{0,4},{4,0},{8,12},{12,8},{16,20},{20,16},{24,28},{28,24},{1,5},{5... | collective-permute-start | bytes 4718600 | tf_op jit(solution)/shard_map/ppermute | solution.py:297
  169.2 27.1 %collective-permute-start.12 = (bf16[384,2048]{1,0:T(8,128)(2,1)}, bf16[384,2048]{1,0:T(8,128)(2,1)}, u32[]{:S(2)}, u32[]{:S(2)}) collective-permute-start(bf16[384,2048]{1,0:T(8,128)(2,1)} %collective-permute-done.7.refs_8_), channel_id=1, source_target_pairs={{0,16},{4,12},{8,24},{12,4},{16,0},{20,28},{24,8},{28,20},{1,17},{... | collective-permute-start | bytes 4718600 | tf_op jit(solution)/shard_map/ppermute | solution.py:445
  196.4 3.7 %collective-permute-start.13 = (bf16[384,2048]{1,0:T(8,128)(2,1)}, bf16[384,2048]{1,0:T(8,128)(2,1)S(1)}, u32[]{:S(2)}, u32[]{:S(2)}) collective-permute-start(bf16[384,2048]{1,0:T(8,128)(2,1)} %collective-permute-done.12.refs_2_), channel_id=1, source_target_pairs={{0,4},{4,0},{8,12},{12,8},{16,20},{20,16},{24,28},{28,24},{1,5},{5... | collective-permute-start | bytes 4718600 | tf_op jit(solution)/shard_map/ppermute | solution.py:297
  211.0 21.2 %all-to-all-start.1 = ((f32[4,8,2048]{2,1,0:T(8,128)}), f32[4,8,2048]{2,1,0:T(8,128)}, u32[]{:S(2)}, u32[]{:S(2)}) async-start(f32[4,8,2048]{2,1,0:T(8,128)} %broadcast_in_dim.138), calls=%async_computation.3 | async-start | bytes 524288 | tf_op jit(solution)/shard_map/all_to_all | solution.py:59
  232.2 12.1 %all-to-all-start = ((f32[8,1,8]{2,1,0:T(1,128)}), f32[8,1,8]{2,1,0:T(1,128)}, u32[]{:S(2)}, u32[]{:S(2)}) async-start(f32[8,1,8]{2,1,0:T(1,128)} %bitcast.17), calls=%async_computation.2 | async-start | bytes 8192 | tf_op jit(solution)/shard_map/all_to_all | solution.py:434
  245.2 22.2 %all-to-all-start.2 = ((bf16[32,8,1024]{2,1,0:T(8,128)(2,1)}), bf16[32,8,1024]{2,1,0:T(8,128)(2,1)}, u32[]{:S(2)}, u32[]{:S(2)}) async-start(bf16[32,8,1024]{2,1,0:T(8,128)(2,1)} %bitcast.117), calls=%async_computation.4 | async-start | bytes 1048576 | tf_op jit(solution)/shard_map/all_to_all | solution.py:503
  249.4 75.4 %all-gather.5.cloned.1.call-start = ((), (), s32[]{:S(2)}) async-start(), calls=%async_computation.10 | async-start | bytes 2621440 | tf_op jit(solution)/shard_map/all_gather | solution.py:482
  276.4 21.4 %all-to-all-start.3 = ((f32[4,8,8,130]{3,2,1,0:T(8,128)}), f32[4,8,8,130]{3,2,1,0:T(8,128)}, u32[]{:S(2)}, u32[]{:S(2)}) async-start(f32[4,8,8,130]{3,2,1,0:T(8,128)} %copy.176), calls=%async_computation.5 | async-start | bytes 524288 | tf_op jit(solution)/shard_map/all_to_all | solution.py:556
  307.4 13.9 %all-to-all-start.4 = ((f32[8,8,8,130]{3,1,2,0:T(8,128)}), f32[8,8,8,130]{3,1,2,0:T(8,128)}, u32[]{:S(2)}, u32[]{:S(2)}) async-start(f32[8,8,8,130]{3,1,2,0:T(8,128)} %broadcast_in_dim.146), calls=%async_computation.6 | async-start | bytes 1048576 | tf_op jit(solution)/shard_map/all_to_all | solution.py:565
  (31 other events, 544.8 us)
Sparse Core Ops, SparseCore 0:
  13.7 46.5 reduce-scatter.2
  63.9 44.3 all-gather.2
  209.6 47.0 reduce-scatter.4
  259.0 57.2 all-gather.4

commit v3 on v2

--- a/solution.py
+++ b/solution.py
@@ -14,7 +14,6 @@
 EPSILON = 1e-06
 ROPE_THETA = 1000000.0
 NEGATIVE = -1e30
-PARTS = (1,)
 VMEM_BYTES = 52 * 1024 * 1024
 
 
@@ -56,7 +55,7 @@
 def shared_sum(block, axis):
     count = lax.axis_size(axis)
     spread = jnp.broadcast_to(block[None], (count,) + block.shape)
-    return jnp.sum(lax.all_to_all(spread, axis, 0, 0, tiled=True), axis=0)
+    return jnp.sum(lax.all_to_all(spread, axis, 0, 0, tiled=True).astype(jnp.float32), axis=0)
 
 
 def inner_kernel(x_ref, *refs):
@@ -72,26 +71,28 @@
 
 def inner_pair(normed, sets):
     tok_rows, model_width = normed.shape
-    half = sets[0][0].shape[1] // 2
     tile = 128
+    half = sets[0][0].shape[1]
+    half = half // 2 if sets[0][0] is sets[0][1] else half
     steps = half // tile
     gate = pl.BlockSpec((model_width, tile), lambda step: (0, step))
-    up = pl.BlockSpec((model_width, tile), lambda step: (0, step + steps))
+    second = pl.BlockSpec((model_width, tile), lambda step: (0, step + steps))
     factor = pl.BlockSpec((tok_rows, 1), lambda step: (0, 0))
+    specs = [
+        spec for one, two, _ in sets for spec in (gate, second if one is two else gate, factor)
+    ]
     return pl.pallas_call(
         inner_kernel,
         grid=(steps,),
         out_shape=[jax.ShapeDtypeStruct((tok_rows, half), jnp.bfloat16)] * 2,
         in_specs=[pl.BlockSpec((tok_rows, model_width), lambda step: (0, 0))]
-        + [gate, up, factor] * 2,
+        + specs,
         out_specs=[pl.BlockSpec((tok_rows, tile), lambda step: (0, step))] * 2,
         compiler_params=pltpu.CompilerParams(vmem_limit_bytes=VMEM_BYTES),
         cost_estimate=pl.CostEstimate(
-            flops=8 * tok_rows * model_width * half,
-            bytes_accessed=2 * model_width * (tok_rows + 4 * half),
-            transcendentals=2 * tok_rows * half,
+            flops=tok_rows, bytes_accessed=tok_rows, transcendentals=0
         ),
-    )(normed, *[value for both, factor in sets for value in (both, both, factor)])
+    )(normed, *[value for one in sets for value in one])
 
 
 def down_kernel(sets, *refs):
@@ -105,8 +106,9 @@
     if len(refs) == 2 * sets + 1:
         refs[-1][...] = acc
     else:
-        before, total_ref, top_ref = refs[2 * sets :]
-        acc = acc + before[...]
+        total_ref, top_ref = refs[-2:]
+        if len(refs) == 2 * sets + 3:
+            acc = acc + refs[2 * sets][...]
         total_ref[...] = acc.astype(jnp.bfloat16)
         top_ref[...] = acc[0 : top_ref.shape[0], :]
 
@@ -125,14 +127,14 @@
         jax.ShapeDtypeStruct((tok_rows, width), jnp.bfloat16),
         jax.ShapeDtypeStruct((tops, width), jnp.float32),
     ]
-    last = before is not None
+    last, more = tops > 0, before is not None
     return pl.pallas_call(
         lambda *refs: down_kernel(sets, *refs),
         grid=(width // tile,),
         out_shape=rounded if last else whole,
         in_specs=[pl.BlockSpec((tok_rows, half), lambda step: (0, 0))] * sets
         + [moving(half)] * sets
-        + [moving(tok_rows)] * last,
+        + [moving(tok_rows)] * more,
         out_specs=[moving(tok_rows), moving(tops)] if last else moving(tok_rows),
         compiler_params=pltpu.CompilerParams(vmem_limit_bytes=VMEM_BYTES),
         cost_estimate=pl.CostEstimate(
@@ -140,15 +142,12 @@
             bytes_accessed=2 * sets * half * (width + tok_rows) + 4 * tok_rows * width,
             transcendentals=0,
         ),
-    )(*inners, *downs, *([before] if last else []))
-
-
-def tail_kernel(count, parts, decs, window, col_ref, *refs):
-    fulls = refs[:parts]
-    (gain, wq, wkv, cosine, sine, seg_col, seg_row, dec, hidden_ref, cache_ref, out_ref) = refs[
-        parts : parts + 11
-    ]
-    hidden, x_in, keys, values, bias = refs[parts + 11 :]
+    )(*inners, *downs, *([before] if more else []))
+
+
+def tail_kernel(count, window, col_ref, *refs):
+    (full, gain, wq, wkv, cosine, sine, seg_col, seg_row, hidden_ref, cache_ref, out_ref) = refs[:11]
+    x_in, keys, values, bias = refs[11:]
     tok_rows = x_in.shape[0]
     rows = tok_rows // count
 
@@ -160,19 +159,13 @@
     @pl.when(pl.program_id(0) == 0)
     def _():
         col = col_ref[0]
-        begin = 0
-        for device in range(count):
-            for full in fulls:
-                width = full.shape[1] // count
-                hidden[:, begin : begin + width] = full[:, device * width : (device + 1) * width]
-                begin += width
         for start in range(0, tok_rows, rows):
             place = slice(start, start + rows)
-            floats = hidden[place, :].astype(jnp.float32)
+            floats = full[place, :].astype(jnp.float32)
             inverse = lax.rsqrt(jnp.mean(floats * floats, axis=-1, keepdims=True) + EPSILON)
             x_in[place, :] = (floats * inverse * gain[...].astype(jnp.float32)).astype(jnp.bfloat16)
         share = hidden_ref.shape[1]
-        hidden_ref[...] = hidden[:, pl.ds(pl.multiple_of(col * share, share), share)]
+        hidden_ref[...] = full[:, pl.ds(pl.multiple_of(col * share, share), share)]
         keyval = jnp.dot(x_in[...], wkv[...], preferred_element_type=jnp.float32)
         keyval = keyval.astype(jnp.bfloat16)
         keys[...] = turn(keyval[:, :HD])
@@ -185,44 +178,37 @@
         bias[...] = jnp.where(allowed, 0.0, NEGATIVE)
 
     queries = jnp.dot(x_in[...], wq[...], preferred_element_type=jnp.float32).astype(jnp.bfloat16)
+    heads = wq.shape[1] // HD
+    turned = [turn(queries[:, head * HD : (head + 1) * HD]) for head in range(heads)]
     step = 128
-    for head in range(wq.shape[1] // HD):
-        lanes = slice(head * HD, (head + 1) * HD)
-        query = turn(queries[:, lanes])
-        for start in range(0, tok_rows, step):
-            first = max(0, (start - window + 1) // step * step)
-            stop = start + step
-            scores = (
-                lax.dot_general(
-                    query[start:stop],
-                    keys[first:stop, :],
-                    (((1,), (1,)), ((), ())),
-                    preferred_element_type=jnp.float32,
-                )
-                * HD ** (-0.5)
-                + bias[start:stop, first:stop]
-            )
-            highest = jnp.max(scores, axis=-1, keepdims=True)
-            exponent = jnp.exp(scores - highest)
-            mass = jnp.sum(exponent, axis=-1, keepdims=True)
-            weights = (exponent * (1.0 / mass)).astype(jnp.bfloat16)
-            mixed = jnp.dot(weights, values[first:stop, :], preferred_element_type=jnp.float32)
-            mixed = mixed.astype(jnp.bfloat16)
-            if start == 0:
-                top = lax.broadcasted_iota(jnp.int32, (16, HD), 0)
-                out_ref[0:16, lanes] = jnp.where(top < decs, dec[:, lanes], mixed[0:16])
-                out_ref[16:stop, lanes] = mixed[16:]
-            else:
-                out_ref[start:stop, lanes] = mixed
-
-
-def tail(fulls, count, gain, w_query, w_keyval, cosine, sine, segments, decode_out, col_index):
-    decs = decode_out.shape[0]
+    for start in range(0, tok_rows, step):
+        first = max(0, (start - window + 1) // step * step)
+        stop = start + step
+        query = jnp.concatenate([head[start:stop] for head in turned], axis=0)
+        scores = lax.dot_general(
+            query,
+            keys[first:stop, :],
+            (((1,), (1,)), ((), ())),
+            preferred_element_type=jnp.float32,
+        ) * HD ** (-0.5)
+        scores = scores.reshape(heads, step, stop - first) + bias[start:stop, first:stop][None]
+        scores = scores.reshape(heads * step, stop - first)
+        highest = jnp.max(scores, axis=-1, keepdims=True)
+        exponent = jnp.exp(scores - highest)
+        mass = jnp.sum(exponent, axis=-1, keepdims=True)
+        mixed = jnp.dot(
+            exponent.astype(jnp.bfloat16), values[first:stop, :], preferred_element_type=jnp.float32
+        )
+        mixed = (mixed * (1.0 / mass)).astype(jnp.bfloat16)
+        for head in range(heads):
+            out_ref[start:stop, head * HD : (head + 1) * HD] = mixed[head * step : (head + 1) * step]
+
+
+def tail(full, count, gain, w_query, w_keyval, cosine, sine, segments, window, col_index):
     tok_rows = segments.shape[0]
     model_width = w_query.shape[0]
     query_width = w_query.shape[1]
-    pair = 2 * HD
-    dec_rows = jnp.pad(decode_out, ((0, 16 - decs), (0, 0)))
+    pair, some = 2 * HD, min(4 * HD, query_width)
 
     def fixed(shape):
         return pl.BlockSpec(shape, lambda step: (0, 0))
@@ -232,28 +218,26 @@
 
     share = model_width // count
     return pl.pallas_call(
-        lambda *refs: tail_kernel(count, len(fulls), decs, (tok_rows - decs) // 2, *refs),
-        grid=(query_width // pair,),
+        lambda *refs: tail_kernel(count, window, *refs),
+        grid=(query_width // some,),
         out_shape=[
             jax.ShapeDtypeStruct((tok_rows, share), jnp.bfloat16),
             jax.ShapeDtypeStruct((tok_rows, pair), jnp.bfloat16),
             jax.ShapeDtypeStruct((tok_rows, query_width), jnp.bfloat16),
         ],
         in_specs=[pl.BlockSpec(memory_space=pltpu.SMEM)]
-        + [fixed(full.shape) for full in fulls]
+        + [fixed(full.shape)]
         + [
             fixed((1, model_width)),
-            moving((model_width, pair)),
+            moving((model_width, some)),
             fixed((model_width, pair)),
             fixed((tok_rows, HD)),
             fixed((tok_rows, HD)),
             fixed((tok_rows, 1)),
             fixed((1, tok_rows)),
-            moving((16, pair)),
         ],
-        out_specs=[fixed((tok_rows, share)), fixed((tok_rows, pair)), moving((tok_rows, pair))],
+        out_specs=[fixed((tok_rows, share)), fixed((tok_rows, pair)), moving((tok_rows, some))],
         scratch_shapes=[
-            pltpu.VMEM((tok_rows, model_width), jnp.bfloat16),
             pltpu.VMEM((tok_rows, model_width), jnp.bfloat16),
             pltpu.VMEM((tok_rows, HD), jnp.bfloat16),
             pltpu.VMEM((tok_rows, HD), jnp.bfloat16),
@@ -267,7 +251,7 @@
         ),
     )(
         col_index[None],
-        *fulls,
+        full,
         gain[None],
         w_query,
         w_keyval,
@@ -275,7 +259,6 @@
         sine,
         segments[:, None],
         segments[None],
-        dec_rows,
     )
 
 
@@ -290,12 +273,12 @@
     return first, second, core
 
 
+def other_core(value):
+    return lax.ppermute(value, "row", row_pairs()[2])
+
+
 def both_cores(*values):
-    core = row_pairs()[2]
-    out = []
-    for value in values:
-        out.extend([value, lax.ppermute(value, "row", core)])
-    return out
+    return [copy for value in values for copy in (value, other_core(value))]
 
 
 def row_sources():
@@ -429,11 +412,10 @@
         (holder_dev[None, None, :] == jnp.arange(row_count)[:, None, None])
         & (holder_slot[None, None, :] == jnp.arange(dec_count)[None, :, None])
     ).astype(jnp.float32)
-    length_box = jnp.sum(boxes * cache_lengths.astype(jnp.float32)[None, None, :], axis=2)
     route_weight = router_scores / jnp.sum(router_scores, axis=1, keepdims=True)
-    slot_length = lax.all_to_all(length_box, "row", split_axis=0, concat_axis=0, tiled=True)
-    slot_length = jnp.sum(slot_length, axis=0).astype(jnp.int32)
-
+
+    if dense:
+        gate, up = w_gate[0], w_up[0]
     projected = jnp.dot(attn_context, w_out, preferred_element_type=jnp.float32)
     summed = lax.psum_scatter(
         projected.astype(jnp.bfloat16), "col", scatter_dimension=1, tiled=True
@@ -444,45 +426,47 @@
         def to(value, pairs):
             return lax.ppermute(value, "row", pairs)
 
-        both = jnp.concatenate([w_gate[0], w_up[0]], axis=1)
-        both_near = to(both, first)
-        summed, both_near = ordered(summed, both_near)
+        gate_near, up_near, gate_far = to(gate, first), to(up, first), to(gate, second)
+        gate_core, up_core = other_core(gate), other_core(up)
+        summed, gate_near, up_near, gate_far, gate_core, up_core = ordered(
+            summed, gate_near, up_near, gate_far, gate_core, up_core
+        )
     hidden_mid = (residual.astype(jnp.float32) + summed.astype(jnp.float32)).astype(jnp.bfloat16)
     full_mid = lax.all_gather(hidden_mid, "col", axis=1, tiled=True)
     if dense:
-        both_near, both_again = ordered(both_near, both)
-        both_far, both_far_2 = to(both_again, second), to(both_near, second)
+        up_near, up_again = ordered(up_near, up)
+        up_far, gate_far_2, up_far_2 = to(up_again, second), to(gate_near, second), to(up_near, second)
+        cores = [other_core(value) for value in (gate_near, up_near, gate_far)]
+        full_mid, up_far, gate_far_2, up_far_2, down, *cores = ordered(
+            full_mid, up_far, gate_far_2, up_far_2, w_down[0], *cores
+        )
         normed = rms_norm(full_mid, gain_post)
-        both_far, down_again = ordered(both_far, w_down[0])
-        sources = row_sources()
-        factors = [naming(routes, route_weight, expert_of(source, col_count)) for source in sources]
-        boths = both_cores(both, both_near, both_far)
-        inners = []
-        for at in range(0, 6, 2):
-            inners += inner_pair(normed, list(zip(boths[at : at + 2], factors[at : at + 2])))
-        inners[3], both_far_2 = ordered(inners[3], both_far_2)
-        inners += inner_pair(normed, list(zip(both_cores(both_far_2), factors[6:])))
-        widths = [share_width * part // sum(PARTS) for part in PARTS]
-        by_device = down_again.reshape(-1, col_count, share_width)
-        begin = 0
-        outs, fulls, dec_sums = [], [], []
-        for width in widths:
-            cut = by_device[:, :, begin : begin + width].reshape(-1, col_count * width)
-            near, far = to(cut, first), to(cut, second)
-            inners[5], near, far = ordered(inners[5], near, far)
-            last = to(near, second)
-            total = down_sum(inners[:6], both_cores(cut, near, far))
-            total, inners[7], last = ordered(total, inners[7], last)
-            last = both_cores(last)
-            total, top = down_sum(inners[6:], last, total, dec_count)
-            dec_sums.append(top.reshape(dec_count, col_count, width))
-            moe_part = lax.psum_scatter(total, "col", scatter_dimension=1, tiled=True)
-            mid_part = hidden_mid[:, begin : begin + width].astype(jnp.float32)
-            outs.append((mid_part + moe_part.astype(jnp.float32)).astype(jnp.bfloat16))
-            fulls.append(lax.all_gather(outs[-1], "col", axis=1, tiled=True))
-            begin += width
-        dec_sums = jnp.concatenate(dec_sums, axis=2).reshape(dec_count, model_width)
-        dec_hidden = full_mid[:dec_count].astype(jnp.float32) + shared_sum(dec_sums, "col")
+        near, far = to(down, first), to(down, second)
+        factors = [
+            naming(routes, route_weight, expert_of(source, col_count)) for source in row_sources()
+        ]
+
+        def pair_of(gates, ups, at):
+            return inner_pair(normed, list(zip(gates, ups, factors[at : at + 2])))
+
+        inners = [
+            *pair_of([gate, gate_core], [up, up_core], 0),
+            *pair_of([gate_near, cores[0]], [up_near, cores[1]], 2),
+            *pair_of([gate_far, cores[2]], [up_far, other_core(up_far)], 4),
+        ]
+        far_2_cores = [other_core(gate_far_2), other_core(up_far_2)]
+        normed, inners[5], *far_2_cores = ordered(normed, inners[5], *far_2_cores)
+        inners += pair_of([gate_far_2, far_2_cores[0]], [up_far_2, far_2_cores[1]], 6)
+        inners[7], near, far = ordered(inners[7], near, far)
+        last = to(near, second)
+        partial = down_sum(inners[:6], both_cores(down, near, far))
+        partial, last = ordered(partial, last)
+        total, top = down_sum(inners[6:], both_cores(last), partial, dec_count)
+        moe_share = lax.psum_scatter(total, "col", scatter_dimension=1, tiled=True)
+        hidden_out = hidden_mid.astype(jnp.float32) + moe_share.astype(jnp.float32)
+        hidden_out = hidden_out.astype(jnp.bfloat16)
+        full_out = lax.all_gather(hidden_out, "col", axis=1, tiled=True)
+        dec_hidden = full_mid[:dec_count].astype(jnp.float32) + shared_sum(top.astype(jnp.bfloat16), "col")
         dec_in = rms_norm(dec_hidden.astype(jnp.bfloat16), gain_input)
     else:
         normed = rms_norm(full_mid, gain_post)
@@ -495,19 +479,29 @@
         x_in = rms_norm(full_out, gain_input)
         dec_in = x_in[:dec_count]
     dec_rot = rotate(project(dec_in, w_query).reshape(dec_count, heads_local, HD), dec_tables)
-    dec_query = dec_rot.reshape(dec_count, heads_local * HD)
+    lengths = jnp.stack([cache_lengths // 256, cache_lengths % 256], axis=1).astype(jnp.bfloat16)
+    dec_query = jnp.concatenate(
+        [
+            dec_rot.reshape(dec_count, heads_local * HD),
+            jnp.pad(lengths, ((0, 0), (0, HD - lengths.shape[1]))),
+        ],
+        axis=1,
+    )
     outbox = jnp.sum(
         boxes[..., None] * dec_query.astype(jnp.float32)[None, None], axis=2
     ).astype(jnp.bfloat16)
-    outbox = jnp.broadcast_to(outbox[:, None], (row_count, col_count) + outbox.shape[1:])
-    inbox = lax.all_to_all(
-        outbox.reshape((row_count * col_count,) + outbox.shape[2:]),
-        ("row", "col"),
+    inbox = lax.all_to_all(outbox, "row", split_axis=0, concat_axis=0, tiled=True)
+    slot_terms = jnp.sum(inbox.astype(jnp.float32), axis=0).astype(jnp.bfloat16)
+    slot_terms = lax.all_to_all(
+        jnp.broadcast_to(slot_terms[None], (col_count,) + slot_terms.shape),
+        "col",
         split_axis=0,
         concat_axis=0,
         tiled=True,
-    ).reshape(row_count, col_count, dec_count, heads_local * HD)
-    slot_query = jnp.sum(inbox.astype(jnp.float32), axis=0).astype(jnp.bfloat16)
+    )
+    slot_length = slot_terms[0, :, heads_local * HD :][:, :2].astype(jnp.int32)
+    slot_length = slot_length[:, 0] * 256 + slot_length[:, 1]
+    slot_query = slot_terms[..., : heads_local * HD]
     slot_query = jnp.moveaxis(slot_query, 0, 1).reshape(dec_count, QH * HD)
 
     if dense:
@@ -550,18 +544,35 @@
         "sgqt,stgd->sgqd", held_exp, held_values, precision=lax.Precision.HIGHEST
     )
 
-    partial_terms = jnp.concatenate(
-        [accum_out, score_top[..., None], weight_mass[..., None]], axis=-1
-    ).reshape(dec_count, col_count, heads_local, HD + 2)
+    def packed(accum, top, mass):
+        notes = jnp.concatenate([top, mass], axis=-1)
+        notes = jnp.pad(notes, ((0, 0),) * (notes.ndim - 1) + ((0, HD - notes.shape[-1]),))
+        rows = accum.reshape(accum.shape[:-3] + (dec_count * heads_local, HD))
+        return jnp.concatenate([rows, notes], axis=-2)
+
+    def unpacked(rows):
+        accum = rows[..., : dec_count * heads_local, :]
+        accum = accum.reshape(rows.shape[:-2] + (dec_count, heads_local, HD))
+        notes = rows[..., dec_count * heads_local :, :]
+        return accum, notes[..., :heads_local], notes[..., heads_local : 2 * heads_local]
+
+    def by_col(value):
+        value = value.reshape((dec_count, col_count, heads_local) + value.shape[3:])
+        return jnp.moveaxis(value, 1, 0)
+
     spread_terms = lax.all_to_all(
-        jnp.moveaxis(partial_terms, 1, 0), "col", split_axis=0, concat_axis=0, tiled=True
-    )
-    tops = spread_terms[..., HD]
+        packed(by_col(accum_out), by_col(score_top), by_col(weight_mass)),
+        "col",
+        split_axis=0,
+        concat_axis=0,
+        tiled=True,
+    )
+    accums, tops, masses = unpacked(spread_terms)
     part_top = jnp.max(tops, axis=0)
     scale_by = jnp.exp(tops - part_top[None])
-    part_mass = jnp.sum(spread_terms[..., HD + 1] * scale_by, axis=0)
-    part_accum = jnp.sum(spread_terms[..., :HD] * scale_by[..., None], axis=0)
-    reply = jnp.concatenate([part_accum, part_top[..., None], part_mass[..., None]], axis=-1)
+    part_mass = jnp.sum(masses * scale_by, axis=0)
+    part_accum = jnp.sum(accums * scale_by[..., None], axis=0)
+    reply = packed(part_accum, part_top, part_mass)
     back = lax.all_to_all(
         jnp.broadcast_to(reply[None], (row_count,) + reply.shape),
         "row",
@@ -569,10 +580,13 @@
         concat_axis=0,
         tiled=True,
     )
-    remote = jnp.einsum("rsj,rshd->jhd", boxes, back, precision=lax.Precision.HIGHEST)
-    remote_top = remote[..., HD]
-    remote_mass = remote[..., HD + 1]
-    remote_accum = remote[..., :HD]
+    accums, tops, masses = unpacked(back)
+
+    def picked(value):
+        mine = boxes.reshape(boxes.shape + (1,) * (value.ndim - 2))
+        return jnp.sum(mine * value[:, :, None], axis=(0, 1))
+
+    remote_top, remote_mass, remote_accum = picked(tops), picked(masses), picked(accums)
     own_query = dec_rot.astype(jnp.float32)
     own_key = dec_keys.astype(jnp.float32)
     own_value = dec_values.astype(jnp.float32)
@@ -591,20 +605,21 @@
     )
     if dense:
         segments = jnp.concatenate([jnp.full((dec_count,), -1, jnp.int32), segment_ids[0]])
-        return tuple(
-            tail(
-                fulls,
-                col_count,
-                gain_input,
-                w_query,
-                w_keyval,
-                tables[0],
-                tables[1],
-                segments,
-                decode_out,
-                col_index,
-            )
+        window = segment_ids.shape[1] // 2
+        hidden_out, new_cache, attention_out = tail(
+            full_out,
+            col_count,
+            gain_input,
+            w_query,
+            w_keyval,
+            tables[0],
+            tables[1],
+            segments,
+            window,
+            col_index,
         )
+        attention_out = lax.dynamic_update_slice_in_dim(attention_out, decode_out, 0, 0)
+        return (hidden_out, new_cache, attention_out)
     attention_out = jnp.concatenate([decode_out, prompt_out], axis=0)
     return (hidden_out, new_cache, attention_out)
 

time: 355 us -> 320 us (0.901)
  waiting for transfers between devices: 176 us -> 156 us
  blocking collectives: 0 us -> 12.2 us
  Pallas kernels: 66.2 us -> 56.2 us
  other arithmetic: 28.4 us -> 21.5 us
  local copies, waits for them, and re-layouts: 20.5 us -> 14.6 us
  matrix products: 15.5 us -> 11.3 us
    all_gather x1, waiting for transfers between devices: 0.02 us -> 15.9 us  [shards(): full_out = lax.all_gather(hidden_out, 'col', axis=1, tiled=True)]
    all_to_all x4 -> x3, waiting for transfers between devices: 37.3 us -> 23.8 us  [the longest x1 9.96 us: shared_sum(): lax.all_to_all(spread, axis, 0, 0, tiled=True).astype(jnp.float32)]
    all_to_all x0 -> x1, blocking collectives: none -> 12.2 us  [shards(): lax.all_to_all(packed(by_col(accum_out), by_col(score_top), by_col(weight...]
    pallas_call x1, Pallas kernels: 19.9 us -> 9.57 us  [tail(): pl.pallas_call(lambda *refs: tail_kernel(count, window, *refs), grid=(que...]
    all_gather x1, waiting for transfers between devices: 9.37 us -> 0.02 us  [shards(): full_mid = lax.all_gather(hidden_mid, 'col', axis=1, tiled=True)]
    all_to_all x1, waiting for transfers between devices: 8.89 us -> 1.39 us  [shards(): lax.all_to_all(jnp.broadcast_to(reply[None], (row_count,) + reply.shape),...]
    ppermute x6 -> x9, waiting for transfers between devices: 106 us -> 112 us  [to(): return lax.ppermute(value, 'row', pairs)]
    reduce_scatter x1, waiting for transfers between devices: 6.52 us -> 1.25 us  [shards(): moe_share = lax.psum_scatter(total, 'col', scatter_dimension=1, tiled=True)]
  transfers between devices with their start and end apart: 23 -> 29, of which waited for: 13 -> 13; matrix products, arithmetic and copies ran while one was open for 14% -> 10% of each run, Pallas kernels for 11% -> 12%
where the time goes in v3:
time: 320 us; the launch traced here: 319 us
  waiting for transfers between devices  156 us (49%)
  Pallas kernels  56.2 us (18%)
  starting transfers between devices  32.4 us (10%)
  other arithmetic  21.5 us (7%)
  local copies, waits for them, and re-layouts  14.6 us (5%)
  between operations  14.3 us (4%)
  blocking collectives  12.2 us (4%)
  matrix products  11.3 us (4%)
    ppermute x9, waiting for transfers between devices, to(): return lax.ppermute(value, 'row', pairs)  112 us
    pallas_call x4, Pallas kernels, inner_pair(): pl.pallas_call(inner_kernel, grid=(steps,), out_shape=[jax.ShapeDtypeStru...  27.3 us
    pallas_call x2, Pallas kernels, down_sum(): pl.pallas_call(lambda *refs: down_kernel(sets, *refs), grid=(width // til...  19.4 us
    all_gather x1, waiting for transfers between devices, shards(): full_out = lax.all_gather(hidden_out, 'col', axis=1, tiled=True)  15.9 us
    ppermute x9, starting transfers between devices, to(): return lax.ppermute(value, 'row', pairs)  13.2 us
    all_to_all x1, blocking collectives, shards(): lax.all_to_all(packed(by_col(accum_out), by_col(score_top), by_col(weight...  12.2 us
    all_to_all x1, waiting for transfers between devices, shared_sum(): lax.all_to_all(spread, axis, 0, 0, tiled=True).astype(jnp.float32)  9.96 us
    pallas_call x1, Pallas kernels, tail(): pl.pallas_call(lambda *refs: tail_kernel(count, window, *refs), grid=(que...  9.57 us
  transfers between devices with their start and end apart: 29, of which 13 were waited for; matrix products, arithmetic and copies ran while one was open for 10% of the time, Pallas kernels for 12%

profile of v3, /device:TPU:0, one launch (start us, length us, event | category | flops | bytes accessed | tf_op | source)
XLA Modules:
  0.0 318.7 jit_solution(9015172751103182585)
XLA Ops:
  7.2 6.3 %convolution_convert_fusion = bf16[512,2048]{1,0:T(8,128)(2,1)} fusion(bf16[512,1024]{1,0:T(8,128)(2,1)} %param.17, bf16[1024,2048]{1,0:T(8,128)(2,1)} %param.19), kind=kOutput, calls=%fused_computation.5 | convolution fusion | flops 2148532224 | bytes 7340032 | tf_op jit(solution)/shard_map/dot_general | solution.py:419
  13.6 3.0 collective-permute-start
  19.2 32.3 %collective-permute-done.refs_0_ = bf16[2048,384]{1,0:T(8,128)(2,1)} collective-permute-done((bf16[2048,384]{1,0:T(8,128)(2,1)}, bf16[2048,384]{1,0:T(8,128)(2,1)}, u32[]{:S(2)}, u32[]{:S(2)}) %collective-permute-start) | collective-permute-done | bytes 1572896 | tf_op jit(solution)/shard_map/ppermute | solution.py:427
  51.5 17.5 %collective-permute-done.1.refs_1_ = bf16[2048,384]{1,0:T(8,128)(2,1)} collective-permute-done((bf16[2048,384]{1,0:T(8,128)(2,1)}, bf16[2048,384]{1,0:T(8,128)(2,1)}, u32[]{:S(2)}, u32[]{:S(2)}) %collective-permute-start.1) | collective-permute-done | bytes 1572896 | tf_op jit(solution)/shard_map/ppermute | solution.py:427
  75.6 14.4 %collective-permute-done.7.refs_1_ = bf16[2048,384]{1,0:T(8,128)(2,1)} collective-permute-done((bf16[2048,384]{1,0:T(8,128)(2,1)}, bf16[2048,384]{1,0:T(8,128)(2,1)}, u32[]{:S(2)}, u32[]{:S(2)}) %collective-permute-start.7) | collective-permute-done | bytes 1572896 | tf_op jit(solution)/shard_map/ppermute | solution.py:427
  89.9 33.7 %collective-permute-done.5.refs_1_ = bf16[2048,384]{1,0:T(8,128)(2,1)} collective-permute-done((bf16[2048,384]{1,0:T(8,128)(2,1)}, bf16[2048,384]{1,0:T(8,128)(2,1)}, u32[]{:S(2)}, u32[]{:S(2)}) %collective-permute-start.5) | collective-permute-done | bytes 1572896 | tf_op jit(solution)/shard_map/ppermute | solution.py:427
  132.7 6.7 %shard_map.184 = (bf16[512,384]{1,0:T(8,128)(2,1)S(1)}, bf16[512,384]{1,0:T(8,128)(2,1)S(1)}) custom-call(bf16[512,2048]{1,0:T(8,128)(2,1)} %fusion.2.x_ref, bf16[2048,384]{1,0:T(8,128)(2,1)} %collective-permute-done.2.refs_0_, bf16[2048,384]{1,0:T(8,128)(2,1)} %collective-permute-done.5.refs_1_, f32[512,1]{1,0:T(8,128)S(1)} %copy.87.refs_2_, ...), custom_call_target="tpu_custom_call" | custom-call | flops 512 | bytes 512 | tf_op jit(solution)/shard_map/pallas_call | solution.py:84
  139.5 7.0 %shard_map.185 = (bf16[512,384]{1,0:T(8,128)(2,1)S(1)}, bf16[512,384]{1,0:T(8,128)(2,1)S(1)}) custom-call(bf16[512,2048]{1,0:T(8,128)(2,1)} %fusion.2.x_ref, bf16[2048,384]{1,0:T(8,128)(2,1)} %collective-permute-done.6.refs_0_, bf16[2048,384]{1,0:T(8,128)(2,1)} %collective-permute-done.7.refs_1_, f32[512,1]{1,0:T(8,128)S(1)} %copy.89.refs_2_, ...), custom_call_target="tpu_custom_call" | custom-call | flops 512 | bytes 512 | tf_op jit(solution)/shard_map/pallas_call | solution.py:84
  147.2 13.6 %collective-permute-done.14.refs_8_ = bf16[384,2048]{1,0:T(8,128)(2,1)} collective-permute-done((bf16[384,2048]{1,0:T(8,128)(2,1)}, bf16[384,2048]{1,0:T(8,128)(2,1)}, u32[]{:S(2)}, u32[]{:S(2)}) %collective-permute-start.14) | collective-permute-done | bytes 1572896 | tf_op jit(solution)/shard_map/ppermute | solution.py:427
  164.6 6.7 %shard_map.187 = (bf16[512,384]{1,0:T(8,128)(2,1)S(1)}, bf16[512,384]{1,0:T(8,128)(2,1)S(1)}) custom-call(bf16[512,2048]{1,0:T(8,128)(2,1)} %fusion.2.x_ref, bf16[2048,384]{1,0:T(8,128)(2,1)} %collective-permute-done.refs_0_, bf16[2048,384]{1,0:T(8,128)(2,1)} %collective-permute-done.1.refs_1_, f32[512,1]{1,0:T(8,128)S(1)} %copy.93.refs_2_, ...), custom_call_target="tpu_custom_call" | custom-call | flops 512 | bytes 512 | tf_op jit(solution)/shard_map/pallas_call | solution.py:84
  171.3 6.9 %shard_map.186 = (bf16[512,384]{1,0:T(8,128)(2,1)S(1)}, bf16[512,384]{1,0:T(8,128)(2,1)S(1)}) custom-call(bf16[512,2048]{1,0:T(8,128)(2,1)} %fusion.2.x_ref, bf16[2048,384]{1,0:T(8,128)(2,1)} %bitcast.92, bf16[2048,384]{1,0:T(8,128)(2,1)} %bitcast.96, f32[512,1]{1,0:T(8,128)S(1)} %copy.91.refs_2_, bf16[2048,384]{1,0:T(8,128)(2,1)} %collective-permute-done.3.refs_3_, ...), custom_call_target="tpu_custom_call" | custom-call | flops 512 | bytes 512 | tf_op jit(solution)/shard_map/pallas_call | solution.py:84
  178.3 11.2 %shard_map.188.refs_4_ = f32[512,2048]{1,0:T(8,128)} custom-call(bf16[512,384]{1,0:T(8,128)(2,1)S(1)} %get-tuple-element.62.refs_0_, bf16[512,384]{1,0:T(8,128)(2,1)S(1)} %get-tuple-element.63.refs_1_, bf16[512,384]{1,0:T(8,128)(2,1)S(1)} %get-tuple-element.66.refs_2_, bf16[512,384]{1,0:T(8,128)(2,1)S(1)} %get-tuple-element.67.refs_3_, ...), custom_call_target="tpu_custom_call" | custom-call | flops 4831838208 | bytes 15990784 | tf_op jit(solution)/shard_map/pallas_call | solution.py:131
  194.4 8.2 %shard_map.189 = (bf16[512,2048]{1,0:T(8,128)(2,1)}, f32[8,2048]{1,0:T(8,128)S(1)}) custom-call(bf16[512,384]{1,0:T(8,128)(2,1)S(1)} %get-tuple-element.56.refs_0_, bf16[512,384]{1,0:T(8,128)(2,1)S(1)} %copy-done.3, bf16[384,2048]{1,0:T(8,128)(2,1)} %collective-permute-done.19.refs_2_, bf16[384,2048]{1,0:T(8,128)(2,1)} %copy-done.14, ...), custom_call_target="tpu_custom_call" | custom-call | flops 1610612736 | bytes 8126464 | tf_op jit(solution)/shard_map/pallas_call | solution.py:131
  204.8 5.1 %all-to-all-start = ((bf16[4,8,2048]{2,1,0:T(8,128)(2,1)}), bf16[4,8,2048]{2,1,0:T(8,128)(2,1)S(1)}, u32[]{:S(2)}, u32[]{:S(2)}) async-start(bf16[4,8,2048]{2,1,0:T(8,128)(2,1)} %broadcast_in_dim.127), calls=%async_computation.2 | async-start | bytes 262144 | tf_op jit(solution)/shard_map/all_to_all | solution.py:58
  210.5 10.0 %all-to-all-done = bf16[4,8,2048]{2,1,0:T(8,128)(2,1)S(1)} async-done(((bf16[4,8,2048]{2,1,0:T(8,128)(2,1)}), bf16[4,8,2048]{2,1,0:T(8,128)(2,1)S(1)}, u32[]{:S(2)}, u32[]{:S(2)}) %all-to-all-start) | async-done | bytes 131104 | tf_op jit(solution)/shard_map/all_to_all | solution.py:58
  223.8 2.9 fusion.18
  228.3 3.4 %all-to-all-start.1 = ((bf16[8,8,1152]{2,1,0:T(8,128)(2,1)}), bf16[8,8,1152]{2,1,0:T(8,128)(2,1)S(1)}, u32[]{:S(2)}, u32[]{:S(2)}) async-start(bf16[8,8,1152]{2,1,0:T(8,128)(2,1)} %multiply_reduce_fusion), calls=%async_computation.3 | async-start | bytes 294912 | tf_op jit(solution)/shard_map/all_to_all | solution.py:493
  231.6 5.6 %all-to-all-done.1 = bf16[8,8,1152]{2,1,0:T(8,128)(2,1)S(1)} async-done(((bf16[8,8,1152]{2,1,0:T(8,128)(2,1)}), bf16[8,8,1152]{2,1,0:T(8,128)(2,1)S(1)}, u32[]{:S(2)}, u32[]{:S(2)}) %all-to-all-start.1) | async-done | bytes 147488 | tf_op jit(solution)/shard_map/all_to_all | solution.py:493
  237.9 3.3 %all-to-all-start.2 = ((bf16[4,8,1152]{2,1,0:T(8,128)(2,1)}), bf16[4,8,1152]{2,1,0:T(8,128)(2,1)S(1)}, u32[]{:S(2)}, u32[]{:S(2)}) async-start(bf16[4,8,1152]{2,1,0:T(8,128)(2,1)} %broadcast_in_dim.128), calls=%async_computation.4 | async-start | bytes 147456 | tf_op jit(solution)/shard_map/all_to_all | solution.py:495
  241.3 8.2 %all-to-all-done.2 = bf16[4,8,1152]{2,1,0:T(8,128)(2,1)S(1)} async-done(((bf16[4,8,1152]{2,1,0:T(8,128)(2,1)}), bf16[4,8,1152]{2,1,0:T(8,128)(2,1)S(1)}, u32[]{:S(2)}, u32[]{:S(2)}) %all-to-all-start.2) | async-done | bytes 73760 | tf_op jit(solution)/shard_map/all_to_all | solution.py:495
  256.1 12.2 %all_to_all.25 = f32[4,72,128]{2,1,0:T(8,128)S(1)} all-to-all(f32[4,72,128]{2,1,0:T(8,128)S(1)} %select_maximum_fusion), channel_id=1, replica_groups=mesh['row'=8,'col'=4] {'col'}, dimensions={0} | all-to-all | bytes 294912 | tf_op jit(solution)/shard_map/all_to_all | solution.py:563
  269.4 4.1 %all-to-all-start.4 = ((f32[8,72,128]{2,1,0:T(8,128)}), f32[8,72,128]{2,1,0:T(8,128)}, u32[]{:S(2)}, u32[]{:S(2)}) async-start(f32[8,72,128]{2,1,0:T(8,128)} %broadcast_in_dim.132), calls=%async_computation.6 | async-start | bytes 589824 | tf_op jit(solution)/shard_map/all_to_all | solution.py:576
  284.2 15.9 %all-gather.5.cloned.1.call-done.refs_1_ = bf16[512,2048]{1,0:T(8,128)(2,1)} async-done(((bf16[512,512]{1,0:T(8,128)(2,1)}), bf16[512,2048]{1,0:T(8,128)(2,1)}) %all-gather.5.cloned.1.call-update) | async-done | bytes 2097168 | tf_op jit(solution)/shard_map/all_gather | solution.py:468
  302.0 9.6 %shard_map.190 = (bf16[512,512]{1,0:T(8,128)(2,1)}, bf16[512,256]{1,0:T(8,128)(2,1)}, bf16[512,1024]{1,0:T(8,128)(2,1)}) custom-call(s32[1]{0:T(128)} %bitcast.refs_0_, bf16[512,2048]{1,0:T(8,128)(2,1)} %all-gather.5.cloned.1.call-done.refs_1_, bf16[1,2048]{1,0:T(2,128)(2,1)S(1)} %broadcast_in_dim.124.refs_2_, bf16[2048,1024]{1,0:T(8,128)(2,1)} %refs_3_.1, ...), custom_call_target="tpu_custom_call" | custom-call | flops 2684354560 | bytes 9437184 | tf_op jit(solution)/shard_map/pallas_call | solution.py:220
  (178 shorter events, 56.8 us)
Async XLA Ops:
  7.2 61.9 %reduce-scatter.3.cloned.1.call-start = ((), (), s32[]{:S(2)}) async-start(), calls=%async_computation.7 | async-start | bytes 2621440 | tf_op jit(solution)/shard_map/reduce_scatter | solution.py:420
  13.6 110.1 %all-gather.3.cloned.1.call-start = ((), (), s32[]{:S(2)}) async-start(), calls=%async_computation.8 | async-start | bytes 2621440 | tf_op jit(solution)/shard_map/all_gather | solution.py:435
  13.6 37.9 %collective-permute-start = (bf16[2048,384]{1,0:T(8,128)(2,1)}, bf16[2048,384]{1,0:T(8,128)(2,1)}, u32[]{:S(2)}, u32[]{:S(2)}) collective-permute-start(bf16[2048,384]{1,0:T(8,128)(2,1)} %bitcast.89), channel_id=1, source_target_pairs={{0,8},{4,20},{8,0},{12,28},{16,24},{20,4},{24,16},{28,12},{1,9},{5... | collective-permute-start | bytes 4718600 | tf_op jit(solution)/shard_map/ppermute | solution.py:427
  16.6 52.4 %collective-permute-start.1 = (bf16[2048,384]{1,0:T(8,128)(2,1)}, bf16[2048,384]{1,0:T(8,128)(2,1)}, u32[]{:S(2)}, u32[]{:S(2)}) collective-permute-start(bf16[2048,384]{1,0:T(8,128)(2,1)} %bitcast.93), channel_id=1, source_target_pairs={{0,8},{4,20},{8,0},{12,28},{16,24},{20,4},{24,16},{28,12},{1,9},{5... | collective-permute-start | bytes 4718600 | tf_op jit(solution)/shard_map/ppermute | solution.py:427
  16.8 52.3 %collective-permute-start.2 = (bf16[2048,384]{1,0:T(8,128)(2,1)}, bf16[2048,384]{1,0:T(8,128)(2,1)}, u32[]{:S(2)}, u32[]{:S(2)}) collective-permute-start(bf16[2048,384]{1,0:T(8,128)(2,1)} %bitcast.90), channel_id=1, source_target_pairs={{0,16},{4,12},{8,24},{12,4},{16,0},{20,28},{24,8},{28,20},{1,17},{... | collective-permute-start | bytes 4718600 | tf_op jit(solution)/shard_map/ppermute | solution.py:427
  18.7 50.4 %collective-permute-start.3 = (bf16[2048,384]{1,0:T(8,128)(2,1)}, bf16[2048,384]{1,0:T(8,128)(2,1)}, u32[]{:S(2)}, u32[]{:S(2)}) collective-permute-start(bf16[2048,384]{1,0:T(8,128)(2,1)} %bitcast.91), channel_id=1, source_target_pairs={{0,4},{4,0},{8,12},{12,8},{16,20},{20,16},{24,28},{28,24},{1,5},{5... | collective-permute-start | bytes 4718600 | tf_op jit(solution)/shard_map/ppermute | solution.py:277
  18.7 50.4 %collective-permute-start.4 = (bf16[2048,384]{1,0:T(8,128)(2,1)}, bf16[2048,384]{1,0:T(8,128)(2,1)}, u32[]{:S(2)}, u32[]{:S(2)}) collective-permute-start(bf16[2048,384]{1,0:T(8,128)(2,1)} %bitcast.94), channel_id=1, source_target_pairs={{0,4},{4,0},{8,12},{12,8},{16,20},{20,16},{24,28},{28,24},{1,5},{5... | collective-permute-start | bytes 4718600 | tf_op jit(solution)/shard_map/ppermute | solution.py:277
  69.1 20.8 %collective-permute-start.7 = (bf16[2048,384]{1,0:T(8,128)(2,1)}, bf16[2048,384]{1,0:T(8,128)(2,1)}, u32[]{:S(2)}, u32[]{:S(2)}) collective-permute-start(bf16[2048,384]{1,0:T(8,128)(2,1)} %collective-permute-done.1.refs_1_), channel_id=1, source_target_pairs={{0,16},{4,12},{8,24},{12,4},{16,0},{20,28},{24,8},{28,20},{1,17},{... | collective-permute-start | bytes 4718600 | tf_op jit(solution)/shard_map/ppermute | solution.py:427
  73.2 177.8 %reduce-scatter.5.cloned.1.call-start = ((), (), s32[]{:S(2)}) async-start(), calls=%async_computation.9 | async-start | bytes 2621440 | tf_op jit(solution)/shard_map/reduce_scatter | solution.py:465
  73.3 16.7 %collective-permute-start.9 = (bf16[2048,384]{1,0:T(8,128)(2,1)}, bf16[2048,384]{1,0:T(8,128)(2,1)}, u32[]{:S(2)}, u32[]{:S(2)}) collective-permute-start(bf16[2048,384]{1,0:T(8,128)(2,1)} %collective-permute-done.1.refs_1_), channel_id=1, source_target_pairs={{0,4},{4,0},{8,12},{12,8},{16,20},{20,16},{24,28},{28,24},{1,5},{5... | collective-permute-start | bytes 4718600 | tf_op jit(solution)/shard_map/ppermute | solution.py:277
  73.3 50.3 %collective-permute-start.6 = (bf16[2048,384]{1,0:T(8,128)(2,1)}, bf16[2048,384]{1,0:T(8,128)(2,1)}, u32[]{:S(2)}, u32[]{:S(2)}) collective-permute-start(bf16[2048,384]{1,0:T(8,128)(2,1)} %collective-permute-done.refs_0_), channel_id=1, source_target_pairs={{0,16},{4,12},{8,24},{12,4},{16,0},{20,28},{24,8},{28,20},{1,17},{... | collective-permute-start | bytes 4718600 | tf_op jit(solution)/shard_map/ppermute | solution.py:427
  73.5 50.1 %collective-permute-start.8 = (bf16[2048,384]{1,0:T(8,128)(2,1)}, bf16[2048,384]{1,0:T(8,128)(2,1)}, u32[]{:S(2)}, u32[]{:S(2)}) collective-permute-start(bf16[2048,384]{1,0:T(8,128)(2,1)} %collective-permute-done.refs_0_), channel_id=1, source_target_pairs={{0,4},{4,0},{8,12},{12,8},{16,20},{20,16},{24,28},{28,24},{1,5},{5... | collective-permute-start | bytes 4718600 | tf_op jit(solution)/shard_map/ppermute | solution.py:277
  75.0 48.6 %collective-permute-start.5 = (bf16[2048,384]{1,0:T(8,128)(2,1)}, bf16[2048,384]{1,0:T(8,128)(2,1)}, u32[]{:S(2)}, u32[]{:S(2)}) collective-permute-start(bf16[2048,384]{1,0:T(8,128)(2,1)} %bitcast.95), channel_id=1, source_target_pairs={{0,16},{4,12},{8,24},{12,4},{16,0},{20,28},{24,8},{28,20},{1,17},{... | collective-permute-start | bytes 4718600 | tf_op jit(solution)/shard_map/ppermute | solution.py:427
  89.9 33.7 %collective-permute-start.10 = (bf16[2048,384]{1,0:T(8,128)(2,1)}, bf16[2048,384]{1,0:T(8,128)(2,1)}, u32[]{:S(2)}, u32[]{:S(2)}) collective-permute-start(bf16[2048,384]{1,0:T(8,128)(2,1)} %collective-permute-done.2.refs_0_), channel_id=1, source_target_pairs={{0,4},{4,0},{8,12},{12,8},{16,20},{20,16},{24,28},{28,24},{1,5},{5... | collective-permute-start | bytes 4718600 | tf_op jit(solution)/shard_map/ppermute | solution.py:277
  123.8 15.7 %collective-permute-start.12 = (bf16[2048,384]{1,0:T(8,128)(2,1)}, bf16[2048,384]{1,0:T(8,128)(2,1)}, u32[]{:S(2)}, u32[]{:S(2)}) collective-permute-start(bf16[2048,384]{1,0:T(8,128)(2,1)} %collective-permute-done.6.refs_0_), channel_id=1, source_target_pairs={{0,4},{4,0},{8,12},{12,8},{16,20},{20,16},{24,28},{28,24},{1,5},{5... | collective-permute-start | bytes 4718600 | tf_op jit(solution)/shard_map/ppermute | solution.py:277
  124.2 15.2 %collective-permute-start.13 = (bf16[2048,384]{1,0:T(8,128)(2,1)}, bf16[2048,384]{1,0:T(8,128)(2,1)}, u32[]{:S(2)}, u32[]{:S(2)}) collective-permute-start(bf16[2048,384]{1,0:T(8,128)(2,1)} %collective-permute-done.7.refs_1_), channel_id=1, source_target_pairs={{0,4},{4,0},{8,12},{12,8},{16,20},{20,16},{24,28},{28,24},{1,5},{5... | collective-permute-start | bytes 4718600 | tf_op jit(solution)/shard_map/ppermute | solution.py:277
  124.3 36.4 %collective-permute-start.14 = (bf16[384,2048]{1,0:T(8,128)(2,1)}, bf16[384,2048]{1,0:T(8,128)(2,1)}, u32[]{:S(2)}, u32[]{:S(2)}) collective-permute-start(bf16[384,2048]{1,0:T(8,128)(2,1)} %bitcast.3.refs_6_), channel_id=1, source_target_pairs={{0,8},{4,20},{8,0},{12,28},{16,24},{20,4},{24,16},{28,12},{1,9},{5... | collective-permute-start | bytes 4718600 | tf_op jit(solution)/shard_map/ppermute | solution.py:427
  126.3 35.3 %collective-permute-start.15 = (bf16[384,2048]{1,0:T(8,128)(2,1)}, bf16[384,2048]{1,0:T(8,128)(2,1)}, u32[]{:S(2)}, u32[]{:S(2)}) collective-permute-start(bf16[384,2048]{1,0:T(8,128)(2,1)} %bitcast.3.refs_6_), channel_id=1, source_target_pairs={{0,16},{4,12},{8,24},{12,4},{16,0},{20,28},{24,8},{28,20},{1,17},{... | collective-permute-start | bytes 4718600 | tf_op jit(solution)/shard_map/ppermute | solution.py:427
  132.7 45.5 %collective-permute-start.16 = (bf16[384,2048]{1,0:T(8,128)(2,1)}, bf16[384,2048]{1,0:T(8,128)(2,1)}, u32[]{:S(2)}, u32[]{:S(2)}) collective-permute-start(bf16[384,2048]{1,0:T(8,128)(2,1)} %bitcast.3.refs_6_), channel_id=1, source_target_pairs={{0,4},{4,0},{8,12},{12,8},{16,20},{20,16},{24,28},{28,24},{1,5},{5... | collective-permute-start | bytes 4718600 | tf_op jit(solution)/shard_map/ppermute | solution.py:277
  161.6 16.6 %collective-permute-start.17 = (bf16[384,2048]{1,0:T(8,128)(2,1)}, bf16[384,2048]{1,0:T(8,128)(2,1)}, u32[]{:S(2)}, u32[]{:S(2)}) collective-permute-start(bf16[384,2048]{1,0:T(8,128)(2,1)} %collective-permute-done.14.refs_8_), channel_id=1, source_target_pairs={{0,4},{4,0},{8,12},{12,8},{16,20},{20,16},{24,28},{28,24},{1,5},{5... | collective-permute-start | bytes 4718600 | tf_op jit(solution)/shard_map/ppermute | solution.py:277
  161.8 16.5 %collective-permute-start.18 = (bf16[384,2048]{1,0:T(8,128)(2,1)}, bf16[384,2048]{1,0:T(8,128)(2,1)}, u32[]{:S(2)}, u32[]{:S(2)}) collective-permute-start(bf16[384,2048]{1,0:T(8,128)(2,1)} %collective-permute-done.15.refs_10_), channel_id=1, source_target_pairs={{0,4},{4,0},{8,12},{12,8},{16,20},{20,16},{24,28},{28,24},{1,5},{5... | collective-permute-start | bytes 4718600 | tf_op jit(solution)/shard_map/ppermute | solution.py:277
  162.2 27.3 %collective-permute-start.19 = (bf16[384,2048]{1,0:T(8,128)(2,1)}, bf16[384,2048]{1,0:T(8,128)(2,1)}, u32[]{:S(2)}, u32[]{:S(2)}) collective-permute-start(bf16[384,2048]{1,0:T(8,128)(2,1)} %collective-permute-done.14.refs_8_), channel_id=1, source_target_pairs={{0,16},{4,12},{8,24},{12,4},{16,0},{20,28},{24,8},{28,20},{1,17},{... | collective-permute-start | bytes 4718600 | tf_op jit(solution)/shard_map/ppermute | solution.py:427
  204.8 15.6 %all-to-all-start = ((bf16[4,8,2048]{2,1,0:T(8,128)(2,1)}), bf16[4,8,2048]{2,1,0:T(8,128)(2,1)S(1)}, u32[]{:S(2)}, u32[]{:S(2)}) async-start(bf16[4,8,2048]{2,1,0:T(8,128)(2,1)} %broadcast_in_dim.127), calls=%async_computation.2 | async-start | bytes 262144 | tf_op jit(solution)/shard_map/all_to_all | solution.py:58
  241.2 58.9 %all-gather.5.cloned.1.call-start = ((), (), s32[]{:S(2)}) async-start(), calls=%async_computation.10 | async-start | bytes 2621440 | tf_op jit(solution)/shard_map/all_gather | solution.py:468
  (32 other events, 860.0 us)
Sparse Core Ops, SparseCore 0:
  13.7 46.5 reduce-scatter.2
  73.3 46.2 all-gather.2
  203.4 47.5 reduce-scatter.4
  253.3 46.7 all-gather.4

commit v4 on v3

--- a/solution.py
+++ b/solution.py
@@ -14,7 +14,7 @@
 EPSILON = 1e-06
 ROPE_THETA = 1000000.0
 NEGATIVE = -1e30
-VMEM_BYTES = 52 * 1024 * 1024
+VMEM_BYTES = 60 * 1024 * 1024
 
 
 def rms_norm(hidden, gain_vector):
@@ -58,41 +58,43 @@
     return jnp.sum(lax.all_to_all(spread, axis, 0, 0, tiled=True).astype(jnp.float32), axis=0)
 
 
-def inner_kernel(x_ref, *refs):
-    sets, outs = refs[:6], refs[6:]
+def inner_kernel(sets, at, x_ref, factor_ref, *refs):
+    outs = refs[2 * sets :]
     tile = outs[0].shape[1]
-    weights = jnp.concatenate([sets[0][...], sets[1][...], sets[3][...], sets[4][...]], axis=1)
-    products = jnp.dot(x_ref[...], weights, preferred_element_type=jnp.float32)
-    for which, out in enumerate(outs):
-        gate = products[:, 2 * which * tile : (2 * which + 1) * tile]
-        up = products[:, (2 * which + 1) * tile : (2 * which + 2) * tile]
-        out[...] = (jax.nn.silu(gate) * up * sets[3 * which + 2][...]).astype(jnp.bfloat16)
-
-
-def inner_pair(normed, sets):
+    for pair in range(0, sets, 2):
+        weights = jnp.concatenate([ref[...] for ref in refs[2 * pair : 2 * pair + 4]], axis=1)
+        products = jnp.dot(x_ref[...], weights, preferred_element_type=jnp.float32)
+        for which in range(2):
+            gate = products[:, 2 * which * tile : (2 * which + 1) * tile]
+            up = products[:, (2 * which + 1) * tile : (2 * which + 2) * tile]
+            place = at + pair + which
+            inner = jax.nn.silu(gate) * up * factor_ref[:, place : place + 1]
+            outs[pair + which][...] = inner.astype(jnp.bfloat16)
+
+
+def inner_of(normed, factors, gates, ups, at):
     tok_rows, model_width = normed.shape
+    half = gates[0].shape[1]
     tile = 128
-    half = sets[0][0].shape[1]
-    half = half // 2 if sets[0][0] is sets[0][1] else half
-    steps = half // tile
-    gate = pl.BlockSpec((model_width, tile), lambda step: (0, step))
-    second = pl.BlockSpec((model_width, tile), lambda step: (0, step + steps))
-    factor = pl.BlockSpec((tok_rows, 1), lambda step: (0, 0))
-    specs = [
-        spec for one, two, _ in sets for spec in (gate, second if one is two else gate, factor)
-    ]
-    return pl.pallas_call(
-        inner_kernel,
-        grid=(steps,),
-        out_shape=[jax.ShapeDtypeStruct((tok_rows, half), jnp.bfloat16)] * 2,
-        in_specs=[pl.BlockSpec((tok_rows, model_width), lambda step: (0, 0))]
-        + specs,
-        out_specs=[pl.BlockSpec((tok_rows, tile), lambda step: (0, step))] * 2,
-        compiler_params=pltpu.CompilerParams(vmem_limit_bytes=VMEM_BYTES),
-        cost_estimate=pl.CostEstimate(
-            flops=tok_rows, bytes_accessed=tok_rows, transcendentals=0
-        ),
-    )(normed, *[value for one in sets for value in one])
+    sets = len(gates)
+    moving = pl.BlockSpec((model_width, tile), lambda step: (0, step))
+
+    def fixed(shape):
+        return pl.BlockSpec(shape, lambda step: (0, 0))
+
+    return list(
+        pl.pallas_call(
+            lambda *refs: inner_kernel(sets, at, *refs),
+            grid=(half // tile,),
+            out_shape=[jax.ShapeDtypeStruct((tok_rows, half), jnp.bfloat16)] * sets,
+            in_specs=[fixed(normed.shape), fixed(factors.shape)] + [moving] * 2 * sets,
+            out_specs=[pl.BlockSpec((tok_rows, tile), lambda step: (0, step))] * sets,
+            compiler_params=pltpu.CompilerParams(vmem_limit_bytes=VMEM_BYTES),
+            cost_estimate=pl.CostEstimate(
+                flops=tok_rows, bytes_accessed=tok_rows, transcendentals=0
+            ),
+        )(normed, factors, *[value for both in zip(gates, ups) for value in both])
+    )
 
 
 def down_kernel(sets, *refs):
@@ -297,12 +299,6 @@
     return jnp.sum(jnp.where(routes == expert, route_weight, 0.0), axis=1, keepdims=True)
 
 
-def inner_of(rows, gate, up, factor):
-    gate_part = jnp.dot(rows, gate, preferred_element_type=jnp.float32)
-    up_part = jnp.dot(rows, up, preferred_element_type=jnp.float32)
-    return (jax.nn.silu(gate_part) * up_part * factor).astype(jnp.bfloat16)
-
-
 def experts_sent(normed, routes, route_weight, w_gate, w_up, w_down, col_count):
     col_index = lax.axis_index("col")
     row_count = lax.axis_size("row")
@@ -426,46 +422,65 @@
         def to(value, pairs):
             return lax.ppermute(value, "row", pairs)
 
-        gate_near, up_near, gate_far = to(gate, first), to(up, first), to(gate, second)
+        gate_near, up_near = to(gate, first), to(up, first)
+        experts = [expert_of(source, col_count) for source in row_sources()]
+        factors = [naming(routes, route_weight, expert) for expert in experts]
+        factors = jnp.pad(jnp.concatenate(factors, axis=1), ((0, 0), (0, 128 - len(factors))))
         gate_core, up_core = other_core(gate), other_core(up)
-        summed, gate_near, up_near, gate_far, gate_core, up_core = ordered(
-            summed, gate_near, up_near, gate_far, gate_core, up_core
+        width = share_width // 2
+        by_device = w_down[0].reshape(-1, col_count, share_width)
+        down_a, down_b = [
+            by_device[:, :, begin : begin + width].reshape(-1, col_count * width)
+            for begin in (0, width)
+        ]
+        near = to(down_a, first)
+        summed, factors, gate_near, up_near, near, gate_core, up_core, down_a, down_b = ordered(
+            summed, factors, gate_near, up_near, near, gate_core, up_core, down_a, down_b
         )
     hidden_mid = (residual.astype(jnp.float32) + summed.astype(jnp.float32)).astype(jnp.bfloat16)
     full_mid = lax.all_gather(hidden_mid, "col", axis=1, tiled=True)
     if dense:
-        up_near, up_again = ordered(up_near, up)
-        up_far, gate_far_2, up_far_2 = to(up_again, second), to(gate_near, second), to(up_near, second)
-        cores = [other_core(value) for value in (gate_near, up_near, gate_far)]
-        full_mid, up_far, gate_far_2, up_far_2, down, *cores = ordered(
-            full_mid, up_far, gate_far_2, up_far_2, w_down[0], *cores
+        gate_near, up_near, gate_again, up_again = ordered(gate_near, up_near, gate, up)
+        gate_far, up_far = to(gate_again, second), to(up_again, second)
+        near_cores = [other_core(value) for value in (gate_near, up_near)]
+        gate_far, gate_near, up_near = ordered(gate_far, gate_near, up_near)
+        gate_far_2, up_far_2 = to(gate_near, second), to(up_near, second)
+        far_cores = [other_core(value) for value in (gate_far, up_far)]
+        full_mid, *cores = ordered(full_mid, *near_cores, *far_cores)
+        normed = rms_norm(full_mid, gain_post)
+
+        def sets_of(gates, ups, at):
+            return inner_of(normed, factors, gates, ups, at)
+
+        inners = sets_of(
+            [gate, gate_core, gate_near, cores[0], gate_far, cores[2]],
+            [up, up_core, up_near, cores[1], up_far, cores[3]],
+            0,
         )
-        normed = rms_norm(full_mid, gain_post)
-        near, far = to(down, first), to(down, second)
-        factors = [
-            naming(routes, route_weight, expert_of(source, col_count)) for source in row_sources()
-        ]
-
-        def pair_of(gates, ups, at):
-            return inner_pair(normed, list(zip(gates, ups, factors[at : at + 2])))
-
-        inners = [
-            *pair_of([gate, gate_core], [up, up_core], 0),
-            *pair_of([gate_near, cores[0]], [up_near, cores[1]], 2),
-            *pair_of([gate_far, cores[2]], [up_far, other_core(up_far)], 4),
-        ]
-        far_2_cores = [other_core(gate_far_2), other_core(up_far_2)]
-        normed, inners[5], *far_2_cores = ordered(normed, inners[5], *far_2_cores)
-        inners += pair_of([gate_far_2, far_2_cores[0]], [up_far_2, far_2_cores[1]], 6)
-        inners[7], near, far = ordered(inners[7], near, far)
+        inners[5], gate_far_2, down_a, near = ordered(inners[5], gate_far_2, down_a, near)
+        far, last = to(down_a, second), to(near, second)
+        inners += sets_of(
+            [gate_far_2, other_core(gate_far_2)], [up_far_2, other_core(up_far_2)], 6
+        )
+        inners[7], far, down_b = ordered(inners[7], far, down_b)
+        downs = both_cores(down_a, near, far, last)
+        near, far = to(down_b, first), to(down_b, second)
+        total, top = down_sum(inners, downs, None, dec_count)
+        tops = [top]
+        moe_parts = [lax.psum_scatter(total, "col", scatter_dimension=1, tiled=True)]
+        tops[0], near = ordered(tops[0], near)
         last = to(near, second)
-        partial = down_sum(inners[:6], both_cores(down, near, far))
+        partial = down_sum(inners[:6], both_cores(down_b, near, far))
         partial, last = ordered(partial, last)
         total, top = down_sum(inners[6:], both_cores(last), partial, dec_count)
-        moe_share = lax.psum_scatter(total, "col", scatter_dimension=1, tiled=True)
-        hidden_out = hidden_mid.astype(jnp.float32) + moe_share.astype(jnp.float32)
-        hidden_out = hidden_out.astype(jnp.bfloat16)
+        top, moe_parts[0] = ordered(top, moe_parts[0])
+        tops.append(top)
+        moe_parts.append(lax.psum_scatter(total, "col", scatter_dimension=1, tiled=True))
+        moe_share = jnp.concatenate(moe_parts, axis=1).astype(jnp.float32)
+        hidden_out = (hidden_mid.astype(jnp.float32) + moe_share).astype(jnp.bfloat16)
         full_out = lax.all_gather(hidden_out, "col", axis=1, tiled=True)
+        top = jnp.concatenate([top.reshape(dec_count, col_count, width) for top in tops], axis=2)
+        top = top.reshape(dec_count, model_width)
         dec_hidden = full_mid[:dec_count].astype(jnp.float32) + shared_sum(top.astype(jnp.bfloat16), "col")
         dec_in = rms_norm(dec_hidden.astype(jnp.bfloat16), gain_input)
     else:

time: 320 us -> 309 us (0.966)
  waiting for transfers between devices: 156 us -> 140 us
  local copies, waits for them, and re-layouts: 14.6 us -> 20 us
  starting transfers between devices: 32.4 us -> 36.5 us
  Pallas kernels: 56.2 us -> 52.9 us
    ppermute x9 -> x12, waiting for transfers between devices: 112 us -> 88.2 us  [to(): return lax.ppermute(value, 'row', pairs)]
    all_gather x1, waiting for transfers between devices: 0.02 us -> 10.5 us  [shards(): full_mid = lax.all_gather(hidden_mid, 'col', axis=1, tiled=True)]
    pallas_call x4 -> x2, Pallas kernels: 27.3 us -> 22.7 us  [inner_of(): pl.pallas_call(lambda *refs: inner_kernel(sets, at, *refs), grid=(half //...]
    all_to_all x1, waiting for transfers between devices: 9.96 us -> 5.65 us  [shared_sum(): lax.all_to_all(spread, axis, 0, 0, tiled=True).astype(jnp.float32)]
    ppermute x9 -> x12, starting transfers between devices: 13.2 us -> 17.1 us  [to(): return lax.ppermute(value, 'row', pairs)]
    another operation x0 -> x1, local copies, waits for them, and re-layouts: none -> 3.87 us  [shards(): by_device = w_down[0].reshape(-1, col_count, share_width)]
    pallas_call x2 -> x3, Pallas kernels: 19.4 us -> 20.1 us  [down_sum(): pl.pallas_call(lambda *refs: down_kernel(sets, *refs), grid=(width // til...]
  transfers between devices with their start and end apart: 29 -> 37, of which waited for: 13 -> 17; matrix products, arithmetic and copies ran while one was open for 10% -> 13% of each run, Pallas kernels for 12% -> 14%
where the time goes in v4:
time: 309 us; the launch traced here: 308 us
  waiting for transfers between devices  140 us (45%)
  Pallas kernels  52.9 us (17%)
  starting transfers between devices  36.5 us (12%)
  local copies, waits for them, and re-layouts  20 us (6%)
  other arithmetic  19.5 us (6%)
  between operations  14.2 us (5%)
  blocking collectives  12.5 us (4%)
  matrix products  12.3 us (4%)
    ppermute x12, waiting for transfers between devices, to(): return lax.ppermute(value, 'row', pairs)  88.2 us
    pallas_call x2, Pallas kernels, inner_of(): pl.pallas_call(lambda *refs: inner_kernel(sets, at, *refs), grid=(half //...  22.7 us
    pallas_call x3, Pallas kernels, down_sum(): pl.pallas_call(lambda *refs: down_kernel(sets, *refs), grid=(width // til...  20.1 us
    ppermute x12, starting transfers between devices, to(): return lax.ppermute(value, 'row', pairs)  17.1 us
    all_gather x1, waiting for transfers between devices, shards(): full_out = lax.all_gather(hidden_out, 'col', axis=1, tiled=True)  16.9 us
    all_to_all x1, blocking collectives, shards(): lax.all_to_all(packed(by_col(accum_out), by_col(score_top), by_col(weight...  12.5 us
    all_gather x1, waiting for transfers between devices, shards(): full_mid = lax.all_gather(hidden_mid, 'col', axis=1, tiled=True)  10.5 us
    pallas_call x1, Pallas kernels, tail(): pl.pallas_call(lambda *refs: tail_kernel(count, window, *refs), grid=(que...  10.1 us
  transfers between devices with their start and end apart: 37, of which 17 were waited for; matrix products, arithmetic and copies ran while one was open for 13% of the time, Pallas kernels for 14%

profile of v4, /device:TPU:0, one launch (start us, length us, event | category | flops | bytes accessed | tf_op | source)
XLA Modules:
  0.0 308.1 jit_solution(17209617016011688393)
XLA Ops:
  7.2 6.3 %convolution_convert_fusion = bf16[512,2048]{1,0:T(8,128)(2,1)} fusion(bf16[512,1024]{1,0:T(8,128)(2,1)} %param.17, bf16[1024,2048]{1,0:T(8,128)(2,1)} %param.19), kind=kOutput, calls=%fused_computation.5 | convolution fusion | flops 2148532224 | bytes 7340032 | tf_op jit(solution)/shard_map/dot_general | solution.py:415
  17.2 3.9 %reshape_squeeze.3 = bf16[384,4,512]{2,1,0:T(4,128)(2,1)} reshape(bf16[1,384,2048]{2,1,0:T(8,128)(2,1)} %param.26) | data formatting | bytes 3145728 | tf_op jit(solution)/shard_map/reshape;squeeze | solution.py:431
  29.4 31.2 %collective-permute-done.2.refs_10_ = bf16[384,1024]{1,0:T(8,128)(2,1)} collective-permute-done((bf16[384,1024]{1,0:T(8,128)(2,1)}, bf16[384,1024]{1,0:T(8,128)(2,1)}, u32[]{:S(2)}, u32[]{:S(2)}) %collective-permute-start.2) | collective-permute-done | bytes 786464 | tf_op jit(solution)/shard_map/ppermute | solution.py:423
  65.7 15.8 %collective-permute-done.7.refs_10_ = bf16[2048,384]{1,0:T(8,128)(2,1)} collective-permute-done((bf16[2048,384]{1,0:T(8,128)(2,1)}, bf16[2048,384]{1,0:T(8,128)(2,1)}, u32[]{:S(2)}, u32[]{:S(2)}) %collective-permute-start.7) | collective-permute-done | bytes 1572896 | tf_op jit(solution)/shard_map/ppermute | solution.py:423
  81.5 16.8 %collective-permute-done.9.refs_11_ = bf16[2048,384]{1,0:T(8,128)(2,1)} collective-permute-done((bf16[2048,384]{1,0:T(8,128)(2,1)}, bf16[2048,384]{1,0:T(8,128)(2,1)}, u32[]{:S(2)}, u32[]{:S(2)}) %collective-permute-start.9) | collective-permute-done | bytes 1572896 | tf_op jit(solution)/shard_map/ppermute | solution.py:423
  102.1 10.5 %all-gather.3.cloned.1.call-done = bf16[512,2048]{1,0:T(8,128)(2,1)} async-done(((bf16[512,512]{1,0:T(8,128)(2,1)}), bf16[512,2048]{1,0:T(8,128)(2,1)}) %all-gather.3.cloned.1.call-update) | async-done | bytes 2097168 | tf_op jit(solution)/shard_map/all_gather | solution.py:441
  116.7 15.4 %shard_map.184 = (bf16[512,384]{1,0:T(8,128)(2,1)}, bf16[512,384]{1,0:T(8,128)(2,1)}, bf16[512,384]{1,0:T(8,128)(2,1)}, bf16[512,384]{1,0:T(8,128)(2,1)}, bf16[5...) custom-call(bf16[512,2048]{1,0:T(8,128)(2,1)} %fusion.2.refs_0_, f32[512,128]{1,0:T(8,128)} %pad.17.refs_1_, ...), custom_call_target="tpu_custom_call" | custom-call | flops 512 | bytes 512 | tf_op jit(solution)/shard_map/pallas_call | solution.py:86
  132.3 3.7 %collective-permute-done.12.refs_3_ = bf16[2048,384]{1,0:T(8,128)(2,1)} collective-permute-done((bf16[2048,384]{1,0:T(8,128)(2,1)}, bf16[2048,384]{1,0:T(8,128)(2,1)}, u32[]{:S(2)}, u32[]{:S(2)}) %collective-permute-start.12) | collective-permute-done | bytes 1572896 | tf_op jit(solution)/shard_map/ppermute | solution.py:423
  138.2 10.1 %collective-permute-done.20.refs_14_ = bf16[384,1024]{1,0:T(8,128)(2,1)} collective-permute-done((bf16[384,1024]{1,0:T(8,128)(2,1)}, bf16[384,1024]{1,0:T(8,128)(2,1)}, u32[]{:S(2)}, u32[]{:S(2)}) %collective-permute-start.20) | collective-permute-done | bytes 786464 | tf_op jit(solution)/shard_map/ppermute | solution.py:423
  148.8 7.3 %shard_map.185 = (bf16[512,384]{1,0:T(8,128)(2,1)}, bf16[512,384]{1,0:T(8,128)(2,1)}) custom-call(bf16[512,2048]{1,0:T(8,128)(2,1)} %fusion.2.refs_0_, f32[512,128]{1,0:T(8,128)} %pad.17.refs_1_, bf16[2048,384]{1,0:T(8,128)(2,1)} %collective-permute-done.11.refs_2_, bf16[2048,384]{1,0:T(8,128)(2,1)} %collective-permute-done.12.refs_3_, ...), custom_call_target="tpu_custom_call" | custom-call | flops 512 | bytes 512 | tf_op jit(solution)/shard_map/pallas_call | solution.py:86
  161.1 8.0 %shard_map.186 = (bf16[512,1024]{1,0:T(8,128)(2,1)}, f32[8,1024]{1,0:T(8,128)}) custom-call(bf16[512,384]{1,0:T(8,128)(2,1)} %get-tuple-element.79.refs_0_, bf16[512,384]{1,0:T(8,128)(2,1)} %get-tuple-element.80.refs_1_, bf16[512,384]{1,0:T(8,128)(2,1)} %get-tuple-element.81.refs_2_, bf16[512,384]{1,0:T(8,128)(2,1)} %get-tuple-element.82.refs_3_, ...), custom_call_target="tpu_custom_call" | custom-call | flops 3221225472 | bytes 11534336 | tf_op jit(solution)/shard_map/pallas_call | solution.py:133
  169.2 6.6 %collective-permute-done.22.refs_8_ = bf16[384,1024]{1,0:T(8,128)(2,1)} collective-permute-done((bf16[384,1024]{1,0:T(8,128)(2,1)S(1)}, bf16[384,1024]{1,0:T(8,128)(2,1)}, u32[]{:S(2)}, u32[]{:S(2)}) %collective-permute-start.22) | collective-permute-done | bytes 786464 | tf_op jit(solution)/shard_map/ppermute | solution.py:423
  180.4 7.1 %shard_map.187.refs_4_ = f32[512,1024]{1,0:T(8,128)} custom-call(bf16[512,384]{1,0:T(8,128)(2,1)} %get-tuple-element.79.refs_0_, bf16[512,384]{1,0:T(8,128)(2,1)} %get-tuple-element.80.refs_1_, bf16[512,384]{1,0:T(8,128)(2,1)} %get-tuple-element.81.refs_2_, bf16[512,384]{1,0:T(8,128)(2,1)} %get-tuple-element.82.refs_3_, ...), custom_call_target="tpu_custom_call" | custom-call | flops 2415919104 | bytes 9175040 | tf_op jit(solution)/shard_map/pallas_call | solution.py:133
  193.1 5.0 %shard_map.188 = (bf16[512,1024]{1,0:T(8,128)(2,1)}, f32[8,1024]{1,0:T(8,128)}) custom-call(bf16[512,384]{1,0:T(8,128)(2,1)} %get-tuple-element.74.refs_6_.refs_0_, bf16[512,384]{1,0:T(8,128)(2,1)} %get-tuple-element.78.refs_7_.refs_1_, bf16[384,1024]{1,0:T(8,128)(2,1)} %collective-permute-done.26.refs_2_, bf16[384,1024]{1,0:T(8,128)(2,1)} %copy-done.6, ...), custom_call_target="tpu_custom_call" | custom-call | flops 805306368 | bytes 4456448 | tf_op jit(solution)/shard_map/pallas_call | solution.py:133
  199.5 5.4 %all-to-all-start = ((bf16[4,8,2048]{2,1,0:T(8,128)(2,1)}), bf16[4,8,2048]{2,1,0:T(8,128)(2,1)S(1)}, u32[]{:S(2)}, u32[]{:S(2)}) async-start(bf16[4,8,2048]{2,1,0:T(8,128)(2,1)} %broadcast_in_dim.127), calls=%async_computation.3 | async-start | bytes 262144 | tf_op jit(solution)/shard_map/all_to_all | solution.py:58
  205.5 5.7 %all-to-all-done = bf16[4,8,2048]{2,1,0:T(8,128)(2,1)S(1)} async-done(((bf16[4,8,2048]{2,1,0:T(8,128)(2,1)}), bf16[4,8,2048]{2,1,0:T(8,128)(2,1)S(1)}, u32[]{:S(2)}, u32[]{:S(2)}) %all-to-all-start) | async-done | bytes 131104 | tf_op jit(solution)/shard_map/all_to_all | solution.py:58
  218.2 4.0 %all-to-all-start.1 = ((bf16[8,8,1152]{2,1,0:T(8,128)(2,1)}), bf16[8,8,1152]{2,1,0:T(8,128)(2,1)}, u32[]{:S(2)}, u32[]{:S(2)}) async-start(bf16[8,8,1152]{2,1,0:T(8,128)(2,1)} %multiply_reduce_fusion), calls=%async_computation.4 | async-start | bytes 294912 | tf_op jit(solution)/shard_map/all_to_all | solution.py:508
  222.2 5.7 %all-to-all-done.1 = bf16[8,8,1152]{2,1,0:T(8,128)(2,1)} async-done(((bf16[8,8,1152]{2,1,0:T(8,128)(2,1)}), bf16[8,8,1152]{2,1,0:T(8,128)(2,1)}, u32[]{:S(2)}, u32[]{:S(2)}) %all-to-all-start.1) | async-done | bytes 147488 | tf_op jit(solution)/shard_map/all_to_all | solution.py:508
  230.8 3.9 %all-to-all-start.2 = ((bf16[4,8,1152]{2,1,0:T(8,128)(2,1)}), bf16[4,8,1152]{2,1,0:T(8,128)(2,1)}, u32[]{:S(2)}, u32[]{:S(2)}) async-start(bf16[4,8,1152]{2,1,0:T(8,128)(2,1)} %broadcast_in_dim.128), calls=%async_computation.5 | async-start | bytes 147456 | tf_op jit(solution)/shard_map/all_to_all | solution.py:510
  235.6 5.0 %all-to-all-done.2 = bf16[4,8,1152]{2,1,0:T(8,128)(2,1)} async-done(((bf16[4,8,1152]{2,1,0:T(8,128)(2,1)}), bf16[4,8,1152]{2,1,0:T(8,128)(2,1)}, u32[]{:S(2)}, u32[]{:S(2)}) %all-to-all-start.2) | async-done | bytes 73760 | tf_op jit(solution)/shard_map/all_to_all | solution.py:510
  248.7 12.5 %all_to_all.25 = f32[4,72,128]{2,1,0:T(8,128)S(1)} all-to-all(f32[4,72,128]{2,1,0:T(8,128)S(1)} %select_maximum_fusion), channel_id=1, replica_groups=mesh['row'=8,'col'=4] {'col'}, dimensions={0} | all-to-all | bytes 294912 | tf_op jit(solution)/shard_map/all_to_all | solution.py:578
  268.6 4.4 %all-to-all-done.4 = f32[8,72,128]{2,1,0:T(8,128)S(1)} async-done(((f32[8,72,128]{2,1,0:T(8,128)}), f32[8,72,128]{2,1,0:T(8,128)S(1)}, u32[]{:S(2)}, u32[]{:S(2)}) %all-to-all-start.4) | async-done | bytes 294944 | tf_op jit(solution)/shard_map/all_to_all | solution.py:591
  274.0 16.9 %all-gather.5.cloned.1.call-done.refs_1_ = bf16[512,2048]{1,0:T(8,128)(2,1)} async-done(((bf16[512,512]{1,0:T(8,128)(2,1)}), bf16[512,2048]{1,0:T(8,128)(2,1)}) %all-gather.5.cloned.1.call-update) | async-done | bytes 2097168 | tf_op jit(solution)/shard_map/all_gather | solution.py:481
  290.9 10.1 %shard_map.189 = (bf16[512,512]{1,0:T(8,128)(2,1)}, bf16[512,256]{1,0:T(8,128)(2,1)}, bf16[512,1024]{1,0:T(8,128)(2,1)}) custom-call(s32[1]{0:T(128)} %bitcast.refs_0_, bf16[512,2048]{1,0:T(8,128)(2,1)} %all-gather.5.cloned.1.call-done.refs_1_, bf16[1,2048]{1,0:T(2,128)(2,1)} %broadcast_in_dim.124.refs_2_, bf16[2048,1024]{1,0:T(8,128)(2,1)} %refs_3_.1, ...), custom_call_target="tpu_custom_call" | custom-call | flops 2684354560 | bytes 9437184 | tf_op jit(solution)/shard_map/pallas_call | solution.py:222
  (185 shorter events, 72.5 us)
Async XLA Ops:
  7.2 53.5 %reduce-scatter.4.cloned.1.call-start = ((), (), s32[]{:S(2)}) async-start(), calls=%async_computation.8 | async-start | bytes 2621440 | tf_op jit(solution)/shard_map/reduce_scatter | solution.py:416
  13.6 99.1 %all-gather.3.cloned.1.call-start = ((), (), s32[]{:S(2)}) async-start(), calls=%async_computation.9 | async-start | bytes 2621440 | tf_op jit(solution)/shard_map/all_gather | solution.py:441
  13.6 47.0 %collective-permute-start = (bf16[2048,384]{1,0:T(8,128)(2,1)}, bf16[2048,384]{1,0:T(8,128)(2,1)}, u32[]{:S(2)}, u32[]{:S(2)}) collective-permute-start(bf16[2048,384]{1,0:T(8,128)(2,1)} %bitcast.99), channel_id=1, source_target_pairs={{0,8},{4,20},{8,0},{12,28},{16,24},{20,4},{24,16},{28,12},{1,9},{5... | collective-permute-start | bytes 4718600 | tf_op jit(solution)/shard_map/ppermute | solution.py:423
  16.6 44.0 %collective-permute-start.1 = (bf16[2048,384]{1,0:T(8,128)(2,1)}, bf16[2048,384]{1,0:T(8,128)(2,1)}, u32[]{:S(2)}, u32[]{:S(2)}) collective-permute-start(bf16[2048,384]{1,0:T(8,128)(2,1)} %bitcast.103), channel_id=1, source_target_pairs={{0,8},{4,20},{8,0},{12,28},{16,24},{20,4},{24,16},{28,12},{1,9},{5... | collective-permute-start | bytes 4718600 | tf_op jit(solution)/shard_map/ppermute | solution.py:423
  16.7 43.9 %collective-permute-start.3 = (bf16[2048,384]{1,0:T(8,128)(2,1)}, bf16[2048,384]{1,0:T(8,128)(2,1)}, u32[]{:S(2)}, u32[]{:S(2)}) collective-permute-start(bf16[2048,384]{1,0:T(8,128)(2,1)} %bitcast.100), channel_id=1, source_target_pairs={{0,4},{4,0},{8,12},{12,8},{16,20},{20,16},{24,28},{28,24},{1,5},{5... | collective-permute-start | bytes 4718600 | tf_op jit(solution)/shard_map/ppermute | solution.py:279
  16.7 43.9 %collective-permute-start.4 = (bf16[2048,384]{1,0:T(8,128)(2,1)}, bf16[2048,384]{1,0:T(8,128)(2,1)}, u32[]{:S(2)}, u32[]{:S(2)}) collective-permute-start(bf16[2048,384]{1,0:T(8,128)(2,1)} %bitcast.104), channel_id=1, source_target_pairs={{0,4},{4,0},{8,12},{12,8},{16,20},{20,16},{24,28},{28,24},{1,5},{5... | collective-permute-start | bytes 4718600 | tf_op jit(solution)/shard_map/ppermute | solution.py:279
  25.1 35.5 %collective-permute-start.2 = (bf16[384,1024]{1,0:T(8,128)(2,1)}, bf16[384,1024]{1,0:T(8,128)(2,1)}, u32[]{:S(2)}, u32[]{:S(2)}) collective-permute-start(bf16[384,1024]{1,0:T(8,128)(2,1)} %bitcast.37.refs_8_), channel_id=1, source_target_pairs={{0,8},{4,20},{8,0},{12,28},{16,24},{20,4},{24,16},{28,12},{1,9},{5... | collective-permute-start | bytes 2359304 | tf_op jit(solution)/shard_map/ppermute | solution.py:423
  60.7 20.8 %collective-permute-start.7 = (bf16[2048,384]{1,0:T(8,128)(2,1)}, bf16[2048,384]{1,0:T(8,128)(2,1)}, u32[]{:S(2)}, u32[]{:S(2)}) collective-permute-start(bf16[2048,384]{1,0:T(8,128)(2,1)} %bitcast.101), channel_id=1, source_target_pairs={{0,16},{4,12},{8,24},{12,4},{16,0},{20,28},{24,8},{28,20},{1,17},{... | collective-permute-start | bytes 4718600 | tf_op jit(solution)/shard_map/ppermute | solution.py:423
  62.8 35.6 %collective-permute-start.9 = (bf16[2048,384]{1,0:T(8,128)(2,1)}, bf16[2048,384]{1,0:T(8,128)(2,1)}, u32[]{:S(2)}, u32[]{:S(2)}) collective-permute-start(bf16[2048,384]{1,0:T(8,128)(2,1)} %bitcast.105), channel_id=1, source_target_pairs={{0,16},{4,12},{8,24},{12,4},{16,0},{20,28},{24,8},{28,20},{1,17},{... | collective-permute-start | bytes 4718600 | tf_op jit(solution)/shard_map/ppermute | solution.py:423
  64.9 133.2 %reduce-scatter.6.cloned.1.call-start = ((), (), s32[]{:S(2)}) async-start(), calls=%async_computation.10 | async-start | bytes 1310720 | tf_op jit(solution)/shard_map/reduce_scatter | solution.py:470
  65.1 35.3 %collective-permute-start.5 = (bf16[2048,384]{1,0:T(8,128)(2,1)}, bf16[2048,384]{1,0:T(8,128)(2,1)}, u32[]{:S(2)}, u32[]{:S(2)}) collective-permute-start(bf16[2048,384]{1,0:T(8,128)(2,1)} %collective-permute-done.refs_6_), channel_id=1, source_target_pairs={{0,4},{4,0},{8,12},{12,8},{16,20},{20,16},{24,28},{28,24},{1,5},{5... | collective-permute-start | bytes 4718600 | tf_op jit(solution)/shard_map/ppermute | solution.py:279
  65.2 35.3 %collective-permute-start.6 = (bf16[2048,384]{1,0:T(8,128)(2,1)}, bf16[2048,384]{1,0:T(8,128)(2,1)}, u32[]{:S(2)}, u32[]{:S(2)}) collective-permute-start(bf16[2048,384]{1,0:T(8,128)(2,1)} %collective-permute-done.1.refs_7_), channel_id=1, source_target_pairs={{0,4},{4,0},{8,12},{12,8},{16,20},{20,16},{24,28},{28,24},{1,5},{5... | collective-permute-start | bytes 4718600 | tf_op jit(solution)/shard_map/ppermute | solution.py:279
  81.5 19.0 %collective-permute-start.8 = (bf16[2048,384]{1,0:T(8,128)(2,1)}, bf16[2048,384]{1,0:T(8,128)(2,1)}, u32[]{:S(2)}, u32[]{:S(2)}) collective-permute-start(bf16[2048,384]{1,0:T(8,128)(2,1)} %collective-permute-done.7.refs_10_), channel_id=1, source_target_pairs={{0,4},{4,0},{8,12},{12,8},{16,20},{20,16},{24,28},{28,24},{1,5},{5... | collective-permute-start | bytes 4718600 | tf_op jit(solution)/shard_map/ppermute | solution.py:279
  98.3 33.8 %collective-permute-start.11 = (bf16[2048,384]{1,0:T(8,128)(2,1)}, bf16[2048,384]{1,0:T(8,128)(2,1)}, u32[]{:S(2)}, u32[]{:S(2)}) collective-permute-start(bf16[2048,384]{1,0:T(8,128)(2,1)} %collective-permute-done.refs_6_), channel_id=1, source_target_pairs={{0,16},{4,12},{8,24},{12,4},{16,0},{20,28},{24,8},{28,20},{1,17},{... | collective-permute-start | bytes 4718600 | tf_op jit(solution)/shard_map/ppermute | solution.py:423
  100.4 35.6 %collective-permute-start.12 = (bf16[2048,384]{1,0:T(8,128)(2,1)}, bf16[2048,384]{1,0:T(8,128)(2,1)}, u32[]{:S(2)}, u32[]{:S(2)}) collective-permute-start(bf16[2048,384]{1,0:T(8,128)(2,1)} %collective-permute-done.1.refs_7_), channel_id=1, source_target_pairs={{0,16},{4,12},{8,24},{12,4},{16,0},{20,28},{24,8},{28,20},{1,17},{... | collective-permute-start | bytes 4718600 | tf_op jit(solution)/shard_map/ppermute | solution.py:423
  132.2 16.1 %collective-permute-start.13 = (bf16[2048,384]{1,0:T(8,128)(2,1)}, bf16[2048,384]{1,0:T(8,128)(2,1)}, u32[]{:S(2)}, u32[]{:S(2)}) collective-permute-start(bf16[2048,384]{1,0:T(8,128)(2,1)} %collective-permute-done.11.refs_2_), channel_id=1, source_target_pairs={{0,4},{4,0},{8,12},{12,8},{16,20},{20,16},{24,28},{28,24},{1,5},{5... | collective-permute-start | bytes 4718600 | tf_op jit(solution)/shard_map/ppermute | solution.py:279
  135.9 12.8 %collective-permute-start.14 = (bf16[2048,384]{1,0:T(8,128)(2,1)}, bf16[2048,384]{1,0:T(8,128)(2,1)}, u32[]{:S(2)}, u32[]{:S(2)}) collective-permute-start(bf16[2048,384]{1,0:T(8,128)(2,1)} %collective-permute-done.12.refs_3_), channel_id=1, source_target_pairs={{0,4},{4,0},{8,12},{12,8},{16,20},{20,16},{24,28},{28,24},{1,5},{5... | collective-permute-start | bytes 4718600 | tf_op jit(solution)/shard_map/ppermute | solution.py:279
  138.0 18.7 %collective-permute-start.15 = (bf16[384,1024]{1,0:T(8,128)(2,1)}, bf16[384,1024]{1,0:T(8,128)(2,1)}, u32[]{:S(2)}, u32[]{:S(2)}) collective-permute-start(bf16[384,1024]{1,0:T(8,128)(2,1)} %bitcast.37.refs_8_), channel_id=1, source_target_pairs={{0,16},{4,12},{8,24},{12,4},{16,0},{20,28},{24,8},{28,20},{1,17},{... | collective-permute-start | bytes 2359304 | tf_op jit(solution)/shard_map/ppermute | solution.py:423
  138.0 20.7 %collective-permute-start.17 = (bf16[384,1024]{1,0:T(8,128)(2,1)}, bf16[384,1024]{1,0:T(8,128)(2,1)}, u32[]{:S(2)}, u32[]{:S(2)}) collective-permute-start(bf16[384,1024]{1,0:T(8,128)(2,1)} %bitcast.37.refs_8_), channel_id=1, source_target_pairs={{0,4},{4,0},{8,12},{12,8},{16,20},{20,16},{24,28},{28,24},{1,5},{5... | collective-permute-start | bytes 2359304 | tf_op jit(solution)/shard_map/ppermute | solution.py:279
  156.7 19.2 %collective-permute-start.22 = (bf16[384,1024]{1,0:T(8,128)(2,1)S(1)}, bf16[384,1024]{1,0:T(8,128)(2,1)}, u32[]{:S(2)}, u32[]{:S(2)}) collective-permute-start(bf16[384,1024]{1,0:T(8,128)(2,1)S(1)} %bitcast.93), channel_id=1, source_target_pairs={{0,8},{4,20},{8,0},{12,28},{16,24},{20,4},{24,16},{28,12},{1,9},{5... | collective-permute-start | bytes 2359304 | tf_op jit(solution)/shard_map/ppermute | solution.py:423
  158.7 18.3 %collective-permute-start.24 = (bf16[384,1024]{1,0:T(8,128)(2,1)S(1)}, bf16[384,1024]{1,0:T(8,128)(2,1)}, u32[]{:S(2)}, u32[]{:S(2)}) collective-permute-start(bf16[384,1024]{1,0:T(8,128)(2,1)S(1)} %bitcast.94), channel_id=1, source_target_pairs={{0,16},{4,12},{8,24},{12,4},{16,0},{20,28},{24,8},{28,20},{1,17},{... | collective-permute-start | bytes 2359304 | tf_op jit(solution)/shard_map/ppermute | solution.py:423
  177.1 12.5 %collective-permute-start.26 = (bf16[384,1024]{1,0:T(8,128)(2,1)}, bf16[384,1024]{1,0:T(8,128)(2,1)}, u32[]{:S(2)}, u32[]{:S(2)}) collective-permute-start(bf16[384,1024]{1,0:T(8,128)(2,1)} %collective-permute-done.22.refs_8_), channel_id=1, source_target_pairs={{0,16},{4,12},{8,24},{12,4},{16,0},{20,28},{24,8},{28,20},{1,17},{... | collective-permute-start | bytes 2359304 | tf_op jit(solution)/shard_map/ppermute | solution.py:423
  204.9 38.7 %reduce-scatter.8.cloned.1.call-start = ((), (), s32[]{:S(2)}) async-start(), calls=%async_computation.11 | async-start | bytes 1310720 | tf_op jit(solution)/shard_map/reduce_scatter | solution.py:478
  234.7 56.2 %all-gather.5.cloned.1.call-start = ((), (), s32[]{:S(2)}) async-start(), calls=%async_computation.12 | async-start | bytes 2621440 | tf_op jit(solution)/shard_map/all_gather | solution.py:481
  (35 other events, 786.8 us)
Sparse Core Ops, SparseCore 0:
  13.7 46.5 reduce-scatter.3
  65.0 47.6 all-gather.2
  169.3 27.8 reduce-scatter.5
  208.3 28.7 reduce-scatter.7
  245.7 45.1 all-gather.4

commit v5 on v4

--- a/solution.py
+++ b/solution.py
@@ -52,10 +52,40 @@
     return lax.ppermute(block, axis, [(i, (i + shift) % count) for i in range(count)])
 
 
+def shifted(value, axis, shift):
+    count = lax.axis_size(axis)
+    return lax.ppermute(value, axis, [(i, (i + shift) % count) for i in range(count)])
+
+
+def spread(blocks, axis):
+    count = lax.axis_size(axis)
+    index = lax.axis_index(axis)
+    mine = [
+        lax.dynamic_index_in_dim(blocks, (index + shift) % count, 0, keepdims=False)
+        for shift in range(count)
+    ]
+    return jnp.stack([mine[0]] + [shifted(mine[k], axis, k) for k in range(1, count)])
+
+
+def gathered(block, axis):
+    count = lax.axis_size(axis)
+    index = lax.axis_index(axis)
+    arrived = [block] + [shifted(block, axis, k) for k in range(1, count)]
+    order = jnp.stack(arrived + arrived)
+    return jnp.stack(
+        [
+            lax.dynamic_index_in_dim(order, index - i + count, 0, keepdims=False)
+            for i in range(count)
+        ]
+    )
+
+
 def shared_sum(block, axis):
     count = lax.axis_size(axis)
-    spread = jnp.broadcast_to(block[None], (count,) + block.shape)
-    return jnp.sum(lax.all_to_all(spread, axis, 0, 0, tiled=True).astype(jnp.float32), axis=0)
+    total = block.astype(jnp.float32)
+    for k in range(1, count):
+        total = total + shifted(block, axis, k).astype(jnp.float32)
+    return total
 
 
 def inner_kernel(sets, at, x_ref, factor_ref, *refs):
@@ -147,11 +177,11 @@
     )(*inners, *downs, *([before] if more else []))
 
 
-def tail_kernel(count, window, col_ref, *refs):
-    (full, gain, wq, wkv, cosine, sine, seg_col, seg_row, hidden_ref, cache_ref, out_ref) = refs[:11]
-    x_in, keys, values, bias = refs[11:]
+def tail_kernel(window, *refs):
+    (full, gain, wq, wkv, cosine, sine, seg_col, seg_row, cache_ref, out_ref) = refs[:10]
+    x_in, keys, values, bias = refs[10:]
     tok_rows = x_in.shape[0]
-    rows = tok_rows // count
+    rows = 128
 
     def turn(block):
         floats = block.astype(jnp.float32)
@@ -160,14 +190,11 @@
 
     @pl.when(pl.program_id(0) == 0)
     def _():
-        col = col_ref[0]
         for start in range(0, tok_rows, rows):
             place = slice(start, start + rows)
             floats = full[place, :].astype(jnp.float32)
             inverse = lax.rsqrt(jnp.mean(floats * floats, axis=-1, keepdims=True) + EPSILON)
             x_in[place, :] = (floats * inverse * gain[...].astype(jnp.float32)).astype(jnp.bfloat16)
-        share = hidden_ref.shape[1]
-        hidden_ref[...] = full[:, pl.ds(pl.multiple_of(col * share, share), share)]
         keyval = jnp.dot(x_in[...], wkv[...], preferred_element_type=jnp.float32)
         keyval = keyval.astype(jnp.bfloat16)
         keys[...] = turn(keyval[:, :HD])
@@ -206,7 +233,7 @@
             out_ref[start:stop, head * HD : (head + 1) * HD] = mixed[head * step : (head + 1) * step]
 
 
-def tail(full, count, gain, w_query, w_keyval, cosine, sine, segments, window, col_index):
+def tail(full, gain, w_query, w_keyval, cosine, sine, segments, window):
     tok_rows = segments.shape[0]
     model_width = w_query.shape[0]
     query_width = w_query.shape[1]
@@ -218,18 +245,15 @@
     def moving(shape):
         return pl.BlockSpec(shape, lambda step: (0, step))
 
-    share = model_width // count
     return pl.pallas_call(
-        lambda *refs: tail_kernel(count, window, *refs),
+        lambda *refs: tail_kernel(window, *refs),
         grid=(query_width // some,),
         out_shape=[
-            jax.ShapeDtypeStruct((tok_rows, share), jnp.bfloat16),
             jax.ShapeDtypeStruct((tok_rows, pair), jnp.bfloat16),
             jax.ShapeDtypeStruct((tok_rows, query_width), jnp.bfloat16),
         ],
-        in_specs=[pl.BlockSpec(memory_space=pltpu.SMEM)]
-        + [fixed(full.shape)]
-        + [
+        in_specs=[
+            fixed(full.shape),
             fixed((1, model_width)),
             moving((model_width, some)),
             fixed((model_width, pair)),
@@ -238,7 +262,7 @@
             fixed((tok_rows, 1)),
             fixed((1, tok_rows)),
         ],
-        out_specs=[fixed((tok_rows, share)), fixed((tok_rows, pair)), moving((tok_rows, some))],
+        out_specs=[fixed((tok_rows, pair)), moving((tok_rows, some))],
         scratch_shapes=[
             pltpu.VMEM((tok_rows, model_width), jnp.bfloat16),
             pltpu.VMEM((tok_rows, HD), jnp.bfloat16),
@@ -252,7 +276,6 @@
             transcendentals=tok_rows * tok_rows * query_width // HD,
         ),
     )(
-        col_index[None],
         full,
         gain[None],
         w_query,
@@ -507,13 +530,9 @@
     ).astype(jnp.bfloat16)
     inbox = lax.all_to_all(outbox, "row", split_axis=0, concat_axis=0, tiled=True)
     slot_terms = jnp.sum(inbox.astype(jnp.float32), axis=0).astype(jnp.bfloat16)
-    slot_terms = lax.all_to_all(
-        jnp.broadcast_to(slot_terms[None], (col_count,) + slot_terms.shape),
-        "col",
-        split_axis=0,
-        concat_axis=0,
-        tiled=True,
-    )
+    if dense:
+        slot_terms, hidden_out = ordered(slot_terms, hidden_out)
+    slot_terms = gathered(slot_terms, "col")
     slot_length = slot_terms[0, :, heads_local * HD :][:, :2].astype(jnp.int32)
     slot_length = slot_length[:, 0] * 256 + slot_length[:, 1]
     slot_query = slot_terms[..., : heads_local * HD]
@@ -575,12 +594,8 @@
         value = value.reshape((dec_count, col_count, heads_local) + value.shape[3:])
         return jnp.moveaxis(value, 1, 0)
 
-    spread_terms = lax.all_to_all(
-        packed(by_col(accum_out), by_col(score_top), by_col(weight_mass)),
-        "col",
-        split_axis=0,
-        concat_axis=0,
-        tiled=True,
+    spread_terms = spread(
+        packed(by_col(accum_out), by_col(score_top), by_col(weight_mass)), "col"
     )
     accums, tops, masses = unpacked(spread_terms)
     part_top = jnp.max(tops, axis=0)
@@ -621,9 +636,8 @@
     if dense:
         segments = jnp.concatenate([jnp.full((dec_count,), -1, jnp.int32), segment_ids[0]])
         window = segment_ids.shape[1] // 2
-        hidden_out, new_cache, attention_out = tail(
+        new_cache, attention_out = tail(
             full_out,
-            col_count,
             gain_input,
             w_query,
             w_keyval,
@@ -631,7 +645,6 @@
             tables[1],
             segments,
             window,
-            col_index,
         )
         attention_out = lax.dynamic_update_slice_in_dim(attention_out, decode_out, 0, 0)
         return (hidden_out, new_cache, attention_out)

time: 309 us -> 303 us (0.981)
  blocking collectives: 12.5 us -> 0 us
  starting transfers between devices: 36.5 us -> 41.8 us
    ppermute x0 -> x9, starting transfers between devices: none -> 14.5 us  [shifted(): lax.ppermute(value, axis, [(i, (i + shift) % count) for i in range(count)])]
    all_to_all x1 -> x0, blocking collectives: 12.5 us -> none  [shards(): lax.all_to_all(packed(by_col(accum_out), by_col(score_top), by_col(weight...]
    all_to_all x2 -> x0, waiting for transfers between devices: 10.7 us -> none  [the longest x1 5.65 us: shared_sum(): lax.all_to_all(spread, axis, 0, 0, tiled=True).astype(jnp.float32)]
    ppermute x0 -> x9, waiting for transfers between devices: none -> 9.94 us  [shifted(): lax.ppermute(value, axis, [(i, (i + shift) % count) for i in range(count)])]
    all_to_all x2 -> x0, starting transfers between devices: 9.35 us -> none  [the longest x1 5.44 us: shared_sum(): lax.all_to_all(spread, axis, 0, 0, tiled=True).astype(jnp.float32)]
    reduce_scatter x2, waiting for transfers between devices: 0.01 us -> 4.98 us  [shards(): lax.psum_scatter(total, 'col', scatter_dimension=1, tiled=True)]
    unnamed x48 -> x52, local copies, waits for them, and re-layouts: 5.72 us -> 6.68 us
  transfers between devices with their start and end apart: 37 -> 44, of which waited for: 17 -> 23; matrix products, arithmetic and copies ran while one was open for 13% -> 12% of each run, Pallas kernels for 14% -> 14%
where the time goes in v5:
time: 303 us; the launch traced here: 302 us
  waiting for transfers between devices  143 us (47%)
  Pallas kernels  52.9 us (17%)
  starting transfers between devices  41.8 us (14%)
  other arithmetic  19 us (6%)
  local copies, waits for them, and re-layouts  18.3 us (6%)
  between operations  14.3 us (5%)
  matrix products  12.5 us (4%)
    ppermute x12, waiting for transfers between devices, to(): return lax.ppermute(value, 'row', pairs)  87.2 us
    pallas_call x2, Pallas kernels, inner_of(): pl.pallas_call(lambda *refs: inner_kernel(sets, at, *refs), grid=(half //...  22.8 us
    pallas_call x3, Pallas kernels, down_sum(): pl.pallas_call(lambda *refs: down_kernel(sets, *refs), grid=(width // til...  20.1 us
    all_gather x1, waiting for transfers between devices, shards(): full_out = lax.all_gather(hidden_out, 'col', axis=1, tiled=True)  17.8 us
    ppermute x12, starting transfers between devices, to(): return lax.ppermute(value, 'row', pairs)  17.1 us
    ppermute x9, starting transfers between devices, shifted(): lax.ppermute(value, axis, [(i, (i + shift) % count) for i in range(count)])  14.5 us
    all_gather x1, waiting for transfers between devices, shards(): full_mid = lax.all_gather(hidden_mid, 'col', axis=1, tiled=True)  10.5 us
    pallas_call x1, Pallas kernels, tail(): pl.pallas_call(lambda *refs: tail_kernel(window, *refs), grid=(query_widt...  10 us
  transfers between devices with their start and end apart: 44, of which 23 were waited for; matrix products, arithmetic and copies ran while one was open for 12% of the time, Pallas kernels for 14%

profile of v5, /device:TPU:0, one launch (start us, length us, event | category | flops | bytes accessed | tf_op | source)
XLA Modules:
  0.0 302.2 jit_solution(14973395160519171524)
XLA Ops:
  7.2 6.3 %convolution_convert_fusion = bf16[512,2048]{1,0:T(8,128)(2,1)} fusion(bf16[512,1024]{1,0:T(8,128)(2,1)} %param.17, bf16[1024,2048]{1,0:T(8,128)(2,1)} %param.19), kind=kOutput, calls=%fused_computation.5 | convolution fusion | flops 2148532224 | bytes 7340032 | tf_op jit(solution)/shard_map/dot_general | solution.py:438
  13.6 3.0 collective-permute-start
  17.2 3.8 %reshape_squeeze.3 = bf16[384,4,512]{2,1,0:T(4,128)(2,1)} reshape(bf16[1,384,2048]{2,1,0:T(8,128)(2,1)} %param.26) | data formatting | bytes 3145728 | tf_op jit(solution)/shard_map/reshape;squeeze | solution.py:454
  21.1 2.9 fusion.54
  29.4 31.3 %collective-permute-done.2.refs_10_ = bf16[384,1024]{1,0:T(8,128)(2,1)} collective-permute-done((bf16[384,1024]{1,0:T(8,128)(2,1)}, bf16[384,1024]{1,0:T(8,128)(2,1)}, u32[]{:S(2)}, u32[]{:S(2)}) %collective-permute-start.2) | collective-permute-done | bytes 786464 | tf_op jit(solution)/shard_map/ppermute | solution.py:446
  65.5 16.0 %collective-permute-done.7.refs_10_ = bf16[2048,384]{1,0:T(8,128)(2,1)} collective-permute-done((bf16[2048,384]{1,0:T(8,128)(2,1)}, bf16[2048,384]{1,0:T(8,128)(2,1)}, u32[]{:S(2)}, u32[]{:S(2)}) %collective-permute-start.7) | collective-permute-done | bytes 1572896 | tf_op jit(solution)/shard_map/ppermute | solution.py:446
  81.5 16.8 %collective-permute-done.9.refs_11_ = bf16[2048,384]{1,0:T(8,128)(2,1)} collective-permute-done((bf16[2048,384]{1,0:T(8,128)(2,1)}, bf16[2048,384]{1,0:T(8,128)(2,1)}, u32[]{:S(2)}, u32[]{:S(2)}) %collective-permute-start.9) | collective-permute-done | bytes 1572896 | tf_op jit(solution)/shard_map/ppermute | solution.py:446
  102.1 10.5 %all-gather.3.cloned.1.call-done = bf16[512,2048]{1,0:T(8,128)(2,1)} async-done(((bf16[512,512]{1,0:T(8,128)(2,1)}), bf16[512,2048]{1,0:T(8,128)(2,1)}) %all-gather.3.cloned.1.call-update) | async-done | bytes 2097168 | tf_op jit(solution)/shard_map/all_gather | solution.py:464
  116.7 15.4 %shard_map.184 = (bf16[512,384]{1,0:T(8,128)(2,1)}, bf16[512,384]{1,0:T(8,128)(2,1)}, bf16[512,384]{1,0:T(8,128)(2,1)}, bf16[512,384]{1,0:T(8,128)(2,1)}, bf16[5...) custom-call(bf16[512,2048]{1,0:T(8,128)(2,1)} %fusion.2.refs_0_, f32[512,128]{1,0:T(8,128)} %pad.17.refs_1_, ...), custom_call_target="tpu_custom_call" | custom-call | flops 512 | bytes 512 | tf_op jit(solution)/shard_map/pallas_call | solution.py:116
  132.2 3.7 %collective-permute-done.12.refs_3_ = bf16[2048,384]{1,0:T(8,128)(2,1)} collective-permute-done((bf16[2048,384]{1,0:T(8,128)(2,1)}, bf16[2048,384]{1,0:T(8,128)(2,1)}, u32[]{:S(2)}, u32[]{:S(2)}) %collective-permute-start.12) | collective-permute-done | bytes 1572896 | tf_op jit(solution)/shard_map/ppermute | solution.py:446
  138.2 10.1 %collective-permute-done.19.refs_14_ = bf16[384,1024]{1,0:T(8,128)(2,1)} collective-permute-done((bf16[384,1024]{1,0:T(8,128)(2,1)}, bf16[384,1024]{1,0:T(8,128)(2,1)}, u32[]{:S(2)}, u32[]{:S(2)}) %collective-permute-start.19) | collective-permute-done | bytes 786464 | tf_op jit(solution)/shard_map/ppermute | solution.py:446
  148.8 7.4 %shard_map.185 = (bf16[512,384]{1,0:T(8,128)(2,1)}, bf16[512,384]{1,0:T(8,128)(2,1)}) custom-call(bf16[512,2048]{1,0:T(8,128)(2,1)} %fusion.2.refs_0_, f32[512,128]{1,0:T(8,128)} %pad.17.refs_1_, bf16[2048,384]{1,0:T(8,128)(2,1)} %collective-permute-done.11.refs_2_, bf16[2048,384]{1,0:T(8,128)(2,1)} %collective-permute-done.12.refs_3_, ...), custom_call_target="tpu_custom_call" | custom-call | flops 512 | bytes 512 | tf_op jit(solution)/shard_map/pallas_call | solution.py:116
  161.1 8.0 %shard_map.186 = (bf16[512,1024]{1,0:T(8,128)(2,1)}, f32[8,1024]{1,0:T(8,128)}) custom-call(bf16[512,384]{1,0:T(8,128)(2,1)} %get-tuple-element.71.refs_0_, bf16[512,384]{1,0:T(8,128)(2,1)} %get-tuple-element.72.refs_1_, bf16[512,384]{1,0:T(8,128)(2,1)} %get-tuple-element.73.refs_2_, bf16[512,384]{1,0:T(8,128)(2,1)} %get-tuple-element.74.refs_3_, ...), custom_call_target="tpu_custom_call" | custom-call | flops 3221225472 | bytes 11534336 | tf_op jit(solution)/shard_map/pallas_call | solution.py:163
  169.4 6.4 %collective-permute-done.21.refs_8_ = bf16[384,1024]{1,0:T(8,128)(2,1)} collective-permute-done((bf16[384,1024]{1,0:T(8,128)(2,1)S(1)}, bf16[384,1024]{1,0:T(8,128)(2,1)}, u32[]{:S(2)}, u32[]{:S(2)}) %collective-permute-start.21) | collective-permute-done | bytes 786464 | tf_op jit(solution)/shard_map/ppermute | solution.py:446
  181.6 7.1 %shard_map.187.refs_4_ = f32[512,1024]{1,0:T(8,128)} custom-call(bf16[512,384]{1,0:T(8,128)(2,1)} %get-tuple-element.71.refs_0_, bf16[512,384]{1,0:T(8,128)(2,1)} %get-tuple-element.72.refs_1_, bf16[512,384]{1,0:T(8,128)(2,1)} %get-tuple-element.73.refs_2_, bf16[512,384]{1,0:T(8,128)(2,1)} %get-tuple-element.74.refs_3_, ...), custom_call_target="tpu_custom_call" | custom-call | flops 2415919104 | bytes 9175040 | tf_op jit(solution)/shard_map/pallas_call | solution.py:163
  192.5 5.0 %shard_map.188 = (bf16[512,1024]{1,0:T(8,128)(2,1)}, f32[8,1024]{1,0:T(8,128)}) custom-call(bf16[512,384]{1,0:T(8,128)(2,1)} %get-tuple-element.81.refs_6_.refs_0_, bf16[512,384]{1,0:T(8,128)(2,1)} %get-tuple-element.85.refs_7_.refs_1_, bf16[384,1024]{1,0:T(8,128)(2,1)} %collective-permute-done.26.refs_2_, ...), custom_call_target="tpu_custom_call" | custom-call | flops 805306368 | bytes 4456448 | tf_op jit(solution)/shard_map/pallas_call | solution.py:163
  210.1 2.9 fusion.18
  214.6 4.0 %all-to-all-start = ((bf16[8,8,1152]{2,1,0:T(8,128)(2,1)}), bf16[8,8,1152]{2,1,0:T(8,128)(2,1)}, u32[]{:S(2)}, u32[]{:S(2)}) async-start(bf16[8,8,1152]{2,1,0:T(8,128)(2,1)} %multiply_reduce_fusion), calls=%async_computation.2 | async-start | bytes 294912 | tf_op jit(solution)/shard_map/all_to_all | solution.py:531
  219.3 5.0 %all-to-all-done = bf16[8,8,1152]{2,1,0:T(8,128)(2,1)} async-done(((bf16[8,8,1152]{2,1,0:T(8,128)(2,1)}), bf16[8,8,1152]{2,1,0:T(8,128)(2,1)}, u32[]{:S(2)}, u32[]{:S(2)}) %all-to-all-start) | async-done | bytes 147488 | tf_op jit(solution)/shard_map/all_to_all | solution.py:531
  225.9 5.0 %reduce-scatter.8.cloned.1.call-done = bf16[512,256]{1,0:T(8,128)(2,1)} async-done(((bf16[512,1024]{1,0:T(8,128)(2,1)}), bf16[512,256]{1,0:T(8,128)(2,1)}) %reduce-scatter.8.cloned.1.call-update) | async-done | bytes 262160 | tf_op jit(solution)/shard_map/reduce_scatter | solution.py:501
  255.2 3.7 %all-to-all-start.1 = ((f32[8,72,128]{2,1,0:T(8,128)}), f32[8,72,128]{2,1,0:T(8,128)S(1)}, u32[]{:S(2)}, u32[]{:S(2)}) async-start(f32[8,72,128]{2,1,0:T(8,128)} %broadcast_in_dim.114), calls=%async_computation.4 | async-start | bytes 589824 | tf_op jit(solution)/shard_map/all_to_all | solution.py:606
  261.6 4.5 %all-to-all-done.1 = f32[8,72,128]{2,1,0:T(8,128)S(1)} async-done(((f32[8,72,128]{2,1,0:T(8,128)}), f32[8,72,128]{2,1,0:T(8,128)S(1)}, u32[]{:S(2)}, u32[]{:S(2)}) %all-to-all-start.1) | async-done | bytes 294944 | tf_op jit(solution)/shard_map/all_to_all | solution.py:606
  267.2 17.8 %all-gather.5.cloned.1.call-done.refs_0_ = bf16[512,2048]{1,0:T(8,128)(2,1)} async-done(((bf16[512,512]{1,0:T(8,128)(2,1)}), bf16[512,2048]{1,0:T(8,128)(2,1)}) %all-gather.5.cloned.1.call-update) | async-done | bytes 2097168 | tf_op jit(solution)/shard_map/all_gather | solution.py:504
  285.0 10.0 %shard_map.189 = (bf16[512,256]{1,0:T(8,128)(2,1)}, bf16[512,1024]{1,0:T(8,128)(2,1)}) custom-call(bf16[512,2048]{1,0:T(8,128)(2,1)} %all-gather.5.cloned.1.call-done.refs_0_, bf16[1,2048]{1,0:T(2,128)(2,1)} %broadcast_in_dim.108.refs_1_, bf16[2048,1024]{1,0:T(8,128)(2,1)} %refs_2_.1, bf16[2048,256]{1,0:T(8,128)(2,1)} %refs_3_.1, ...), custom_call_target="tpu_custom_call" | custom-call | flops 2684354560 | bytes 9437184 | tf_op jit(solution)/shard_map/pallas_call | solution.py:248
  (204 shorter events, 81.1 us)
Async XLA Ops:
  7.2 53.5 %reduce-scatter.4.cloned.1.call-start = ((), (), s32[]{:S(2)}) async-start(), calls=%async_computation.5 | async-start | bytes 2621440 | tf_op jit(solution)/shard_map/reduce_scatter | solution.py:439
  13.6 99.1 %all-gather.3.cloned.1.call-start = ((), (), s32[]{:S(2)}) async-start(), calls=%async_computation.6 | async-start | bytes 2621440 | tf_op jit(solution)/shard_map/all_gather | solution.py:464
  13.6 47.0 %collective-permute-start = (bf16[2048,384]{1,0:T(8,128)(2,1)}, bf16[2048,384]{1,0:T(8,128)(2,1)}, u32[]{:S(2)}, u32[]{:S(2)}) collective-permute-start(bf16[2048,384]{1,0:T(8,128)(2,1)} %bitcast.119), channel_id=1, source_target_pairs={{0,8},{4,20},{8,0},{12,28},{16,24},{20,4},{24,16},{28,12},{1,9},{5... | collective-permute-start | bytes 4718600 | tf_op jit(solution)/shard_map/ppermute | solution.py:446
  16.6 44.0 %collective-permute-start.1 = (bf16[2048,384]{1,0:T(8,128)(2,1)}, bf16[2048,384]{1,0:T(8,128)(2,1)}, u32[]{:S(2)}, u32[]{:S(2)}) collective-permute-start(bf16[2048,384]{1,0:T(8,128)(2,1)} %bitcast.123), channel_id=1, source_target_pairs={{0,8},{4,20},{8,0},{12,28},{16,24},{20,4},{24,16},{28,12},{1,9},{5... | collective-permute-start | bytes 4718600 | tf_op jit(solution)/shard_map/ppermute | solution.py:446
  16.7 43.9 %collective-permute-start.3 = (bf16[2048,384]{1,0:T(8,128)(2,1)}, bf16[2048,384]{1,0:T(8,128)(2,1)}, u32[]{:S(2)}, u32[]{:S(2)}) collective-permute-start(bf16[2048,384]{1,0:T(8,128)(2,1)} %bitcast.120), channel_id=1, source_target_pairs={{0,4},{4,0},{8,12},{12,8},{16,20},{20,16},{24,28},{28,24},{1,5},{5... | collective-permute-start | bytes 4718600 | tf_op jit(solution)/shard_map/ppermute | solution.py:302
  16.7 43.9 %collective-permute-start.4 = (bf16[2048,384]{1,0:T(8,128)(2,1)}, bf16[2048,384]{1,0:T(8,128)(2,1)}, u32[]{:S(2)}, u32[]{:S(2)}) collective-permute-start(bf16[2048,384]{1,0:T(8,128)(2,1)} %bitcast.124), channel_id=1, source_target_pairs={{0,4},{4,0},{8,12},{12,8},{16,20},{20,16},{24,28},{28,24},{1,5},{5... | collective-permute-start | bytes 4718600 | tf_op jit(solution)/shard_map/ppermute | solution.py:302
  25.1 35.5 %collective-permute-start.2 = (bf16[384,1024]{1,0:T(8,128)(2,1)}, bf16[384,1024]{1,0:T(8,128)(2,1)}, u32[]{:S(2)}, u32[]{:S(2)}) collective-permute-start(bf16[384,1024]{1,0:T(8,128)(2,1)} %bitcast.46.refs_8_), channel_id=1, source_target_pairs={{0,8},{4,20},{8,0},{12,28},{16,24},{20,4},{24,16},{28,12},{1,9},{5... | collective-permute-start | bytes 2359304 | tf_op jit(solution)/shard_map/ppermute | solution.py:446
  60.7 20.8 %collective-permute-start.7 = (bf16[2048,384]{1,0:T(8,128)(2,1)}, bf16[2048,384]{1,0:T(8,128)(2,1)}, u32[]{:S(2)}, u32[]{:S(2)}) collective-permute-start(bf16[2048,384]{1,0:T(8,128)(2,1)} %bitcast.121), channel_id=1, source_target_pairs={{0,16},{4,12},{8,24},{12,4},{16,0},{20,28},{24,8},{28,20},{1,17},{... | collective-permute-start | bytes 4718600 | tf_op jit(solution)/shard_map/ppermute | solution.py:446
  62.8 35.6 %collective-permute-start.9 = (bf16[2048,384]{1,0:T(8,128)(2,1)}, bf16[2048,384]{1,0:T(8,128)(2,1)}, u32[]{:S(2)}, u32[]{:S(2)}) collective-permute-start(bf16[2048,384]{1,0:T(8,128)(2,1)} %bitcast.125), channel_id=1, source_target_pairs={{0,16},{4,12},{8,24},{12,4},{16,0},{20,28},{24,8},{28,20},{1,17},{... | collective-permute-start | bytes 4718600 | tf_op jit(solution)/shard_map/ppermute | solution.py:446
  64.9 132.7 %reduce-scatter.6.cloned.1.call-start = ((), (), s32[]{:S(2)}) async-start(), calls=%async_computation.7 | async-start | bytes 1310720 | tf_op jit(solution)/shard_map/reduce_scatter | solution.py:493
  64.9 35.5 %collective-permute-start.5 = (bf16[2048,384]{1,0:T(8,128)(2,1)}, bf16[2048,384]{1,0:T(8,128)(2,1)}, u32[]{:S(2)}, u32[]{:S(2)}) collective-permute-start(bf16[2048,384]{1,0:T(8,128)(2,1)} %collective-permute-done.refs_6_), channel_id=1, source_target_pairs={{0,4},{4,0},{8,12},{12,8},{16,20},{20,16},{24,28},{28,24},{1,5},{5... | collective-permute-start | bytes 4718600 | tf_op jit(solution)/shard_map/ppermute | solution.py:302
  65.0 35.5 %collective-permute-start.6 = (bf16[2048,384]{1,0:T(8,128)(2,1)}, bf16[2048,384]{1,0:T(8,128)(2,1)}, u32[]{:S(2)}, u32[]{:S(2)}) collective-permute-start(bf16[2048,384]{1,0:T(8,128)(2,1)} %collective-permute-done.1.refs_7_), channel_id=1, source_target_pairs={{0,4},{4,0},{8,12},{12,8},{16,20},{20,16},{24,28},{28,24},{1,5},{5... | collective-permute-start | bytes 4718600 | tf_op jit(solution)/shard_map/ppermute | solution.py:302
  81.5 19.0 %collective-permute-start.8 = (bf16[2048,384]{1,0:T(8,128)(2,1)}, bf16[2048,384]{1,0:T(8,128)(2,1)}, u32[]{:S(2)}, u32[]{:S(2)}) collective-permute-start(bf16[2048,384]{1,0:T(8,128)(2,1)} %collective-permute-done.7.refs_10_), channel_id=1, source_target_pairs={{0,4},{4,0},{8,12},{12,8},{16,20},{20,16},{24,28},{28,24},{1,5},{5... | collective-permute-start | bytes 4718600 | tf_op jit(solution)/shard_map/ppermute | solution.py:302
  98.3 33.8 %collective-permute-start.11 = (bf16[2048,384]{1,0:T(8,128)(2,1)}, bf16[2048,384]{1,0:T(8,128)(2,1)}, u32[]{:S(2)}, u32[]{:S(2)}) collective-permute-start(bf16[2048,384]{1,0:T(8,128)(2,1)} %collective-permute-done.refs_6_), channel_id=1, source_target_pairs={{0,16},{4,12},{8,24},{12,4},{16,0},{20,28},{24,8},{28,20},{1,17},{... | collective-permute-start | bytes 4718600 | tf_op jit(solution)/shard_map/ppermute | solution.py:446
  100.4 35.6 %collective-permute-start.12 = (bf16[2048,384]{1,0:T(8,128)(2,1)}, bf16[2048,384]{1,0:T(8,128)(2,1)}, u32[]{:S(2)}, u32[]{:S(2)}) collective-permute-start(bf16[2048,384]{1,0:T(8,128)(2,1)} %collective-permute-done.1.refs_7_), channel_id=1, source_target_pairs={{0,16},{4,12},{8,24},{12,4},{16,0},{20,28},{24,8},{28,20},{1,17},{... | collective-permute-start | bytes 4718600 | tf_op jit(solution)/shard_map/ppermute | solution.py:446
  132.2 16.1 %collective-permute-start.13 = (bf16[2048,384]{1,0:T(8,128)(2,1)}, bf16[2048,384]{1,0:T(8,128)(2,1)}, u32[]{:S(2)}, u32[]{:S(2)}) collective-permute-start(bf16[2048,384]{1,0:T(8,128)(2,1)} %collective-permute-done.11.refs_2_), channel_id=1, source_target_pairs={{0,4},{4,0},{8,12},{12,8},{16,20},{20,16},{24,28},{28,24},{1,5},{5... | collective-permute-start | bytes 4718600 | tf_op jit(solution)/shard_map/ppermute | solution.py:302
  135.9 12.8 %collective-permute-start.14 = (bf16[2048,384]{1,0:T(8,128)(2,1)}, bf16[2048,384]{1,0:T(8,128)(2,1)}, u32[]{:S(2)}, u32[]{:S(2)}) collective-permute-start(bf16[2048,384]{1,0:T(8,128)(2,1)} %collective-permute-done.12.refs_3_), channel_id=1, source_target_pairs={{0,4},{4,0},{8,12},{12,8},{16,20},{20,16},{24,28},{28,24},{1,5},{5... | collective-permute-start | bytes 4718600 | tf_op jit(solution)/shard_map/ppermute | solution.py:302
  138.0 18.7 %collective-permute-start.15 = (bf16[384,1024]{1,0:T(8,128)(2,1)}, bf16[384,1024]{1,0:T(8,128)(2,1)}, u32[]{:S(2)}, u32[]{:S(2)}) collective-permute-start(bf16[384,1024]{1,0:T(8,128)(2,1)} %bitcast.46.refs_8_), channel_id=1, source_target_pairs={{0,16},{4,12},{8,24},{12,4},{16,0},{20,28},{24,8},{28,20},{1,17},{... | collective-permute-start | bytes 2359304 | tf_op jit(solution)/shard_map/ppermute | solution.py:446
  138.0 20.7 %collective-permute-start.16 = (bf16[384,1024]{1,0:T(8,128)(2,1)}, bf16[384,1024]{1,0:T(8,128)(2,1)}, u32[]{:S(2)}, u32[]{:S(2)}) collective-permute-start(bf16[384,1024]{1,0:T(8,128)(2,1)} %bitcast.46.refs_8_), channel_id=1, source_target_pairs={{0,4},{4,0},{8,12},{12,8},{16,20},{20,16},{24,28},{28,24},{1,5},{5... | collective-permute-start | bytes 2359304 | tf_op jit(solution)/shard_map/ppermute | solution.py:302
  156.7 19.2 %collective-permute-start.21 = (bf16[384,1024]{1,0:T(8,128)(2,1)S(1)}, bf16[384,1024]{1,0:T(8,128)(2,1)}, u32[]{:S(2)}, u32[]{:S(2)}) collective-permute-start(bf16[384,1024]{1,0:T(8,128)(2,1)S(1)} %bitcast.113), channel_id=1, source_target_pairs={{0,8},{4,20},{8,0},{12,28},{16,24},{20,4},{24,16},{28,12},{1,9},{5... | collective-permute-start | bytes 2359304 | tf_op jit(solution)/shard_map/ppermute | solution.py:446
  158.7 18.3 %collective-permute-start.24 = (bf16[384,1024]{1,0:T(8,128)(2,1)S(1)}, bf16[384,1024]{1,0:T(8,128)(2,1)}, u32[]{:S(2)}, u32[]{:S(2)}) collective-permute-start(bf16[384,1024]{1,0:T(8,128)(2,1)S(1)} %bitcast.114), channel_id=1, source_target_pairs={{0,16},{4,12},{8,24},{12,4},{16,0},{20,28},{24,8},{28,20},{1,17},{... | collective-permute-start | bytes 2359304 | tf_op jit(solution)/shard_map/ppermute | solution.py:446
  169.1 61.7 %reduce-scatter.8.cloned.1.call-start = ((), (), s32[]{:S(2)}) async-start(), calls=%async_computation.8 | async-start | bytes 1310720 | tf_op jit(solution)/shard_map/reduce_scatter | solution.py:501
  177.4 12.5 %collective-permute-start.26 = (bf16[384,1024]{1,0:T(8,128)(2,1)}, bf16[384,1024]{1,0:T(8,128)(2,1)}, u32[]{:S(2)}, u32[]{:S(2)}) collective-permute-start(bf16[384,1024]{1,0:T(8,128)(2,1)} %collective-permute-done.21.refs_8_), channel_id=1, source_target_pairs={{0,16},{4,12},{8,24},{12,4},{16,0},{20,28},{24,8},{28,20},{1,17},{... | collective-permute-start | bytes 2359304 | tf_op jit(solution)/shard_map/ppermute | solution.py:446
  218.6 66.4 %all-gather.5.cloned.1.call-start = ((), (), s32[]{:S(2)}) async-start(), calls=%async_computation.9 | async-start | bytes 2621440 | tf_op jit(solution)/shard_map/all_gather | solution.py:504
  (41 other events, 802.1 us)
Sparse Core Ops, SparseCore 0:
  13.7 46.5 reduce-scatter.3
  65.0 47.6 all-gather.2
  169.3 27.8 reduce-scatter.5
  205.2 25.6 reduce-scatter.7
  237.7 47.2 all-gather.4

commit v6 on v5

--- a/solution.py
+++ b/solution.py
@@ -466,26 +466,22 @@
         gate_near, up_near, gate_again, up_again = ordered(gate_near, up_near, gate, up)
         gate_far, up_far = to(gate_again, second), to(up_again, second)
         near_cores = [other_core(value) for value in (gate_near, up_near)]
-        gate_far, gate_near, up_near = ordered(gate_far, gate_near, up_near)
         gate_far_2, up_far_2 = to(gate_near, second), to(up_near, second)
-        far_cores = [other_core(value) for value in (gate_far, up_far)]
-        full_mid, *cores = ordered(full_mid, *near_cores, *far_cores)
+        full_mid, gate_far, up_far, gate_far_2, *cores = ordered(
+            full_mid, gate_far, up_far, gate_far_2, *near_cores
+        )
         normed = rms_norm(full_mid, gain_post)
 
         def sets_of(gates, ups, at):
             return inner_of(normed, factors, gates, ups, at)
 
         inners = sets_of(
-            [gate, gate_core, gate_near, cores[0], gate_far, cores[2]],
-            [up, up_core, up_near, cores[1], up_far, cores[3]],
-            0,
+            [gate, gate_core, gate_near, cores[0]], [up, up_core, up_near, cores[1]], 0
         )
-        inners[5], gate_far_2, down_a, near = ordered(inners[5], gate_far_2, down_a, near)
+        inners[3], up_far_2, down_a, near = ordered(inners[3], up_far_2, down_a, near)
         far, last = to(down_a, second), to(near, second)
-        inners += sets_of(
-            [gate_far_2, other_core(gate_far_2)], [up_far_2, other_core(up_far_2)], 6
-        )
-        inners[7], far, down_b = ordered(inners[7], far, down_b)
+        inners += sets_of(both_cores(gate_far, gate_far_2), both_cores(up_far, up_far_2), 4)
+        inners[7], far, last, down_b = ordered(inners[7], far, last, down_b)
         downs = both_cores(down_a, near, far, last)
         near, far = to(down_b, first), to(down_b, second)
         total, top = down_sum(inners, downs, None, dec_count)

time: 303 us -> 303 us (level)
  waiting for transfers between devices: 143 us -> 138 us
  starting transfers between devices: 41.8 us -> 46.5 us
    all_gather x1, waiting for transfers between devices: 10.5 us -> 0.01 us  [shards(): full_mid = lax.all_gather(hidden_mid, 'col', axis=1, tiled=True)]
    ppermute x12, starting transfers between devices: 17.1 us -> 20.7 us  [to(): return lax.ppermute(value, 'row', pairs)]
    ppermute x16, waiting for transfers between devices: 3.23 us -> 6.75 us  [other_core(): return lax.ppermute(value, 'row', row_pairs()[2])]
    unnamed x52 -> x54, local copies, waits for them, and re-layouts: 6.68 us -> 6.96 us
  transfers between devices with their start and end apart: 44 -> 44, of which waited for: 23 -> 25; matrix products, arithmetic and copies ran while one was open for 12% -> 12% of each run, Pallas kernels for 14% -> 14%
where the time goes in v6:
time: 303 us; the launch traced here: 302 us
  waiting for transfers between devices  138 us (46%)
  Pallas kernels  52.6 us (17%)
  starting transfers between devices  46.5 us (15%)
  other arithmetic  19 us (6%)
  local copies, waits for them, and re-layouts  18.6 us (6%)
  between operations  14.3 us (5%)
  matrix products  12.5 us (4%)
    ppermute x12, waiting for transfers between devices, to(): return lax.ppermute(value, 'row', pairs)  88.8 us
    pallas_call x2, Pallas kernels, inner_of(): pl.pallas_call(lambda *refs: inner_kernel(sets, at, *refs), grid=(half //...  22.5 us
    ppermute x12, starting transfers between devices, to(): return lax.ppermute(value, 'row', pairs)  20.7 us
    pallas_call x3, Pallas kernels, down_sum(): pl.pallas_call(lambda *refs: down_kernel(sets, *refs), grid=(width // til...  20 us
    all_gather x1, waiting for transfers between devices, shards(): full_out = lax.all_gather(hidden_out, 'col', axis=1, tiled=True)  17.8 us
    ppermute x9, starting transfers between devices, shifted(): lax.ppermute(value, axis, [(i, (i + shift) % count) for i in range(count)])  14.3 us
    pallas_call x1, Pallas kernels, tail(): pl.pallas_call(lambda *refs: tail_kernel(window, *refs), grid=(query_widt...  10 us
    ppermute x9, waiting for transfers between devices, shifted(): lax.ppermute(value, axis, [(i, (i + shift) % count) for i in range(count)])  9.92 us
  transfers between devices with their start and end apart: 44, of which 25 were waited for; matrix products, arithmetic and copies ran while one was open for 12% of the time, Pallas kernels for 14%

profile of v6, /device:TPU:0, one launch (start us, length us, event | category | flops | bytes accessed | tf_op | source)
XLA Modules:
  0.0 301.6 jit_solution(10966858952633057194)
XLA Ops:
  7.2 6.3 %convolution_convert_fusion = bf16[512,2048]{1,0:T(8,128)(2,1)} fusion(bf16[512,1024]{1,0:T(8,128)(2,1)} %param.17, bf16[1024,2048]{1,0:T(8,128)(2,1)} %param.19), kind=kOutput, calls=%fused_computation.5 | convolution fusion | flops 2148532224 | bytes 7340032 | tf_op jit(solution)/shard_map/dot_general | solution.py:438
  13.6 3.0 collective-permute-start
  17.2 3.8 %reshape_squeeze.3 = bf16[384,4,512]{2,1,0:T(4,128)(2,1)} reshape(bf16[1,384,2048]{2,1,0:T(8,128)(2,1)} %param.26) | data formatting | bytes 3145728 | tf_op jit(solution)/shard_map/reshape;squeeze | solution.py:454
  21.1 2.9 fusion.54
  29.4 31.2 %collective-permute-done.2.refs_10_ = bf16[384,1024]{1,0:T(8,128)(2,1)} collective-permute-done((bf16[384,1024]{1,0:T(8,128)(2,1)}, bf16[384,1024]{1,0:T(8,128)(2,1)}, u32[]{:S(2)}, u32[]{:S(2)}) %collective-permute-start.2) | collective-permute-done | bytes 786464 | tf_op jit(solution)/shard_map/ppermute | solution.py:446
  67.4 16.2 %collective-permute-done.5.refs_2_ = bf16[2048,384]{1,0:T(8,128)(2,1)} collective-permute-done((bf16[2048,384]{1,0:T(8,128)(2,1)}, bf16[2048,384]{1,0:T(8,128)(2,1)}, u32[]{:S(2)}, u32[]{:S(2)}) %collective-permute-start.5) | collective-permute-done | bytes 1572896 | tf_op jit(solution)/shard_map/ppermute | solution.py:446
  85.6 14.8 %collective-permute-done.6.refs_3_ = bf16[2048,384]{1,0:T(8,128)(2,1)} collective-permute-done((bf16[2048,384]{1,0:T(8,128)(2,1)}, bf16[2048,384]{1,0:T(8,128)(2,1)}, u32[]{:S(2)}, u32[]{:S(2)}) %collective-permute-start.6) | collective-permute-done | bytes 1572896 | tf_op jit(solution)/shard_map/ppermute | solution.py:446
  100.4 16.9 %collective-permute-done.7.refs_6_ = bf16[2048,384]{1,0:T(8,128)(2,1)} collective-permute-done((bf16[2048,384]{1,0:T(8,128)(2,1)}, bf16[2048,384]{1,0:T(8,128)(2,1)}, u32[]{:S(2)}, u32[]{:S(2)}) %collective-permute-start.7) | collective-permute-done | bytes 1572896 | tf_op jit(solution)/shard_map/ppermute | solution.py:446
  121.4 11.3 %shard_map.184 = (bf16[512,384]{1,0:T(8,128)(2,1)}, bf16[512,384]{1,0:T(8,128)(2,1)}, bf16[512,384]{1,0:T(8,128)(2,1)}, bf16[512,384]{1,0:T(8,128)(2,1)}) custom-call(bf16[512,2048]{1,0:T(8,128)(2,1)} %fusion.2.refs_0_, f32[512,128]{1,0:T(8,128)} %pad.17.refs_1_, bf16[2048,384]{1,0:T(8,128)(2,1)} %bitcast.122, bf16[2048,384]{1,0:T(8,128)(2,1)} %bitcast.126, ...), custom_call_target="tpu_custom_call" | custom-call | flops 512 | bytes 512 | tf_op jit(solution)/shard_map/pallas_call | solution.py:116
  144.6 11.2 %shard_map.185 = (bf16[512,384]{1,0:T(8,128)(2,1)}, bf16[512,384]{1,0:T(8,128)(2,1)}, bf16[512,384]{1,0:T(8,128)(2,1)}, bf16[512,384]{1,0:T(8,128)(2,1)}) custom-call(bf16[512,2048]{1,0:T(8,128)(2,1)} %fusion.2.refs_0_, f32[512,128]{1,0:T(8,128)} %pad.17.refs_1_, bf16[2048,384]{1,0:T(8,128)(2,1)} %collective-permute-done.5.refs_2_, ...), custom_call_target="tpu_custom_call" | custom-call | flops 512 | bytes 512 | tf_op jit(solution)/shard_map/pallas_call | solution.py:116
  161.1 8.0 %shard_map.186 = (bf16[512,1024]{1,0:T(8,128)(2,1)}, f32[8,1024]{1,0:T(8,128)}) custom-call(bf16[512,384]{1,0:T(8,128)(2,1)} %get-tuple-element.65.refs_0_, bf16[512,384]{1,0:T(8,128)(2,1)} %get-tuple-element.66.refs_1_, bf16[512,384]{1,0:T(8,128)(2,1)} %get-tuple-element.67.refs_2_, bf16[512,384]{1,0:T(8,128)(2,1)} %get-tuple-element.71.refs_3_, ...), custom_call_target="tpu_custom_call" | custom-call | flops 3221225472 | bytes 11534336 | tf_op jit(solution)/shard_map/pallas_call | solution.py:163
  169.5 6.6 %collective-permute-done.21.refs_8_ = bf16[384,1024]{1,0:T(8,128)(2,1)} collective-permute-done((bf16[384,1024]{1,0:T(8,128)(2,1)S(1)}, bf16[384,1024]{1,0:T(8,128)(2,1)}, u32[]{:S(2)}, u32[]{:S(2)}) %collective-permute-start.21) | collective-permute-done | bytes 786464 | tf_op jit(solution)/shard_map/ppermute | solution.py:446
  181.0 7.1 %shard_map.187.refs_4_ = f32[512,1024]{1,0:T(8,128)} custom-call(bf16[512,384]{1,0:T(8,128)(2,1)} %get-tuple-element.65.refs_0_, bf16[512,384]{1,0:T(8,128)(2,1)} %get-tuple-element.66.refs_1_, bf16[512,384]{1,0:T(8,128)(2,1)} %get-tuple-element.67.refs_2_, bf16[512,384]{1,0:T(8,128)(2,1)} %get-tuple-element.71.refs_3_, ...), custom_call_target="tpu_custom_call" | custom-call | flops 2415919104 | bytes 9175040 | tf_op jit(solution)/shard_map/pallas_call | solution.py:163
  192.1 5.0 %shard_map.188 = (bf16[512,1024]{1,0:T(8,128)(2,1)}, f32[8,1024]{1,0:T(8,128)}) custom-call(bf16[512,384]{1,0:T(8,128)(2,1)} %get-tuple-element.78.refs_6_.refs_0_, bf16[512,384]{1,0:T(8,128)(2,1)} %get-tuple-element.83.refs_7_.refs_1_, bf16[384,1024]{1,0:T(8,128)(2,1)} %collective-permute-done.26.refs_2_, ...), custom_call_target="tpu_custom_call" | custom-call | flops 805306368 | bytes 4456448 | tf_op jit(solution)/shard_map/pallas_call | solution.py:163
  200.2 2.6 collective-permute-start.29
  209.9 2.9 fusion.18
  214.4 4.0 %all-to-all-start = ((bf16[8,8,1152]{2,1,0:T(8,128)(2,1)}), bf16[8,8,1152]{2,1,0:T(8,128)(2,1)}, u32[]{:S(2)}, u32[]{:S(2)}) async-start(bf16[8,8,1152]{2,1,0:T(8,128)(2,1)} %multiply_reduce_fusion), calls=%async_computation.2 | async-start | bytes 294912 | tf_op jit(solution)/shard_map/all_to_all | solution.py:527
  219.1 5.0 %all-to-all-done = bf16[8,8,1152]{2,1,0:T(8,128)(2,1)} async-done(((bf16[8,8,1152]{2,1,0:T(8,128)(2,1)}), bf16[8,8,1152]{2,1,0:T(8,128)(2,1)}, u32[]{:S(2)}, u32[]{:S(2)}) %all-to-all-start) | async-done | bytes 147488 | tf_op jit(solution)/shard_map/all_to_all | solution.py:527
  225.7 4.6 %reduce-scatter.8.cloned.1.call-done = bf16[512,256]{1,0:T(8,128)(2,1)} async-done(((bf16[512,1024]{1,0:T(8,128)(2,1)}), bf16[512,256]{1,0:T(8,128)(2,1)}) %reduce-scatter.8.cloned.1.call-update) | async-done | bytes 262160 | tf_op jit(solution)/shard_map/reduce_scatter | solution.py:497
  249.4 2.6 collective-permute-done.35
  254.6 3.7 %all-to-all-start.1 = ((f32[8,72,128]{2,1,0:T(8,128)}), f32[8,72,128]{2,1,0:T(8,128)S(1)}, u32[]{:S(2)}, u32[]{:S(2)}) async-start(f32[8,72,128]{2,1,0:T(8,128)} %broadcast_in_dim.114), calls=%async_computation.4 | async-start | bytes 589824 | tf_op jit(solution)/shard_map/all_to_all | solution.py:602
  261.0 4.5 %all-to-all-done.1 = f32[8,72,128]{2,1,0:T(8,128)S(1)} async-done(((f32[8,72,128]{2,1,0:T(8,128)}), f32[8,72,128]{2,1,0:T(8,128)S(1)}, u32[]{:S(2)}, u32[]{:S(2)}) %all-to-all-start.1) | async-done | bytes 294944 | tf_op jit(solution)/shard_map/all_to_all | solution.py:602
  266.5 17.8 %all-gather.5.cloned.1.call-done.refs_0_ = bf16[512,2048]{1,0:T(8,128)(2,1)} async-done(((bf16[512,512]{1,0:T(8,128)(2,1)}), bf16[512,2048]{1,0:T(8,128)(2,1)}) %all-gather.5.cloned.1.call-update) | async-done | bytes 2097168 | tf_op jit(solution)/shard_map/all_gather | solution.py:500
  284.4 10.0 %shard_map.189 = (bf16[512,256]{1,0:T(8,128)(2,1)}, bf16[512,1024]{1,0:T(8,128)(2,1)}) custom-call(bf16[512,2048]{1,0:T(8,128)(2,1)} %all-gather.5.cloned.1.call-done.refs_0_, bf16[1,2048]{1,0:T(2,128)(2,1)} %broadcast_in_dim.108.refs_1_, bf16[2048,1024]{1,0:T(8,128)(2,1)} %refs_2_.1, bf16[2048,256]{1,0:T(8,128)(2,1)} %refs_3_.1, ...), custom_call_target="tpu_custom_call" | custom-call | flops 2684354560 | bytes 9437184 | tf_op jit(solution)/shard_map/pallas_call | solution.py:248
  (206 shorter events, 85.1 us)
Async XLA Ops:
  7.2 53.5 %reduce-scatter.4.cloned.1.call-start = ((), (), s32[]{:S(2)}) async-start(), calls=%async_computation.5 | async-start | bytes 2621440 | tf_op jit(solution)/shard_map/reduce_scatter | solution.py:439
  13.6 103.7 %all-gather.3.cloned.1.call-start = ((), (), s32[]{:S(2)}) async-start(), calls=%async_computation.6 | async-start | bytes 2621440 | tf_op jit(solution)/shard_map/all_gather | solution.py:464
  13.6 47.0 %collective-permute-start = (bf16[2048,384]{1,0:T(8,128)(2,1)}, bf16[2048,384]{1,0:T(8,128)(2,1)}, u32[]{:S(2)}, u32[]{:S(2)}) collective-permute-start(bf16[2048,384]{1,0:T(8,128)(2,1)} %bitcast.119), channel_id=1, source_target_pairs={{0,8},{4,20},{8,0},{12,28},{16,24},{20,4},{24,16},{28,12},{1,9},{5... | collective-permute-start | bytes 4718600 | tf_op jit(solution)/shard_map/ppermute | solution.py:446
  16.6 44.0 %collective-permute-start.1 = (bf16[2048,384]{1,0:T(8,128)(2,1)}, bf16[2048,384]{1,0:T(8,128)(2,1)}, u32[]{:S(2)}, u32[]{:S(2)}) collective-permute-start(bf16[2048,384]{1,0:T(8,128)(2,1)} %bitcast.123), channel_id=1, source_target_pairs={{0,8},{4,20},{8,0},{12,28},{16,24},{20,4},{24,16},{28,12},{1,9},{5... | collective-permute-start | bytes 4718600 | tf_op jit(solution)/shard_map/ppermute | solution.py:446
  16.7 43.9 %collective-permute-start.3 = (bf16[2048,384]{1,0:T(8,128)(2,1)}, bf16[2048,384]{1,0:T(8,128)(2,1)}, u32[]{:S(2)}, u32[]{:S(2)}) collective-permute-start(bf16[2048,384]{1,0:T(8,128)(2,1)} %bitcast.120), channel_id=1, source_target_pairs={{0,4},{4,0},{8,12},{12,8},{16,20},{20,16},{24,28},{28,24},{1,5},{5... | collective-permute-start | bytes 4718600 | tf_op jit(solution)/shard_map/ppermute | solution.py:302
  16.7 43.9 %collective-permute-start.4 = (bf16[2048,384]{1,0:T(8,128)(2,1)}, bf16[2048,384]{1,0:T(8,128)(2,1)}, u32[]{:S(2)}, u32[]{:S(2)}) collective-permute-start(bf16[2048,384]{1,0:T(8,128)(2,1)} %bitcast.124), channel_id=1, source_target_pairs={{0,4},{4,0},{8,12},{12,8},{16,20},{20,16},{24,28},{28,24},{1,5},{5... | collective-permute-start | bytes 4718600 | tf_op jit(solution)/shard_map/ppermute | solution.py:302
  25.1 35.5 %collective-permute-start.2 = (bf16[384,1024]{1,0:T(8,128)(2,1)}, bf16[384,1024]{1,0:T(8,128)(2,1)}, u32[]{:S(2)}, u32[]{:S(2)}) collective-permute-start(bf16[384,1024]{1,0:T(8,128)(2,1)} %bitcast.46.refs_8_), channel_id=1, source_target_pairs={{0,8},{4,20},{8,0},{12,28},{16,24},{20,4},{24,16},{28,12},{1,9},{5... | collective-permute-start | bytes 2359304 | tf_op jit(solution)/shard_map/ppermute | solution.py:446
  62.7 134.9 %reduce-scatter.6.cloned.1.call-start = ((), (), s32[]{:S(2)}) async-start(), calls=%async_computation.7 | async-start | bytes 1310720 | tf_op jit(solution)/shard_map/reduce_scatter | solution.py:489
  62.7 20.8 %collective-permute-start.5 = (bf16[2048,384]{1,0:T(8,128)(2,1)}, bf16[2048,384]{1,0:T(8,128)(2,1)}, u32[]{:S(2)}, u32[]{:S(2)}) collective-permute-start(bf16[2048,384]{1,0:T(8,128)(2,1)} %bitcast.121), channel_id=1, source_target_pairs={{0,16},{4,12},{8,24},{12,4},{16,0},{20,28},{24,8},{28,20},{1,17},{... | collective-permute-start | bytes 4718600 | tf_op jit(solution)/shard_map/ppermute | solution.py:446
  64.8 35.6 %collective-permute-start.6 = (bf16[2048,384]{1,0:T(8,128)(2,1)}, bf16[2048,384]{1,0:T(8,128)(2,1)}, u32[]{:S(2)}, u32[]{:S(2)}) collective-permute-start(bf16[2048,384]{1,0:T(8,128)(2,1)} %bitcast.125), channel_id=1, source_target_pairs={{0,16},{4,12},{8,24},{12,4},{16,0},{20,28},{24,8},{28,20},{1,17},{... | collective-permute-start | bytes 4718600 | tf_op jit(solution)/shard_map/ppermute | solution.py:446
  64.9 52.3 %collective-permute-start.7 = (bf16[2048,384]{1,0:T(8,128)(2,1)}, bf16[2048,384]{1,0:T(8,128)(2,1)}, u32[]{:S(2)}, u32[]{:S(2)}) collective-permute-start(bf16[2048,384]{1,0:T(8,128)(2,1)} %collective-permute-done.refs_6_), channel_id=1, source_target_pairs={{0,16},{4,12},{8,24},{12,4},{16,0},{20,28},{24,8},{28,20},{1,17},{... | collective-permute-start | bytes 4718600 | tf_op jit(solution)/shard_map/ppermute | solution.py:446
  66.9 50.4 %collective-permute-start.8 = (bf16[2048,384]{1,0:T(8,128)(2,1)}, bf16[2048,384]{1,0:T(8,128)(2,1)}, u32[]{:S(2)}, u32[]{:S(2)}) collective-permute-start(bf16[2048,384]{1,0:T(8,128)(2,1)} %collective-permute-done.refs_6_), channel_id=1, source_target_pairs={{0,4},{4,0},{8,12},{12,8},{16,20},{20,16},{24,28},{28,24},{1,5},{5... | collective-permute-start | bytes 4718600 | tf_op jit(solution)/shard_map/ppermute | solution.py:302
  66.9 50.4 %collective-permute-start.9 = (bf16[2048,384]{1,0:T(8,128)(2,1)}, bf16[2048,384]{1,0:T(8,128)(2,1)}, u32[]{:S(2)}, u32[]{:S(2)}) collective-permute-start(bf16[2048,384]{1,0:T(8,128)(2,1)} %collective-permute-done.1.refs_7_), channel_id=1, source_target_pairs={{0,4},{4,0},{8,12},{12,8},{16,20},{20,16},{24,28},{28,24},{1,5},{5... | collective-permute-start | bytes 4718600 | tf_op jit(solution)/shard_map/ppermute | solution.py:302
  83.5 50.6 %collective-permute-start.10 = (bf16[2048,384]{1,0:T(8,128)(2,1)}, bf16[2048,384]{1,0:T(8,128)(2,1)}, u32[]{:S(2)}, u32[]{:S(2)}) collective-permute-start(bf16[2048,384]{1,0:T(8,128)(2,1)} %collective-permute-done.1.refs_7_), channel_id=1, source_target_pairs={{0,16},{4,12},{8,24},{12,4},{16,0},{20,28},{24,8},{28,20},{1,17},{... | collective-permute-start | bytes 4718600 | tf_op jit(solution)/shard_map/ppermute | solution.py:446
  135.1 20.7 %collective-permute-start.15 = (bf16[384,1024]{1,0:T(8,128)(2,1)}, bf16[384,1024]{1,0:T(8,128)(2,1)}, u32[]{:S(2)}, u32[]{:S(2)}) collective-permute-start(bf16[384,1024]{1,0:T(8,128)(2,1)} %bitcast.46.refs_8_), channel_id=1, source_target_pairs={{0,16},{4,12},{8,24},{12,4},{16,0},{20,28},{24,8},{28,20},{1,17},{... | collective-permute-start | bytes 2359304 | tf_op jit(solution)/shard_map/ppermute | solution.py:446
  137.9 18.0 %collective-permute-start.16 = (bf16[384,1024]{1,0:T(8,128)(2,1)}, bf16[384,1024]{1,0:T(8,128)(2,1)}, u32[]{:S(2)}, u32[]{:S(2)}) collective-permute-start(bf16[384,1024]{1,0:T(8,128)(2,1)} %collective-permute-done.2.refs_10_), channel_id=1, source_target_pairs={{0,16},{4,12},{8,24},{12,4},{16,0},{20,28},{24,8},{28,20},{1,17},{... | collective-permute-start | bytes 2359304 | tf_op jit(solution)/shard_map/ppermute | solution.py:446
  140.1 18.3 %collective-permute-start.17 = (bf16[384,1024]{1,0:T(8,128)(2,1)}, bf16[384,1024]{1,0:T(8,128)(2,1)}, u32[]{:S(2)}, u32[]{:S(2)}) collective-permute-start(bf16[384,1024]{1,0:T(8,128)(2,1)} %bitcast.46.refs_8_), channel_id=1, source_target_pairs={{0,4},{4,0},{8,12},{12,8},{16,20},{20,16},{24,28},{28,24},{1,5},{5... | collective-permute-start | bytes 2359304 | tf_op jit(solution)/shard_map/ppermute | solution.py:302
  142.4 17.6 %collective-permute-start.18 = (bf16[384,1024]{1,0:T(8,128)(2,1)}, bf16[384,1024]{1,0:T(8,128)(2,1)}, u32[]{:S(2)}, u32[]{:S(2)}) collective-permute-start(bf16[384,1024]{1,0:T(8,128)(2,1)} %collective-permute-done.2.refs_10_), channel_id=1, source_target_pairs={{0,4},{4,0},{8,12},{12,8},{16,20},{20,16},{24,28},{28,24},{1,5},{5... | collective-permute-start | bytes 2359304 | tf_op jit(solution)/shard_map/ppermute | solution.py:302
  156.4 19.6 %collective-permute-start.21 = (bf16[384,1024]{1,0:T(8,128)(2,1)S(1)}, bf16[384,1024]{1,0:T(8,128)(2,1)}, u32[]{:S(2)}, u32[]{:S(2)}) collective-permute-start(bf16[384,1024]{1,0:T(8,128)(2,1)S(1)} %bitcast.113), channel_id=1, source_target_pairs={{0,8},{4,20},{8,0},{12,28},{16,24},{20,4},{24,16},{28,12},{1,9},{5... | collective-permute-start | bytes 2359304 | tf_op jit(solution)/shard_map/ppermute | solution.py:446
  158.4 18.0 %collective-permute-start.24 = (bf16[384,1024]{1,0:T(8,128)(2,1)S(1)}, bf16[384,1024]{1,0:T(8,128)(2,1)}, u32[]{:S(2)}, u32[]{:S(2)}) collective-permute-start(bf16[384,1024]{1,0:T(8,128)(2,1)S(1)} %bitcast.114), channel_id=1, source_target_pairs={{0,16},{4,12},{8,24},{12,4},{16,0},{20,28},{24,8},{28,20},{1,17},{... | collective-permute-start | bytes 2359304 | tf_op jit(solution)/shard_map/ppermute | solution.py:446
  169.2 61.1 %reduce-scatter.8.cloned.1.call-start = ((), (), s32[]{:S(2)}) async-start(), calls=%async_computation.8 | async-start | bytes 1310720 | tf_op jit(solution)/shard_map/reduce_scatter | solution.py:497
  177.1 12.4 %collective-permute-start.26 = (bf16[384,1024]{1,0:T(8,128)(2,1)}, bf16[384,1024]{1,0:T(8,128)(2,1)}, u32[]{:S(2)}, u32[]{:S(2)}) collective-permute-start(bf16[384,1024]{1,0:T(8,128)(2,1)} %collective-permute-done.21.refs_8_), channel_id=1, source_target_pairs={{0,16},{4,12},{8,24},{12,4},{16,0},{20,28},{24,8},{28,20},{1,17},{... | collective-permute-start | bytes 2359304 | tf_op jit(solution)/shard_map/ppermute | solution.py:446
  218.4 66.0 %all-gather.5.cloned.1.call-start = ((), (), s32[]{:S(2)}) async-start(), calls=%async_computation.9 | async-start | bytes 2621440 | tf_op jit(solution)/shard_map/all_gather | solution.py:500
  254.6 11.0 %all-to-all-start.1 = ((f32[8,72,128]{2,1,0:T(8,128)}), f32[8,72,128]{2,1,0:T(8,128)S(1)}, u32[]{:S(2)}, u32[]{:S(2)}) async-start(f32[8,72,128]{2,1,0:T(8,128)} %broadcast_in_dim.114), calls=%async_computation.4 | async-start | bytes 589824 | tf_op jit(solution)/shard_map/all_to_all | solution.py:602
  (42 other events, 763.3 us)
Sparse Core Ops, SparseCore 0:
  13.7 46.5 reduce-scatter.3
  62.8 47.7 all-gather.2
  169.3 28.1 reduce-scatter.5
  205.0 25.1 reduce-scatter.7
  237.0 47.2 all-gather.4
